TPU v7x, 32 devices: a whole 2x2x4 slice. The times are simulated.
32 devices in a mesh: dp: 4 (over x, core), fsdp: 8 (over z, y).
Axes of the slice: x: 2, y: 2, z: 4, core: 2. Of those that a mesh axis runs over, the one named last changes fastest.
Arguments:
- hidden_in: bfloat16 [8, 2048, 960], P('dp', 'fsdp'), may hold values from -6 to 6
- segment: int32 [8, 2048], P('dp', 'fsdp'), may hold values from 0 to 8, as said below
- position: int32 [8, 2048], P('dp', 'fsdp'), may hold values from 0 to 1215, as said below
- selected: int32 [8, 2048], P('dp', 'fsdp'), may hold values from 0 to 1, as said below
- gain_attn: bfloat16 [960], replicated, may hold values from 0.5 to 1.5
- gain_ffn: bfloat16 [960], replicated, may hold values from 0.5 to 1.5
- router: bfloat16 [960], replicated, may hold values from -0.1875 to 0.1875
- w_query: bfloat16 [960, 960], P('dp', 'fsdp'), may hold values from -0.1875 to 0.1875
- key_weight: bfloat16 [960, 320], P('dp', 'fsdp'), may hold values from -0.1875 to 0.1875
- value_weight: bfloat16 [960, 320], P('dp', 'fsdp'), may hold values from -0.1875 to 0.1875
- w_output: bfloat16 [960, 960], P('fsdp', 'dp'), may hold values from -1.5 to 1.5
- w_gate: bfloat16 [960, 2560], P('dp', 'fsdp'), may hold values from -0.1875 to 0.1875
- w_up: bfloat16 [960, 2560], P('dp', 'fsdp'), may hold values from -0.1875 to 0.1875
- w_down: bfloat16 [2560, 960], P('fsdp', 'dp'), may hold values from -0.125 to 0.125
- cotangent: bfloat16 [8, 2048, 960], P('dp', 'fsdp'), may hold values from -6 to 6
Outputs:
- hidden_out: bfloat16 [8, 2048, 960], P('dp', 'fsdp')
- grad_in: float32 [8, 2048, 960], P('dp', 'fsdp')
- grad_gain_attn: float32 [960], replicated
- grad_gain_ffn: float32 [960], replicated
- grad_router: float32 [960], replicated
- grad_w_query: float32 [960, 960], P('dp', 'fsdp')
- grad_w_key: float32 [960, 320], P('dp', 'fsdp')
- grad_w_value: float32 [960, 320], P('dp', 'fsdp')
- grad_w_output: float32 [960, 960], P('fsdp', 'dp')
- grad_w_gate: float32 [960, 2560], P('dp', 'fsdp')
- grad_w_up: float32 [960, 2560], P('dp', 'fsdp')
- grad_w_down: float32 [2560, 960], P('fsdp', 'dp')
Inputs may be any that keep to these rules, and one draw needn't show every extreme that they name: Every group begins with 1024 tokens of segment 0; continuations 1 to 8 follow in order, each 64 to 192 tokens long; in every group one or more continuations, which ones drawn from the seed, are exactly 192 tokens long. `position`: A prompt token carries its index in the group; a continuation token carries 1024 plus its index in its continuation. `selected`: exactly 1024 tokens of every group are 1.
All inputs are finite; a program needn't handle non-finite values.
Results may differ from a plain program's by a relative error of at most 0.023.
Values may be sent and summed in bfloat16 or wider, within the bound.
No kernel may reach another device: no remote copies, remote signals or barrier semaphores. Data moves between devices by JAX's collectives and lax.ppermute only.
A program may use at most 192 MiB of HBM per device.

v0:
```python
import jax
import jax.numpy as jnp
from jax import lax
from jax.sharding import PartitionSpec as P

QUERY_HEAD_COUNT = 15
KEY_VALUE_HEADS = 5
HEAD_DIM = 64


EPSILON = 1e-05
THETA = 10000.0
MINUS_LARGE = -1e30
TOP_PRECISION = lax.Precision.HIGHEST


def inverse_rms(value_matrix):
    return lax.rsqrt(jnp.mean(value_matrix * value_matrix, axis=-1, keepdims=True) + EPSILON)


def apply_rotary(value_matrix, cosine_table, sine_table):
    half_width = value_matrix.shape[-1] // 2
    first_half = value_matrix[..., :half_width]
    second_half = value_matrix[..., half_width:]
    return jnp.concatenate(
        [
            first_half * cosine_table - second_half * sine_table,
            second_half * cosine_table + first_half * sine_table,
        ],
        axis=-1,
    )


def gather_weights(w_query, key_weight, value_weight, w_output, w_gate, w_up, w_down):
    sectioned = (
        lax.all_gather(w_query, "fsdp", axis=1, tiled=True),
        lax.all_gather(key_weight, "fsdp", axis=1, tiled=True),
        lax.all_gather(value_weight, "fsdp", axis=1, tiled=True),
        lax.all_gather(w_output, "fsdp", axis=0, tiled=True),
        lax.all_gather(w_gate, "fsdp", axis=1, tiled=True),
        lax.all_gather(w_up, "fsdp", axis=1, tiled=True),
        lax.all_gather(w_down, "fsdp", axis=0, tiled=True),
    )
    return (
        lax.all_gather(sectioned[0], "dp", axis=0, tiled=True),
        lax.all_gather(sectioned[1], "dp", axis=0, tiled=True),
        lax.all_gather(sectioned[2], "dp", axis=0, tiled=True),
        lax.all_gather(sectioned[3], "dp", axis=1, tiled=True),
        lax.all_gather(sectioned[4], "dp", axis=0, tiled=True),
        lax.all_gather(sectioned[5], "dp", axis=0, tiled=True),
        lax.all_gather(sectioned[6], "dp", axis=1, tiled=True),
    )


def scatter_grads(terms):
    sectioned = (
        lax.psum_scatter(
            terms[0].astype(jnp.bfloat16), "dp", scatter_dimension=0, tiled=True
        ).astype(jnp.float32),
        lax.psum_scatter(
            terms[1].astype(jnp.bfloat16), "dp", scatter_dimension=0, tiled=True
        ).astype(jnp.float32),
        lax.psum_scatter(
            terms[2].astype(jnp.bfloat16), "dp", scatter_dimension=0, tiled=True
        ).astype(jnp.float32),
        lax.psum_scatter(
            terms[3].astype(jnp.bfloat16), "dp", scatter_dimension=1, tiled=True
        ).astype(jnp.float32),
        lax.psum_scatter(
            terms[4].astype(jnp.bfloat16), "dp", scatter_dimension=0, tiled=True
        ).astype(jnp.float32),
        lax.psum_scatter(
            terms[5].astype(jnp.bfloat16), "dp", scatter_dimension=0, tiled=True
        ).astype(jnp.float32),
        lax.psum_scatter(
            terms[6].astype(jnp.bfloat16), "dp", scatter_dimension=1, tiled=True
        ).astype(jnp.float32),
    )
    return (
        lax.psum_scatter(
            sectioned[0].astype(jnp.bfloat16), "fsdp", scatter_dimension=1, tiled=True
        ).astype(jnp.float32),
        lax.psum_scatter(
            sectioned[1].astype(jnp.bfloat16), "fsdp", scatter_dimension=1, tiled=True
        ).astype(jnp.float32),
        lax.psum_scatter(
            sectioned[2].astype(jnp.bfloat16), "fsdp", scatter_dimension=1, tiled=True
        ).astype(jnp.float32),
        lax.psum_scatter(
            sectioned[3].astype(jnp.bfloat16), "fsdp", scatter_dimension=0, tiled=True
        ).astype(jnp.float32),
        lax.psum_scatter(
            sectioned[4].astype(jnp.bfloat16), "fsdp", scatter_dimension=1, tiled=True
        ).astype(jnp.float32),
        lax.psum_scatter(
            sectioned[5].astype(jnp.bfloat16), "fsdp", scatter_dimension=1, tiled=True
        ).astype(jnp.float32),
        lax.psum_scatter(
            sectioned[6].astype(jnp.bfloat16), "fsdp", scatter_dimension=0, tiled=True
        ).astype(jnp.float32),
    )


def key_sight(query_rows, query_segment, tag_block, first_row):
    key_rows = first_row + jnp.arange(tag_block.shape[1], dtype=jnp.int32)
    key_tags = tag_block.astype(jnp.int32)[:, None, :]
    earlier = key_rows[None, None, :] <= query_rows[None, :, None]
    allowed = (key_tags == 0) | (key_tags == query_segment[:, :, None])
    itself = key_rows[None, None, :] == query_rows[None, :, None]
    return earlier & allowed | itself


def over_blocks(block_fn, running, piece, first_row):
    kv_piece, tag_piece = piece
    piece_rows = kv_piece.shape[1]
    rows_per_block = min(piece_rows, 256)
    while piece_rows % rows_per_block:
        rows_per_block = rows_per_block - 1
    for offset in range(0, piece_rows, rows_per_block):
        running = block_fn(
            running,
            kv_piece[:, offset : offset + rows_per_block],
            tag_piece[:, offset : offset + rows_per_block],
            first_row + offset,
        )
    return running


def shards(
    hidden_in,
    segment,
    position,
    selected,
    gain_attn,
    gain_ffn,
    router,
    w_query,
    key_weight,
    value_weight,
    w_output,
    w_gate,
    w_up,
    w_down,
    cotangent,
):
    group_count, count_of_rows, model_width = hidden_in.shape
    count_of_tokens = group_count * count_of_rows
    grouped_heads = QUERY_HEAD_COUNT // KEY_VALUE_HEADS
    key_value_width = KEY_VALUE_HEADS * HEAD_DIM
    score_scale = HEAD_DIM ** (-0.5)
    full_set = gather_weights(w_query, key_weight, value_weight, w_output, w_gate, w_up, w_down)
    full_query, full_key, full_value, full_output, full_gate, full_up, full_down = full_set
    flat_in = hidden_in.reshape(count_of_tokens, model_width)
    inputs = flat_in.astype(jnp.float32)
    gain_one = gain_attn.astype(jnp.float32)
    gain_two = gain_ffn.astype(jnp.float32)
    router_wide = router.astype(jnp.float32)
    scale_one = inverse_rms(inputs)
    first_normed = (inputs * scale_one * gain_one).astype(jnp.bfloat16)
    frequency = THETA ** (-(jnp.arange(HEAD_DIM // 2).astype(jnp.float32) * 2.0) / HEAD_DIM)
    angles = position.reshape(count_of_tokens).astype(jnp.float32)[:, None] * frequency[None, :]
    cosine_table = jnp.cos(angles)[:, None, :]
    sine_table = jnp.sin(angles)[:, None, :]
    query_proj = jnp.dot(first_normed, full_query, preferred_element_type=jnp.float32).reshape(
        count_of_tokens, QUERY_HEAD_COUNT, HEAD_DIM
    )
    key_proj = jnp.dot(first_normed, full_key, preferred_element_type=jnp.float32).reshape(
        count_of_tokens, KEY_VALUE_HEADS, HEAD_DIM
    )
    value_low = jnp.dot(first_normed, full_value, preferred_element_type=jnp.float32).astype(
        jnp.bfloat16
    )
    query_lower_cast = apply_rotary(query_proj, cosine_table, sine_table).astype(jnp.bfloat16)
    key_low = apply_rotary(key_proj, cosine_table, sine_table).astype(jnp.bfloat16)
    heads_of_query = query_lower_cast.reshape(
        group_count, count_of_rows, KEY_VALUE_HEADS, grouped_heads, HEAD_DIM
    )
    kv_local = jnp.concatenate(
        [key_low.reshape(count_of_tokens, key_value_width), value_low], axis=1
    ).reshape(group_count, count_of_rows, 2 * key_value_width)
    tag_local = jnp.where(selected == 1, segment, -1).astype(jnp.bfloat16)
    query_rows = lax.axis_index("fsdp") * count_of_rows + jnp.arange(count_of_rows, dtype=jnp.int32)
    group_rows = count_of_rows * lax.axis_size("fsdp")

    def split_block(key_value_block):
        rows_per_block = key_value_block.shape[1]
        block_of_keys = key_value_block[..., :key_value_width].reshape(
            group_count, rows_per_block, KEY_VALUE_HEADS, HEAD_DIM
        )
        block_of_values = key_value_block[..., key_value_width:].reshape(
            group_count, rows_per_block, KEY_VALUE_HEADS, HEAD_DIM
        )
        return (block_of_keys, block_of_values)

    def attend_block(running, key_value_block, tag_block, first_row):
        visible = key_sight(query_rows, segment, tag_block, first_row)
        sight = visible[:, None, None, :, :]

        def work(current):
            row_peak, row_total, accum = current
            block_of_keys, block_of_values = split_block(key_value_block)
            scores = (
                jnp.einsum(
                    "gqkhd,gckd->gkhqc",
                    heads_of_query,
                    block_of_keys,
                    preferred_element_type=jnp.float32,
                )
                * score_scale
            )
            scores = jnp.where(sight, scores, MINUS_LARGE)
            new_peak = jnp.maximum(row_peak, jnp.max(scores, axis=-1))
            weights = jnp.where(sight, jnp.exp(scores - new_peak[..., None]), 0.0)
            fade_factor = jnp.exp(row_peak - new_peak)
            new_total = row_total * fade_factor + jnp.sum(weights, axis=-1)
            new_accum = accum * fade_factor[..., None] + jnp.einsum(
                "gkhqc,gckd->gkhqd",
                weights.astype(jnp.bfloat16),
                block_of_values,
                preferred_element_type=jnp.float32,
            )
            return (new_peak, new_total, new_accum)

        return lax.cond(jnp.any(visible), work, lambda current: current, running)

    initial_maximum = jnp.full(
        (group_count, KEY_VALUE_HEADS, grouped_heads, count_of_rows), MINUS_LARGE, jnp.float32
    )
    initial_total = jnp.zeros(
        (group_count, KEY_VALUE_HEADS, grouped_heads, count_of_rows), jnp.float32
    )
    initial_accumulator = jnp.zeros(
        (group_count, KEY_VALUE_HEADS, grouped_heads, count_of_rows, HEAD_DIM), jnp.float32
    )
    row_peak, row_total, accum = over_blocks(
        attend_block,
        (initial_maximum, initial_total, initial_accumulator),
        (
            lax.all_gather(kv_local, "fsdp", axis=1, tiled=True),
            lax.all_gather(tag_local, "fsdp", axis=1, tiled=True),
        ),
        jnp.int32(0),
    )
    log_total = row_peak + jnp.log(row_total)
    attention_blended = jnp.transpose(accum / row_total[..., None], (0, 3, 1, 2, 4)).reshape(
        count_of_tokens, QUERY_HEAD_COUNT * HEAD_DIM
    )
    mixed_low = attention_blended.astype(jnp.bfloat16)
    attn_out = jnp.dot(mixed_low, full_output, preferred_element_type=jnp.float32)
    middle = inputs + attn_out
    scale_two = inverse_rms(middle)
    normed_two = (middle * scale_two * gain_two).astype(jnp.bfloat16)
    gate_proj = jnp.dot(normed_two, full_gate, preferred_element_type=jnp.float32)
    up_proj = jnp.dot(normed_two, full_up, preferred_element_type=jnp.float32)
    gate_sigmoid = jax.nn.sigmoid(gate_proj)
    hidden = (gate_proj * gate_sigmoid * up_proj).astype(jnp.bfloat16)
    ffn_out = jnp.dot(hidden, full_down, preferred_element_type=jnp.float32)
    logit = jnp.dot(flat_in, router, preferred_element_type=jnp.float32)
    router_sigmoid = jax.nn.sigmoid(logit)
    chosen = selected.reshape(count_of_tokens).astype(jnp.float32)
    mix_weight = chosen * router_sigmoid
    branch = attn_out + ffn_out
    hidden_out = (
        (inputs + mix_weight[:, None] * branch)
        .astype(jnp.bfloat16)
        .reshape(group_count, count_of_rows, model_width)
    )
    back_set = gather_weights(w_query, key_weight, value_weight, w_output, w_gate, w_up, w_down)
    back_query, back_key, back_value, back_output, back_gate, back_up, back_down = back_set
    upstream = cotangent.reshape(count_of_tokens, model_width).astype(jnp.float32)
    branch_grad = upstream * mix_weight[:, None]
    logit_grad = (
        chosen * router_sigmoid * (1.0 - router_sigmoid) * jnp.sum(upstream * branch, axis=-1)
    )
    grad_router = jnp.dot(logit_grad, inputs, precision=TOP_PRECISION)
    ffn_grad = branch_grad.astype(jnp.bfloat16)
    grad_w_down = jnp.einsum("nf,nd->fd", hidden, ffn_grad, preferred_element_type=jnp.float32)
    hidden_grad = jnp.einsum("nd,fd->nf", ffn_grad, back_down, preferred_element_type=jnp.float32)
    up_grad = (hidden_grad * gate_proj * gate_sigmoid).astype(jnp.bfloat16)
    gate_grad = (
        hidden_grad * up_proj * gate_sigmoid * (1.0 + gate_proj * (1.0 - gate_sigmoid))
    ).astype(jnp.bfloat16)
    grad_w_gate = jnp.einsum("nd,nf->df", normed_two, gate_grad, preferred_element_type=jnp.float32)
    grad_w_up = jnp.einsum("nd,nf->df", normed_two, up_grad, preferred_element_type=jnp.float32)
    normed_two_grad = jnp.einsum(
        "nf,df->nd", gate_grad, back_gate, preferred_element_type=jnp.float32
    ) + jnp.einsum("nf,df->nd", up_grad, back_up, preferred_element_type=jnp.float32)
    grad_gain_ffn = jnp.sum(normed_two_grad * middle * scale_two, axis=0)
    scaled_two = normed_two_grad * gain_two
    middle_grad = scale_two * scaled_two - middle * scale_two**3 * jnp.mean(
        scaled_two * middle, axis=-1, keepdims=True
    )
    attn_grad = (branch_grad + middle_grad).astype(jnp.bfloat16)
    grad_w_output = jnp.einsum(
        "nh,nd->hd", mixed_low, attn_grad, preferred_element_type=jnp.float32
    )
    head_gradient = jnp.einsum(
        "nd,hd->nh", attn_grad, back_output, preferred_element_type=jnp.float32
    ).astype(jnp.bfloat16)
    head_gradient_five = head_gradient.reshape(
        group_count, count_of_rows, KEY_VALUE_HEADS, grouped_heads, HEAD_DIM
    )
    row_delta = jnp.sum(
        head_gradient.astype(jnp.float32).reshape(
            group_count, count_of_rows, KEY_VALUE_HEADS, grouped_heads, HEAD_DIM
        )
        * attention_blended.reshape(
            group_count, count_of_rows, KEY_VALUE_HEADS, grouped_heads, HEAD_DIM
        ),
        axis=-1,
    )
    row_delta = jnp.transpose(row_delta, (0, 2, 3, 1))

    def attend_back_block(running, key_value_block, tag_block, first_row):
        visible = key_sight(query_rows, segment, tag_block, first_row)
        sight = visible[:, None, None, :, :]

        def work(current):
            query_acc, kv_acc = current
            block_of_keys, block_of_values = split_block(key_value_block)
            rows_per_block = key_value_block.shape[1]
            scores = (
                jnp.einsum(
                    "gqkhd,gckd->gkhqc",
                    heads_of_query,
                    block_of_keys,
                    preferred_element_type=jnp.float32,
                )
                * score_scale
            )
            probability = jnp.where(sight, jnp.exp(scores - log_total[..., None]), 0.0)
            value_grad = jnp.einsum(
                "gkhqc,gqkhd->gckd",
                probability.astype(jnp.bfloat16),
                head_gradient_five,
                preferred_element_type=jnp.float32,
            )
            prob_grad = jnp.einsum(
                "gqkhd,gckd->gkhqc",
                head_gradient_five,
                block_of_values,
                preferred_element_type=jnp.float32,
            )
            score_grad = (probability * (prob_grad - row_delta[..., None])).astype(jnp.bfloat16)
            query_acc = (
                query_acc
                + jnp.einsum(
                    "gkhqc,gckd->gkhqd",
                    score_grad,
                    block_of_keys,
                    preferred_element_type=jnp.float32,
                )
                * score_scale
            )
            key_grad = (
                jnp.einsum(
                    "gkhqc,gqkhd->gckd",
                    score_grad,
                    heads_of_query,
                    preferred_element_type=jnp.float32,
                )
                * score_scale
            )
            grad_block = jnp.concatenate(
                [
                    key_grad.reshape(group_count, rows_per_block, key_value_width),
                    value_grad.reshape(group_count, rows_per_block, key_value_width),
                ],
                axis=-1,
            )
            kv_acc = lax.dynamic_update_slice_in_dim(kv_acc, grad_block, first_row, 1)
            return (query_acc, kv_acc)

        return lax.cond(jnp.any(visible), work, lambda current: current, running)

    query_start_index = jnp.zeros(
        (group_count, KEY_VALUE_HEADS, grouped_heads, count_of_rows, HEAD_DIM), jnp.float32
    )
    start_kv = jnp.zeros((group_count, group_rows, 2 * key_value_width), jnp.float32)
    query_acc, kv_acc = over_blocks(
        attend_back_block,
        (query_start_index, start_kv),
        (
            lax.all_gather(kv_local, "fsdp", axis=1, tiled=True),
            lax.all_gather(tag_local, "fsdp", axis=1, tiled=True),
        ),
        jnp.int32(0),
    )
    key_value_local = (
        lax.psum_scatter(kv_acc.astype(jnp.bfloat16), "fsdp", scatter_dimension=1, tiled=True)
        .astype(jnp.float32)
        .reshape(count_of_tokens, 2 * key_value_width)
    )
    query_back = apply_rotary(
        jnp.transpose(query_acc, (0, 3, 1, 2, 4)).reshape(
            count_of_tokens, QUERY_HEAD_COUNT, HEAD_DIM
        ),
        cosine_table,
        -sine_table,
    )
    query_back = query_back.reshape(count_of_tokens, QUERY_HEAD_COUNT * HEAD_DIM).astype(
        jnp.bfloat16
    )
    key_reverse = apply_rotary(
        key_value_local[:, :key_value_width].reshape(count_of_tokens, KEY_VALUE_HEADS, HEAD_DIM),
        cosine_table,
        -sine_table,
    )
    key_reverse = key_reverse.reshape(count_of_tokens, key_value_width).astype(jnp.bfloat16)
    value_back = key_value_local[:, key_value_width:].astype(jnp.bfloat16)
    grad_w_query = jnp.einsum(
        "nd,nh->dh", first_normed, query_back, preferred_element_type=jnp.float32
    )
    grad_w_key = jnp.einsum(
        "nd,nh->dh", first_normed, key_reverse, preferred_element_type=jnp.float32
    )
    grad_w_value = jnp.einsum(
        "nd,nh->dh", first_normed, value_back, preferred_element_type=jnp.float32
    )
    normed_one_grad = jnp.einsum(
        "nh,dh->nd", query_back, back_query, preferred_element_type=jnp.float32
    )
    normed_one_grad = normed_one_grad + jnp.einsum(
        "nh,dh->nd", key_reverse, back_key, preferred_element_type=jnp.float32
    )
    normed_one_grad = normed_one_grad + jnp.einsum(
        "nh,dh->nd", value_back, back_value, preferred_element_type=jnp.float32
    )
    grad_gain_attn = jnp.sum(normed_one_grad * inputs * scale_one, axis=0)
    scaled_one = normed_one_grad * gain_one
    grad_in = upstream + logit_grad[:, None] * router_wide[None, :] + middle_grad
    grad_in = (
        grad_in
        + scale_one * scaled_one
        - inputs * scale_one**3 * jnp.mean(scaled_one * inputs, axis=-1, keepdims=True)
    )
    vector_sums = lax.psum((grad_gain_attn, grad_gain_ffn, grad_router), ("dp", "fsdp"))
    owned = scatter_grads(
        (grad_w_query, grad_w_key, grad_w_value, grad_w_output, grad_w_gate, grad_w_up, grad_w_down)
    )
    return (
        hidden_out,
        grad_in.reshape(group_count, count_of_rows, model_width),
        vector_sums[0],
        vector_sums[1],
        vector_sums[2],
        owned[0],
        owned[1],
        owned[2],
        owned[3],
        owned[4],
        owned[5],
        owned[6],
    )


def solution(mesh):
    return jax.shard_map(
        shards,
        mesh=mesh,
        in_specs=(
            P("dp", "fsdp", None),
            P("dp", "fsdp"),
            P("dp", "fsdp"),
            P("dp", "fsdp"),
            P(),
            P(),
            P(),
            P("dp", "fsdp"),
            P("dp", "fsdp"),
            P("dp", "fsdp"),
            P("fsdp", "dp"),
            P("dp", "fsdp"),
            P("dp", "fsdp"),
            P("fsdp", "dp"),
            P("dp", "fsdp", None),
        ),
        out_specs=(
            P("dp", "fsdp", None),
            P("dp", "fsdp", None),
            P(),
            P(),
            P(),
            P("dp", "fsdp"),
            P("dp", "fsdp"),
            P("dp", "fsdp"),
            P("fsdp", "dp"),
            P("dp", "fsdp"),
            P("dp", "fsdp"),
            P("fsdp", "dp"),
        ),
        check_vma=False,
    )
```

profile of v0, /device:TPU:0, one launch (start us, length us, event | category | flops | bytes accessed | tf_op | source)
XLA Modules:
  0.0 1320.8 jit_solution(11652173049757351501)
XLA Ops:
  10.4 33.5 %all_gather.70 = bf16[240,960]{0,1:T(8,128)(2,1)S(1)} all-gather(bf16[240,120]{0,1:T(8,128)(2,1)S(1)} %copy.471), channel_id=1, replica_groups=mesh['dp'=4,'fsdp'=8] {'fsdp'}, dimensions={1}, use_global_device_ids=true | all-gather | bytes 518400 | tf_op jit(solution)/shard_map/all_gather | solution.py:36
  51.1 30.8 %all_gather.65 = bf16[240,320]{0,1:T(8,128)(2,1)S(1)} all-gather(bf16[240,40]{0,1:T(8,128)(2,1)S(1)} %copy-done.57), channel_id=1, replica_groups=mesh['dp'=4,'fsdp'=8] {'fsdp'}, dimensions={1}, use_global_device_ids=true | all-gather | bytes 172800 | tf_op jit(solution)/shard_map/all_gather | solution.py:37
  81.9 7.9 all-gather
  94.1 31.0 %all_gather.67 = bf16[240,320]{0,1:T(8,128)(2,1)S(1)} all-gather(bf16[240,40]{0,1:T(8,128)(2,1)S(1)} %copy-done.58), channel_id=1, replica_groups=mesh['dp'=4,'fsdp'=8] {'fsdp'}, dimensions={1}, use_global_device_ids=true | all-gather | bytes 172800 | tf_op jit(solution)/shard_map/all_gather | solution.py:38
  134.6 31.8 %all_gather.72 = bf16[960,240]{1,0:T(8,128)(2,1)S(1)} all-gather(bf16[120,240]{1,0:T(8,128)(2,1)S(1)} %copy-done.51), channel_id=1, replica_groups=mesh['dp'=4,'fsdp'=8] {'fsdp'}, dimensions={0}, use_global_device_ids=true | all-gather | bytes 518400 | tf_op jit(solution)/shard_map/all_gather | solution.py:39
  179.3 20.3 %all_gather.64 = bf16[2,2048]{1,0:T(2,128)(2,1)S(1)} all-gather(bf16[2,256]{1,0:T(2,128)(2,1)S(1)} %get-tuple-element.1087), channel_id=1, replica_groups=mesh['dp'=4,'fsdp'=8] {'fsdp'}, dimensions={1}, use_global_device_ids=true | all-gather | bytes 9216 | tf_op jit(solution)/shard_map/all_gather | solution.py:240
  229.4 24.9 %all-gather.12.cloned.1.call-done = bf16[2,2048,640]{1,2,0:T(8,128)(2,1)} async-done(((bf16[2,256,640]{1,2,0:T(8,128)(2,1)}), bf16[2,2048,640]{1,2,0:T(8,128)(2,1)}) %all-gather.12.cloned.1.call-update) | async-done | bytes 5242896 | tf_op jit(solution)/shard_map/all_gather | solution.py:239
  258.8 11.4 conditional.16
  270.4 7.9 conditional.19
  278.3 7.7 conditional.21
  300.6 15.3 %all-gather.20.cloned.1.call-done = bf16[960,2560]{1,0:T(8,128)(2,1)} async-done(((bf16[240,2560]{1,0:T(8,128)(2,1)}), bf16[960,2560]{1,0:T(8,128)(2,1)}) %all-gather.20.cloned.1.call-update) | async-done | bytes 4915216 | tf_op jit(solution)/shard_map/all_gather | solution.py:49
  315.9 7.4 fusion.243
  323.3 32.7 %all-gather.24.cloned.1.call-done = bf16[960,2560]{1,0:T(8,128)(2,1)} async-done(((bf16[240,2560]{1,0:T(8,128)(2,1)}), bf16[960,2560]{1,0:T(8,128)(2,1)}) %all-gather.24.cloned.1.call-update) | async-done | bytes 4915216 | tf_op jit(solution)/shard_map/all_gather | solution.py:50
  363.1 33.2 %all-gather.28.cloned.1.call-done = bf16[2560,960]{0,1:T(8,128)(2,1)} async-done(((bf16[2560,240]{0,1:T(8,128)(2,1)}), bf16[2560,960]{0,1:T(8,128)(2,1)}) %all-gather.28.cloned.1.call-update) | async-done | bytes 4915216 | tf_op jit(solution)/shard_map/all_gather | solution.py:51
  396.3 9.7 multiply_convert_fusion
  427.1 12.0 conditional.24
  455.3 7.9 copy.492
  480.8 116.8 %reduce-scatter.30.cloned.1.call-done = bf16[2,256,640]{2,1,0:T(8,128)(2,1)} async-done(((bf16[2,2048,640]{2,1,0:T(8,128)(2,1)}), bf16[2,256,640]{2,1,0:T(8,128)(2,1)}) %reduce-scatter.30.cloned.1.call-update) | async-done | bytes 655376 | tf_op jit(solution)/shard_map/reduce_scatter | solution.py:390
  632.6 31.1 %reduce-scatter.52.cloned.1.call-done = bf16[240,960]{1,0:T(8,128)(2,1)} async-done(((bf16[960,960]{1,0:T(8,128)(2,1)}), bf16[240,960]{1,0:T(8,128)(2,1)}) %reduce-scatter.52.cloned.1.call-update) | async-done | bytes 460816
  665.9 24.0 %reduce-scatter.48.cloned.1.call-done = bf16[240,320]{1,0:T(8,128)(2,1)} async-done(((bf16[960,320]{1,0:T(8,128)(2,1)}), bf16[240,320]{1,0:T(8,128)(2,1)}) %reduce-scatter.48.cloned.1.call-update) | async-done | bytes 153616
  691.7 23.8 %reduce-scatter.50.cloned.1.call-done = bf16[240,320]{1,0:T(8,128)(2,1)} async-done(((bf16[960,320]{1,0:T(8,128)(2,1)}), bf16[240,320]{1,0:T(8,128)(2,1)}) %reduce-scatter.50.cloned.1.call-update) | async-done | bytes 153616
  717.2 49.9 %reduce-scatter.40.cloned.1.call-done = bf16[240,2560]{1,0:T(8,128)(2,1)} async-done(((bf16[960,2560]{1,0:T(8,128)(2,1)}), bf16[240,2560]{1,0:T(8,128)(2,1)}) %reduce-scatter.40.cloned.1.call-update) | async-done | bytes 1228816 | tf_op jit(solution)/shard_map/reduce_scatter | solution.py:69
  769.7 49.3 %reduce-scatter.42.cloned.1.call-done = bf16[240,2560]{1,0:T(8,128)(2,1)} async-done(((bf16[960,2560]{1,0:T(8,128)(2,1)}), bf16[240,2560]{1,0:T(8,128)(2,1)}) %reduce-scatter.42.cloned.1.call-update) | async-done | bytes 1228816 | tf_op jit(solution)/shard_map/reduce_scatter | solution.py:72
  821.5 49.2 %reduce-scatter.44.cloned.1.call-done = bf16[2560,240]{0,1:T(8,128)(2,1)} async-done(((bf16[2560,960]{0,1:T(8,128)(2,1)}), bf16[2560,240]{0,1:T(8,128)(2,1)}) %reduce-scatter.44.cloned.1.call-update) | async-done | bytes 1228816 | tf_op jit(solution)/shard_map/reduce_scatter | solution.py:75
  880.5 53.0 %reduce-scatter.46.cloned.1.call-done = bf16[120,240]{1,0:T(8,128)(2,1)} async-done(((bf16[960,240]{1,0:T(8,128)(2,1)}), bf16[120,240]{1,0:T(8,128)(2,1)}) %reduce-scatter.46.cloned.1.call-update) | async-done | bytes 57616
  935.1 60.4 %reduce-scatter.38.cloned.1.call-done = bf16[120,240]{1,0:T(8,128)(2,1)} async-done(((bf16[960,240]{1,0:T(8,128)(2,1)}), bf16[120,240]{1,0:T(8,128)(2,1)}) %reduce-scatter.38.cloned.1.call-update) | async-done | bytes 57616 | tf_op jit(solution)/shard_map/reduce_scatter | solution.py:89
  1005.2 40.2 %all-reduce.1 = (f32[960]{0:T(1024)}, f32[960]{0:T(1024)}, f32[960]{0:T(1024)}) all-reduce(f32[960]{0:T(1024)S(1)} %get-tuple-element.966, f32[960]{0:T(1024)S(1)} %copy-done.88, f32[960]{0:T(1024)S(1)} %bitcast.893), channel_id=1, replica_groups=mesh['dp'=4,'fsdp'=8] {'dp','fsdp'}, use_global_device_ids=true, to_apply=%region_64.65 | all-reduce | flops 2880 | bytes 23040 | tf_op jit(solution)/shard_map/psum | solution.py:437
  1045.4 7.4 reduce-scatter.34.cloned.1.call-done
  1054.1 56.1 %reduce-scatter.36.cloned.1.call-done = bf16[240,40]{0,1:T(8,128)(2,1)} async-done(((bf16[240,320]{0,1:T(8,128)(2,1)}), bf16[240,40]{0,1:T(8,128)(2,1)}) %reduce-scatter.36.cloned.1.call-update) | async-done | bytes 19216 | tf_op jit(solution)/shard_map/reduce_scatter | solution.py:86
  1111.5 65.9 %reduce-scatter.54.cloned.1.call-done = bf16[320,240]{1,0:T(8,128)(2,1)} async-done(((bf16[2560,240]{1,0:T(8,128)(2,1)}), bf16[320,240]{1,0:T(8,128)(2,1)}) %reduce-scatter.54.cloned.1.call-update) | async-done | bytes 153616
  1179.3 65.2 %reduce-scatter.56.cloned.1.call-done = bf16[320,240]{1,0:T(8,128)(2,1)} async-done(((bf16[2560,240]{1,0:T(8,128)(2,1)}), bf16[320,240]{1,0:T(8,128)(2,1)}) %reduce-scatter.56.cloned.1.call-update) | async-done | bytes 153616
  1246.5 65.1 %reduce-scatter.58.cloned.1.call-done = bf16[320,240]{1,0:T(8,128)(2,1)} async-done(((bf16[2560,240]{1,0:T(8,128)(2,1)}), bf16[320,240]{1,0:T(8,128)(2,1)}) %reduce-scatter.58.cloned.1.call-update) | async-done | bytes 153616
  (395 shorter events, 240.1 us)
Async XLA Ops:
  7.2 160.3 %all-gather.18.cloned.1.call-start = ((), (), s32[]{:S(2)}) async-start(), calls=%async_computation.18 | async-start | bytes 1474560 | tf_op jit(solution)/shard_map/all_gather | solution.py:40
  7.9 162.1 %all-gather.22.cloned.1.call-start = ((), (), s32[]{:S(2)}) async-start(), calls=%async_computation.20 | async-start | bytes 1474560 | tf_op jit(solution)/shard_map/all_gather | solution.py:41
  8.7 164.0 %all-gather.26.cloned.1.call-start = ((), (), s32[]{:S(2)}) async-start(), calls=%async_computation.22 | async-start | bytes 1474560 | tf_op jit(solution)/shard_map/all_gather | solution.py:42
  9.4 212.5 %all-gather.14.cloned.1.call-start = ((), (), s32[]{:S(2)}) async-start(), calls=%async_computation.16 | async-start | bytes 2457600 | tf_op jit(solution)/shard_map/all_gather | solution.py:45
  44.9 209.4 %all-gather.12.cloned.1.call-start = ((), (), s32[]{:S(2)}) async-start(), calls=%async_computation.15 | async-start | bytes 5898240 | tf_op jit(solution)/shard_map/all_gather | solution.py:239
  91.9 136.7 %copy-start.27 = (f32[512,32]{0,1:T(8,128)}, f32[512,32]{0,1:T(8,128)S(1)}, u32[]{:S(2)}) copy-start(f32[512,32]{0,1:T(8,128)S(1)} %get-tuple-element.1083) | copy-start | bytes 196612
  94.0 323.0 %copy-start = (bf16[2,120,8,256]{3,2,0,1:T(8,128)(2,1)}, bf16[2,120,8,256]{3,2,0,1:T(8,128)(2,1)S(1)}, u32[]{:S(2)}) copy-start(bf16[2,120,8,256]{3,2,0,1:T(8,128)(2,1)S(1)} %copy.597) | copy-start | bytes 2949124
  134.5 161.4 %all-gather.16.cloned.1.call-start = ((), (), s32[]{:S(2)}) async-start(), calls=%async_computation.17 | async-start | bytes 2457600 | tf_op jit(solution)/shard_map/all_gather | solution.py:48
  167.4 148.5 %all-gather.20.cloned.1.call-start = ((), (), s32[]{:S(2)}) async-start(), calls=%async_computation.19 | async-start | bytes 6144000 | tf_op jit(solution)/shard_map/all_gather | solution.py:49
  170.0 186.1 %all-gather.24.cloned.1.call-start = ((), (), s32[]{:S(2)}) async-start(), calls=%async_computation.21 | async-start | bytes 6144000 | tf_op jit(solution)/shard_map/all_gather | solution.py:50
  172.6 223.6 %all-gather.28.cloned.1.call-start = ((), (), s32[]{:S(2)}) async-start(), calls=%async_computation.23 | async-start | bytes 6144000 | tf_op jit(solution)/shard_map/all_gather | solution.py:51
  175.3 422.2 %reduce-scatter.30.cloned.1.call-start = ((), (), s32[]{:S(2)}) async-start(), calls=%async_computation.24 | async-start | bytes 5898240 | tf_op jit(solution)/shard_map/reduce_scatter | solution.py:390
  213.6 203.5 %copy-start.53 = (f32[960]{0:T(1024)}, f32[960]{0:T(1024)S(1)}, u32[]{:S(2)}) copy-start(f32[960]{0:T(1024)S(1)} %convert_element_type.359) | copy-start | bytes 11524
  217.0 200.1 %copy-start.90 = (f32[512]{0:T(512)}, f32[512]{0:T(512)S(1)}, u32[]{:S(2)}) copy-start(f32[512]{0:T(512)S(1)} %fusion.213) | copy-start | bytes 6148
  299.0 118.1 %copy-start.61 = (f32[512]{0:T(512)}, f32[512]{0:T(512)S(1)}, u32[]{:S(2)}) copy-start(f32[512]{0:T(512)S(1)} %get-tuple-element.1085) | copy-start | bytes 6148
  463.2 167.3 %reduce-scatter.32.cloned.1.call-start = ((), (), s32[]{:S(2)}) async-start(), calls=%async_computation.25 | async-start | bytes 2457600 | tf_op jit(solution)/shard_map/reduce_scatter | solution.py:57
  475.4 188.4 %reduce-scatter.52.cloned.1.call-start = ((), (), s32[]{:S(2)}) async-start(), calls=%async_computation.35 | async-start | bytes 2457600
  480.7 122.0 %copy-start.1 = (bf16[2,120,8,256]{3,2,0,1:T(8,128)(2,1)S(1)}, bf16[2,120,8,256]{3,2,0,1:T(8,128)(2,1)}, u32[]{:S(2)}) copy-start(bf16[2,120,8,256]{3,2,0,1:T(8,128)(2,1)} %copy-done) | copy-start | bytes 2949124
  480.7 122.0 %copy-start.56 = (f32[1,2,2,128]{3,1,2,0:T(2,128)S(1)}, f32[1,2,2,128]{3,1,2,0:T(2,128)}, u32[]{:S(2)}) copy-start(f32[1,2,2,128]{3,1,2,0:T(2,128)} %copy-done.55) | copy-start | bytes 6148
  480.7 209.2 %reduce-scatter.48.cloned.1.call-start = ((), (), s32[]{:S(2)}) async-start(), calls=%async_computation.33 | async-start | bytes 921600
  602.6 112.8 %reduce-scatter.50.cloned.1.call-start = ((), (), s32[]{:S(2)}) async-start(), calls=%async_computation.34 | async-start | bytes 921600
  605.8 161.3 %reduce-scatter.40.cloned.1.call-start = ((), (), s32[]{:S(2)}) async-start(), calls=%async_computation.29 | async-start | bytes 6144000 | tf_op jit(solution)/shard_map/reduce_scatter | solution.py:69
  612.1 206.8 %reduce-scatter.42.cloned.1.call-start = ((), (), s32[]{:S(2)}) async-start(), calls=%async_computation.30 | async-start | bytes 6144000 | tf_op jit(solution)/shard_map/reduce_scatter | solution.py:72
  618.4 252.2 %reduce-scatter.44.cloned.1.call-start = ((), (), s32[]{:S(2)}) async-start(), calls=%async_computation.31 | async-start | bytes 6144000 | tf_op jit(solution)/shard_map/reduce_scatter | solution.py:75
  626.0 307.5 %reduce-scatter.46.cloned.1.call-start = ((), (), s32[]{:S(2)}) async-start(), calls=%async_computation.32 | async-start | bytes 552960
  632.6 362.9 %reduce-scatter.38.cloned.1.call-start = ((), (), s32[]{:S(2)}) async-start(), calls=%async_computation.28 | async-start | bytes 552960 | tf_op jit(solution)/shard_map/reduce_scatter | solution.py:89
  663.8 157.7 %copy-start.87 = (bf16[960]{0:T(1024)(128)(2,1)S(1)}, bf16[960]{0:T(1024)(128)(2,1)}, u32[]{:S(2)}) copy-start(bf16[960]{0:T(1024)(128)(2,1)} %param.53) | copy-start | bytes 5764
  665.8 386.9 %reduce-scatter.34.cloned.1.call-start = ((), (), s32[]{:S(2)}) async-start(), calls=%async_computation.26 | async-start | bytes 184320 | tf_op jit(solution)/shard_map/reduce_scatter | solution.py:83
  691.6 418.6 %reduce-scatter.36.cloned.1.call-start = ((), (), s32[]{:S(2)}) async-start(), calls=%async_computation.27 | async-start | bytes 184320 | tf_op jit(solution)/shard_map/reduce_scatter | solution.py:86
  717.2 460.2 %reduce-scatter.54.cloned.1.call-start = ((), (), s32[]{:S(2)}) async-start(), calls=%async_computation.36 | async-start | bytes 1474560
  769.6 475.0 %reduce-scatter.56.cloned.1.call-start = ((), (), s32[]{:S(2)}) async-start(), calls=%async_computation.37 | async-start | bytes 1474560
  821.4 490.1 %reduce-scatter.58.cloned.1.call-start = ((), (), s32[]{:S(2)}) async-start(), calls=%async_computation.38 | async-start | bytes 1474560
  (80 other events, 1305.2 us)
Sparse Core Ops, SparseCore 0:
  10.2 45.9 all-gather.17
  58.3 40.9 all-gather.21
  101.5 41.9 all-gather.25
  144.9 20.0 all-gather.13
  166.9 87.3 all-gather.11
  255.7 20.0 all-gather.15
  277.3 38.5 all-gather.19
  317.5 38.5 all-gather.23
  357.6 38.5 all-gather.27
  463.4 134.1 reduce-scatter.29
  600.1 30.3 reduce-scatter.31
  633.1 30.6 reduce-scatter.51
  666.9 22.9 reduce-scatter.47
  692.4 22.9 reduce-scatter.49
  717.9 49.1 reduce-scatter.39
  769.7 49.1 reduce-scatter.41
  821.4 49.1 reduce-scatter.43
  874.1 59.3 reduce-scatter.45
  937.2 58.3 reduce-scatter.37
  999.4 53.2 reduce-scatter.33
  1056.8 53.3 reduce-scatter.35
  1113.9 63.3 reduce-scatter.53
  1181.2 63.3 reduce-scatter.55
  1248.2 63.3 reduce-scatter.57
where the time goes:
time: 1330 us; the launch traced here: 1320 us
  waiting for transfers between devices  830 us (62%)
  blocking collectives  202 us (15%)
  matrix products  99.8 us (8%)
  local copies, waits for them, and re-layouts  92.8 us (7%)
  other arithmetic  38.4 us (3%)
  loops' own time  34.8 us (3%)
  between operations  21.3 us (2%)
    unnamed x31, waiting for transfers between devices  330 us
    reduce_scatter x1, waiting for transfers between devices, shards(): lax.psum_scatter(kv_acc.astype(jnp.bfloat16), 'fsdp', scatter_dimension=1...  117 us
    reduce_scatter x1, waiting for transfers between devices, scatter_grads(): lax.psum_scatter(sectioned[3].astype(jnp.bfloat16), 'fsdp', scatter_dimen...  60.4 us
    reduce_scatter x1, waiting for transfers between devices, scatter_grads(): lax.psum_scatter(sectioned[2].astype(jnp.bfloat16), 'fsdp', scatter_dimen...  56.1 us
    reduce_scatter x1, waiting for transfers between devices, scatter_grads(): lax.psum_scatter(terms[4].astype(jnp.bfloat16), 'dp', scatter_dimension=0...  49.9 us
    reduce_scatter x1, waiting for transfers between devices, scatter_grads(): lax.psum_scatter(terms[5].astype(jnp.bfloat16), 'dp', scatter_dimension=0...  49.3 us
    reduce_scatter x1, waiting for transfers between devices, scatter_grads(): lax.psum_scatter(terms[6].astype(jnp.bfloat16), 'dp', scatter_dimension=1...  49.2 us
    unnamed x203, local copies, waits for them, and re-layouts  40.8 us
  transfers between devices with their start and end apart: 24, of which 19 were waited for; matrix products, arithmetic and copies ran while one was open for 13% of the time, Pallas kernels for 0%

commit v1 on v0

v1 whole, which is shorter than its diff:
```python
import functools
import math

import jax
import jax.numpy as jnp
import numpy as np
from jax import lax
from jax.experimental import pallas as pl
from jax.experimental.pallas import tpu as pltpu
from jax.sharding import PartitionSpec as P

QUERY_HEADS = 15
KV_HEADS = 5
SHARE = QUERY_HEADS // KV_HEADS
HEAD_DIM = 64
TILE = 128
PROMPT = 1024
LONGEST = 192
EPSILON = 1e-05
THETA = 10000.0
MINUS_LARGE = -1e30
AXES = ("dp", "fsdp")
F32 = jnp.float32
BF16 = jnp.bfloat16
VMEM_BYTES = 60 * 1024 * 1024

NT = (((1,), (1,)), ((), ()))
NN = (((1,), (0,)), ((), ()))
TN = (((0,), (0,)), ((), ()))


def dot(a, b, dims=NN):
    return lax.dot_general(a, b, dims, preferred_element_type=F32)


def params(steps=0):
    return pltpu.CompilerParams(
        vmem_limit_bytes=VMEM_BYTES,
        dimension_semantics=("arbitrary",) * steps if steps else None,
    )


def cost(flops, moved, exps=0):
    return pl.CostEstimate(flops=int(flops), bytes_accessed=int(moved), transcendentals=int(exps))


def whole(shape):
    zeros = (0,) * len(shape)
    return pl.BlockSpec(shape, lambda *_: zeros)


def norm_kernel(hid_ref, cot_ref, gain_ref, router_ref, sel_ref, xn_ref, s1_ref, fg_ref, mix_ref, slope_ref):
    parts, _, width = hid_ref.shape
    square = 0.0
    logit = 0.0
    for d in range(parts):
        x = hid_ref[d].astype(F32)
        square = square + jnp.sum(x * x, axis=-1, keepdims=True)
        logit = logit + jnp.sum(x * router_ref[d], axis=-1, keepdims=True)
    scale = lax.rsqrt(square / (parts * width) + EPSILON)
    chance = 1.0 / (1.0 + jnp.exp(-logit))
    mix = sel_ref[...] * chance
    s1_ref[...] = scale
    mix_ref[...] = mix
    slope_ref[...] = mix * (1.0 - chance)
    for d in range(parts):
        x = hid_ref[d].astype(F32)
        xn_ref[d] = (x * scale * gain_ref[d]).astype(BF16)
        fg_ref[d] = (cot_ref[d].astype(F32) * mix).astype(BF16)


def first_norm(hid4, cot4, gain, router, chosen):
    parts, tokens, width = hid4.shape
    rows = 128
    block = pl.BlockSpec((parts, rows, width), lambda i: (0, i, 0))
    column = pl.BlockSpec((rows, 1), lambda i: (i, 0))
    vector = whole((parts, 1, width))
    return pl.pallas_call(
        norm_kernel,
        grid=(tokens // rows,),
        in_specs=[block, block, vector, vector, column],
        out_specs=[block, column, block, column, column],
        out_shape=[
            jax.ShapeDtypeStruct(hid4.shape, BF16),
            jax.ShapeDtypeStruct((tokens, 1), F32),
            jax.ShapeDtypeStruct(hid4.shape, BF16),
            jax.ShapeDtypeStruct((tokens, 1), F32),
            jax.ShapeDtypeStruct((tokens, 1), F32),
        ],
        compiler_params=params(1),
        cost_estimate=cost(tokens * 960 * 10, tokens * 960 * 8),
        name="first_norm",
    )(hid4, cot4, gain, router, chosen)


def kv_kernel(xn_ref, w_ref, cos_ref, sin1_ref, sin2_ref, tag_ref, out_ref):
    rows = xn_ref.shape[1]
    total = 0.0
    for d in range(xn_ref.shape[0]):
        total = total + dot(xn_ref[d], w_ref[d], NT)
    for h in range(KV_HEADS):
        u = total[:, h * TILE : (h + 1) * TILE]
        turned = (
            u * cos_ref[...]
            + pltpu.roll(u, TILE - HEAD_DIM // 2, 1) * sin1_ref[...]
            + pltpu.roll(u, HEAD_DIM // 2, 1) * sin2_ref[...]
        )
        out_ref[0, :rows, h * TILE : (h + 1) * TILE] = turned.astype(BF16)
        out_ref[0, rows:, h * TILE : (h + 1) * TILE] = tag_ref[0]


def kv_project(xn4, wkv, tables, tags, groups):
    parts, tokens, width = xn4.shape
    rows = tokens // groups
    table = pl.BlockSpec((rows, TILE), lambda g: (g, 0))
    return pl.pallas_call(
        kv_kernel,
        grid=(groups,),
        in_specs=[
            pl.BlockSpec((parts, rows, width), lambda g: (0, g, 0)),
            whole(wkv.shape),
            table,
            table,
            table,
            pl.BlockSpec((1, 16, TILE), lambda g: (g, 0, 0)),
        ],
        out_specs=pl.BlockSpec((1, rows + 16, KV_HEADS * TILE), lambda g: (g, 0, 0)),
        out_shape=jax.ShapeDtypeStruct((groups, rows + 16, KV_HEADS * TILE), BF16),
        compiler_params=params(1),
        cost_estimate=cost(2 * tokens * 960 * 640, 3 * tokens * 960 * 2),
        name="kv_project",
    )(xn4, wkv, *tables, tags)


def q_kernel(xn_ref, w_ref, cos_ref, sin_ref, out_ref):
    for h in range(QUERY_HEADS):
        u = 0.0
        for d in range(xn_ref.shape[0]):
            u = u + dot(xn_ref[d], w_ref[d, h * TILE : (h + 1) * TILE], NT)
        turned = u * cos_ref[...] + pltpu.roll(u, HEAD_DIM, 1) * sin_ref[...]
        out_ref[:, h * TILE : (h + 1) * TILE] = turned.astype(BF16)


def q_project(xn4, wq_pad, cos_q, sin_q, groups):
    parts, tokens, width = xn4.shape
    rows = tokens // groups
    table = pl.BlockSpec((rows, TILE), lambda g: (g, 0))
    return pl.pallas_call(
        q_kernel,
        grid=(groups,),
        in_specs=[
            pl.BlockSpec((parts, rows, width), lambda g: (0, g, 0)),
            whole(wq_pad.shape),
            table,
            table,
        ],
        out_specs=pl.BlockSpec((rows, QUERY_HEADS * TILE), lambda g: (g, 0)),
        out_shape=jax.ShapeDtypeStruct((tokens, QUERY_HEADS * TILE), BF16),
        compiler_params=params(1),
        cost_estimate=cost(2 * tokens * 960 * 1920, 6 * tokens * 960 * 2),
        name="q_project",
    )(xn4, wq_pad, cos_q, sin_q)


def slot_needed(slot_ref, s, rows):
    own = slot_ref[0]
    block = slot_ref[s]
    prompt_blocks = PROMPT // rows
    reach = -(-(LONGEST - 1) // rows)
    near = (block < prompt_blocks) | (block >= own - reach)
    return (block >= 0) & (block <= own) & near


def fill_bias(slot_ref, seg_ref, kv_refs, bias_ref):
    rows = bias_ref.shape[1]
    for s, kv_ref in enumerate(kv_refs):

        @pl.when(slot_needed(slot_ref, s, rows))
        def _(s=s, kv_ref=kv_ref):
            for i in range(rows // TILE):
                tag_row = kv_ref[0, rows : rows + 16, 0:TILE].astype(F32)[i : i + 1]
                tag = jnp.broadcast_to(tag_row, (TILE, TILE)).T
                for j in range(rows // TILE):
                    seg = seg_ref[0, :, j * TILE : (j + 1) * TILE]
                    allowed = (tag == 0.0) | (tag == seg)
                    if s == 0:
                        key_row = i * TILE + lax.broadcasted_iota(jnp.int32, (TILE, TILE), 0)
                        query_row = j * TILE + lax.broadcasted_iota(jnp.int32, (TILE, TILE), 1)
                        allowed = (allowed & (key_row <= query_row)) | (key_row == query_row)
                    bias_ref[s, i * TILE : (i + 1) * TILE, j * TILE : (j + 1) * TILE] = jnp.where(
                        allowed, 0.0, MINUS_LARGE
                    )


def stack_heads(ref):
    return jnp.concatenate([ref[:, j * TILE : (j + 1) * TILE] for j in range(SHARE)], axis=0)


def forward_kernel(slot_ref, q_ref, seg_ref, *refs):
    slots = len(refs) - 6
    kv_refs = refs[:slots]
    o_ref, lse_ref, bias_ref, peak_ref, total_ref, acc_ref = refs[slots:]
    rows = q_ref.shape[0]

    @pl.when(pl.program_id(1) == 0)
    def _():
        fill_bias(slot_ref, seg_ref, kv_refs, bias_ref)

    q = stack_heads(q_ref)

    def scores(s):
        kv = kv_refs[s][0, :rows, :]
        bias = bias_ref[s]
        return kv, dot(kv, q, NT) + jnp.concatenate([bias] * SHARE, axis=1)

    kv, score = scores(0)
    peak = jnp.max(score, axis=0, keepdims=True)
    weights = jnp.exp(score - peak)
    peak_ref[...] = peak
    total_ref[...] = jnp.sum(weights, axis=0, keepdims=True)
    acc_ref[...] = dot(kv, weights.astype(BF16), TN)

    for s in range(1, slots):

        @pl.when(slot_needed(slot_ref, s, rows))
        def _(s=s):
            kv, score = scores(s)
            old = peak_ref[...]
            peak = jnp.maximum(old, jnp.max(score, axis=0, keepdims=True))
            fade = jnp.exp(old - peak)
            weights = jnp.exp(score - peak)
            peak_ref[...] = peak
            total_ref[...] = total_ref[...] * fade + jnp.sum(weights, axis=0, keepdims=True)
            acc_ref[...] = acc_ref[...] * fade + dot(kv, weights.astype(BF16), TN)

    total = total_ref[...]
    lse_ref[0, 0] = peak_ref[...] + jnp.log(total)
    mixed = (acc_ref[...] / total).T
    lane = lax.broadcasted_iota(jnp.int32, mixed.shape, 1)
    mixed = jnp.where(lane >= HEAD_DIM, mixed, 0.0).astype(BF16)
    for j in range(SHARE):
        o_ref[:, j * TILE : (j + 1) * TILE] = mixed[j * rows : (j + 1) * rows]


def attention_specs(groups, rows, slots):
    heads = pl.BlockSpec((rows, SHARE * TILE), lambda g, h, _: (g, h))
    seg = pl.BlockSpec((1, 1, rows), lambda g, h, _: (g, 0, 0))
    kv = pl.BlockSpec((1, rows + 16, TILE), lambda g, h, _: (g, 0, h))
    lse = pl.BlockSpec((1, 1, 1, SHARE * rows), lambda g, h, _: (g, h, 0, 0))
    return heads, seg, kv, lse


def attention_forward(slot_ids, q, seg, kvs):
    groups = kvs[0].shape[0]
    tokens = q.shape[0]
    rows = tokens // groups
    slots = len(kvs)
    heads, seg_spec, kv_spec, lse_spec = attention_specs(groups, rows, slots)
    wide = SHARE * rows
    return pl.pallas_call(
        forward_kernel,
        grid_spec=pltpu.PrefetchScalarGridSpec(
            num_scalar_prefetch=1,
            grid=(groups, KV_HEADS),
            in_specs=[heads, seg_spec] + [kv_spec] * slots,
            out_specs=[heads, lse_spec],
            scratch_shapes=[
                pltpu.VMEM((slots, rows, rows), F32),
                pltpu.VMEM((1, wide), F32),
                pltpu.VMEM((1, wide), F32),
                pltpu.VMEM((TILE, wide), F32),
            ],
        ),
        out_shape=[
            jax.ShapeDtypeStruct(q.shape, BF16),
            jax.ShapeDtypeStruct((groups, KV_HEADS, 1, wide), F32),
        ],
        compiler_params=params(2),
        cost_estimate=cost(2 * 15 * tokens * 1536 * 256, 8 * tokens * 960 * 2, 15 * tokens * 1536),
        name="attention_forward",
    )(slot_ids, q, seg, *kvs)


def backward_kernel(slot_ref, q_ref, do_ref, o_ref, lse_ref, seg_ref, cos_ref, sin1_ref, sin2_ref, *refs):
    slots = (len(refs) - 3) // 2
    kv_refs = refs[:slots]
    dq_ref = refs[slots]
    dkv_refs = refs[slots + 1 : 2 * slots + 1]
    bias_ref, acc_ref = refs[2 * slots + 1 :]
    rows = q_ref.shape[0]

    @pl.when(pl.program_id(1) == 0)
    def _():
        fill_bias(slot_ref, seg_ref, kv_refs, bias_ref)

    q = stack_heads(q_ref)
    do = stack_heads(do_ref)
    o = stack_heads(o_ref)
    delta = jnp.sum((do.astype(F32) * o.astype(F32)).T, axis=0, keepdims=True)
    lse = lse_ref[0, 0]

    for s in range(slots):

        def work(s=s):
            kv = kv_refs[s][0, :rows, :]
            bias = bias_ref[s]
            score = dot(kv, q, NT) + jnp.concatenate([bias] * SHARE, axis=1)
            prob = jnp.exp(score - lse)
            slope = (prob * (dot(kv, do, NT) - delta)).astype(BF16)
            dkv_refs[s][0] = (dot(slope, q) + dot(prob.astype(BF16), do)).astype(BF16)
            return dot(kv, slope, TN)

        if s == 0:
            acc_ref[...] = work()
        else:
            needed = slot_needed(slot_ref, s, rows)

            @pl.when(needed)
            def _(s=s, work=work):
                acc_ref[...] += work()

            @pl.when(jnp.logical_not(needed))
            def _(s=s):
                dkv_refs[s][0] = jnp.zeros((rows, TILE), BF16)

    u = acc_ref[...].T
    for j in range(SHARE):
        part = u[j * rows : (j + 1) * rows]
        back = (
            part * cos_ref[...]
            - pltpu.roll(part, TILE - HEAD_DIM // 2, 1) * sin1_ref[...]
            - pltpu.roll(part, HEAD_DIM // 2, 1) * sin2_ref[...]
        )
        dq_ref[:, j * TILE : (j + 1) * TILE] = back.astype(BF16)


def attention_backward(slot_ids, q, do, o, lse, seg, tables, kvs):
    groups = kvs[0].shape[0]
    tokens = q.shape[0]
    rows = tokens // groups
    slots = len(kvs)
    heads, seg_spec, kv_spec, lse_spec = attention_specs(groups, rows, slots)
    table = pl.BlockSpec((rows, TILE), lambda g, h, _: (g, 0))
    grad = pl.BlockSpec((1, rows, TILE), lambda g, h, _: (g, 0, h))
    wide = SHARE * rows
    out = pl.pallas_call(
        backward_kernel,
        grid_spec=pltpu.PrefetchScalarGridSpec(
            num_scalar_prefetch=1,
            grid=(groups, KV_HEADS),
            in_specs=[heads, heads, heads, lse_spec, seg_spec, table, table, table] + [kv_spec] * slots,
            out_specs=[heads] + [grad] * slots,
            scratch_shapes=[
                pltpu.VMEM((slots, rows, rows), F32),
                pltpu.VMEM((TILE, wide), F32),
            ],
        ),
        out_shape=[jax.ShapeDtypeStruct(q.shape, BF16)]
        + [jax.ShapeDtypeStruct((groups, rows, KV_HEADS * TILE), BF16)] * slots,
        compiler_params=params(2),
        cost_estimate=cost(5 * 15 * tokens * 1536 * 256, 16 * tokens * 960 * 2, 15 * tokens * 1536),
        name="attention_backward",
    )(slot_ids, q, do, o, lse, seg, *tables, *kvs)
    return out[0], out[1:]


def out_kernel(o_ref, w_ref, hid_ref, gain_ref, mid_ref, x2_ref, s2_ref):
    parts, _, width = hid_ref.shape
    o = o_ref[...]
    square = 0.0
    for d in range(parts):
        middle = hid_ref[d].astype(F32) + dot(o, w_ref[d])
        mid_ref[d] = middle
        square = square + jnp.sum(middle * middle, axis=-1, keepdims=True)
    scale = lax.rsqrt(square / (parts * width) + EPSILON)
    s2_ref[...] = scale
    for d in range(parts):
        x2_ref[d] = (mid_ref[d] * scale * gain_ref[d]).astype(BF16)


def out_project(o, wo_pad, hid4, gain):
    parts, tokens, width = hid4.shape
    rows = 128
    block = pl.BlockSpec((parts, rows, width), lambda i: (0, i, 0))
    column = pl.BlockSpec((rows, 1), lambda i: (i, 0))
    return pl.pallas_call(
        out_kernel,
        grid=(tokens // rows,),
        in_specs=[
            pl.BlockSpec((rows, o.shape[1]), lambda i: (i, 0)),
            whole(wo_pad.shape),
            block,
            whole((parts, 1, width)),
        ],
        out_specs=[block, block, column],
        out_shape=[
            jax.ShapeDtypeStruct(hid4.shape, F32),
            jax.ShapeDtypeStruct(hid4.shape, BF16),
            jax.ShapeDtypeStruct((tokens, 1), F32),
        ],
        compiler_params=params(1),
        cost_estimate=cost(2 * tokens * 960 * 1920, 8 * tokens * 960 * 2),
        name="out_project",
    )(o, wo_pad, hid4, gain)


def ffn_kernel(meta_ref, x_ref, fg_ref, w_ref, out_ref, xg_ref, keep_ref, send_ref):
    parts = x_ref.shape[0]
    rows = w_ref.shape[2] // 3
    my_part = meta_ref[0]
    odd = meta_ref[1]

    def weight(d, which):
        pair = [w_ref[d, pl.ds(odd ^ i, 1), which * rows : (which + 1) * rows, :] for i in range(2)]
        return jnp.concatenate([p.reshape(rows, p.shape[-1]) for p in pair], axis=0)

    gate = 0.0
    up = 0.0
    hidden_grad = 0.0
    for d in range(parts):
        gate = gate + dot(x_ref[d], weight(d, 0), NT)
        up = up + dot(x_ref[d], weight(d, 1), NT)
        hidden_grad = hidden_grad + dot(fg_ref[d], weight(d, 2), NT)
    chance = 1.0 / (1.0 + jnp.exp(-gate))
    silu = gate * chance
    hidden = (silu * up).astype(BF16)
    up_grad = (hidden_grad * silu).astype(BF16)
    gate_grad = (hidden_grad * up * chance * (1.0 + gate * (1.0 - chance))).astype(BF16)

    first = pl.program_id(0) == 0
    for d in range(parts):
        out = dot(hidden, weight(d, 2))
        back = dot(gate_grad, weight(d, 0)) + dot(up_grad, weight(d, 1))

        @pl.when(first)
        def _(d=d, out=out, back=back):
            out_ref[d] = out
            xg_ref[d] = back

        @pl.when(jnp.logical_not(first))
        def _(d=d, out=out, back=back):
            out_ref[d] += out
            xg_ref[d] += back

    turned = (gate_grad.T, up_grad.T, hidden.T)
    for e in range(parts):
        place = pl.ds(my_part ^ e, 1)
        x = x_ref[place].reshape(x_ref.shape[1:])
        fg = fg_ref[place].reshape(x_ref.shape[1:])
        target = send_ref if e % 2 else keep_ref
        for which in range(3):
            grad = dot(turned[which], fg if which == 2 else x).astype(BF16)
            for i in range(2):
                target[e // 2, i, which * rows : (which + 1) * rows, :] = grad[i * rows : (i + 1) * rows]


def ffn(my_part, my_shard, half, x4, fg4, weights):
    parts, tokens, width = x4.shape
    shards, rows3 = weights.shape[1:3]
    steps = shards // 4
    pair = (my_shard ^ (half * (shards // 2))) // 2
    meta = jnp.stack([my_part, my_shard % 2, pair]).astype(jnp.int32)
    grads = pl.BlockSpec((parts // 2, 2, rows3, width), lambda j, m: (0, j, 0, 0))
    inputs = 2 * tokens * 960 * 2
    return pl.pallas_call(
        ffn_kernel,
        grid_spec=pltpu.PrefetchScalarGridSpec(
            num_scalar_prefetch=1,
            grid=(steps,),
            in_specs=[
                whole(x4.shape),
                whole(x4.shape),
                pl.BlockSpec((parts, 2, rows3, width), lambda j, m: (0, m[2] ^ j, 0, 0)),
            ],
            out_specs=[whole(x4.shape), whole(x4.shape), grads, grads],
        ),
        out_shape=[
            jax.ShapeDtypeStruct(x4.shape, F32),
            jax.ShapeDtypeStruct(x4.shape, F32),
            jax.ShapeDtypeStruct((parts // 2, shards // 2, rows3, width), BF16),
            jax.ShapeDtypeStruct((parts // 2, shards // 2, rows3, width), BF16),
        ],
        compiler_params=params(1),
        cost_estimate=cost(6 * tokens * 960 * rows3 * shards // 2, inputs * 4 + 4 * 960 * rows3 * shards // 2),
        name="ffn",
    )(meta, x4, fg4, weights)


def middle_kernel(
    mid_ref, hid_ref, cot_ref, out_a_ref, out_b_ref, xg_a_ref, xg_b_ref, mix_ref, slope_ref, s2_ref, gain_ref, router_ref,
    hidden_ref, part_ref, ag_ref, router_grad_ref, gain_grad_ref,
):
    parts, rows, width = mid_ref.shape
    mix = mix_ref[...]
    scale = s2_ref[...]
    inner = 0.0
    mean = 0.0
    for d in range(parts):
        middle = mid_ref[d]
        inputs = hid_ref[d].astype(F32)
        branch = (middle - inputs) + (out_a_ref[d] + out_b_ref[d])
        upstream = cot_ref[d].astype(F32)
        inner = inner + jnp.sum(upstream * branch, axis=-1, keepdims=True)
        hidden_ref[d] = (inputs + mix * branch).astype(BF16)
        mean = mean + jnp.sum((xg_a_ref[d] + xg_b_ref[d]) * gain_ref[d] * middle, axis=-1, keepdims=True)
    logit_grad = slope_ref[...] * inner
    mean = mean / (parts * width) * (scale * scale * scale)
    first = pl.program_id(0) == 0
    for d in range(parts):
        middle = mid_ref[d]
        inputs = hid_ref[d].astype(F32)
        upstream = cot_ref[d].astype(F32)
        grad = xg_a_ref[d] + xg_b_ref[d]
        middle_grad = scale * (grad * gain_ref[d]) - middle * mean
        ag_ref[d] = (upstream * mix + middle_grad).astype(BF16)
        part_ref[d] = upstream + logit_grad * router_ref[d] + middle_grad
        router_grad = jnp.sum(logit_grad * inputs, axis=0, keepdims=True)
        gain_grad = jnp.sum(grad * middle * scale, axis=0, keepdims=True)

        @pl.when(first)
        def _(d=d, router_grad=router_grad, gain_grad=gain_grad):
            router_grad_ref[d] = router_grad
            gain_grad_ref[d] = gain_grad

        @pl.when(jnp.logical_not(first))
        def _(d=d, router_grad=router_grad, gain_grad=gain_grad):
            router_grad_ref[d] += router_grad
            gain_grad_ref[d] += gain_grad


def middle_step(mid4, hid4, cot4, outs, grads, mix, slope, s2, gain, router):
    parts, tokens, width = mid4.shape
    rows = 128
    block = pl.BlockSpec((parts, rows, width), lambda i: (0, i, 0))
    column = pl.BlockSpec((rows, 1), lambda i: (i, 0))
    vector = whole((parts, 1, width))
    return pl.pallas_call(
        middle_kernel,
        grid=(tokens // rows,),
        in_specs=[block] * 7 + [column] * 3 + [vector] * 2,
        out_specs=[block, block, block, vector, vector],
        out_shape=[
            jax.ShapeDtypeStruct(mid4.shape, BF16),
            jax.ShapeDtypeStruct(mid4.shape, F32),
            jax.ShapeDtypeStruct(mid4.shape, BF16),
            jax.ShapeDtypeStruct((parts, 1, width), F32),
            jax.ShapeDtypeStruct((parts, 1, width), F32),
        ],
        compiler_params=params(1),
        cost_estimate=cost(tokens * 960 * 30, tokens * 960 * 36),
        name="middle_step",
    )(mid4, hid4, cot4, *outs, *grads, mix, slope, s2, gain, router)


def compact(tile_major, upper):
    count = tile_major.shape[0] // TILE
    start = HEAD_DIM if upper else 0
    return jnp.concatenate(
        [tile_major[h * TILE + start : h * TILE + start + HEAD_DIM] for h in range(count)], axis=0
    )


def out_back_kernel(meta_ref, ag_ref, w_ref, o_ref, do_ref, keep_ref, send_ref):
    parts = ag_ref.shape[0]
    for h in range(QUERY_HEADS):
        total = 0.0
        for d in range(parts):
            total = total + dot(ag_ref[d], w_ref[d, h * TILE : (h + 1) * TILE], NT)
        do_ref[:, h * TILE : (h + 1) * TILE] = total.astype(BF16)
    mixed = compact(o_ref[...].T, True)
    for e in range(parts):
        ag = ag_ref[pl.ds(meta_ref[0] ^ e, 1)].reshape(ag_ref.shape[1:])
        target = send_ref if e % 2 else keep_ref
        target[e // 2] = dot(mixed, ag).astype(BF16)


def out_back(my_part, ag4, wo_pad, o):
    parts, tokens, width = ag4.shape
    grad = jax.ShapeDtypeStruct((parts // 2, QUERY_HEADS * HEAD_DIM, width), BF16)
    return pl.pallas_call(
        out_back_kernel,
        grid_spec=pltpu.PrefetchScalarGridSpec(
            num_scalar_prefetch=1,
            grid=(1,),
            in_specs=[whole(ag4.shape), whole(wo_pad.shape), whole(o.shape)],
            out_specs=[whole(o.shape), whole(grad.shape), whole(grad.shape)],
        ),
        out_shape=[jax.ShapeDtypeStruct(o.shape, BF16), grad, grad],
        compiler_params=params(1),
        cost_estimate=cost(2 * tokens * 960 * 2880, 12 * tokens * 960 * 2),
        name="out_back",
    )(my_part.reshape(1), ag4, wo_pad, o)


def q_back_kernel(meta_ref, dq_ref, xn_ref, keep_ref, send_ref):
    turned = compact(dq_ref[...].T, False)
    for e in range(xn_ref.shape[0]):
        x = xn_ref[pl.ds(meta_ref[0] ^ e, 1)].reshape(xn_ref.shape[1:])
        target = send_ref if e % 2 else keep_ref
        target[e // 2] = dot(turned, x).astype(BF16)


def q_back(my_part, dq, xn4):
    parts, tokens, width = xn4.shape
    grad = jax.ShapeDtypeStruct((parts // 2, QUERY_HEADS * HEAD_DIM, width), BF16)
    return pl.pallas_call(
        q_back_kernel,
        grid_spec=pltpu.PrefetchScalarGridSpec(
            num_scalar_prefetch=1,
            grid=(1,),
            in_specs=[whole(dq.shape), whole(xn4.shape)],
            out_specs=[whole(grad.shape), whole(grad.shape)],
        ),
        out_shape=[grad, grad],
        compiler_params=params(1),
        cost_estimate=cost(2 * tokens * 960 * 960, 6 * tokens * 960 * 2),
        name="q_back",
    )(my_part.reshape(1), dq, xn4)


def kv_back_kernel(meta_ref, dkv_ref, cos_ref, sin1_ref, sin2_ref, xn_ref, back_ref, keep_ref, send_ref):
    for h in range(KV_HEADS):
        u = dkv_ref[:, h * TILE : (h + 1) * TILE].astype(F32)
        back = (
            u * cos_ref[...]
            - pltpu.roll(u, TILE - HEAD_DIM // 2, 1) * sin1_ref[...]
            - pltpu.roll(u, HEAD_DIM // 2, 1) * sin2_ref[...]
        )
        back_ref[:, h * TILE : (h + 1) * TILE] = back.astype(BF16)
    turned = back_ref[...].T
    for e in range(xn_ref.shape[0]):
        x = xn_ref[pl.ds(meta_ref[0] ^ e, 1)].reshape(xn_ref.shape[1:])
        target = send_ref if e % 2 else keep_ref
        target[e // 2] = dot(turned, x).astype(BF16)


def kv_back(my_part, dkv, tables, xn4):
    parts, tokens, width = xn4.shape
    grad = jax.ShapeDtypeStruct((parts // 2, KV_HEADS * TILE, width), BF16)
    table = whole((tokens, TILE))
    return pl.pallas_call(
        kv_back_kernel,
        grid_spec=pltpu.PrefetchScalarGridSpec(
            num_scalar_prefetch=1,
            grid=(1,),
            in_specs=[whole(dkv.shape), table, table, table, whole(xn4.shape)],
            out_specs=[whole((tokens, KV_HEADS * TILE)), whole(grad.shape), whole(grad.shape)],
        ),
        out_shape=[jax.ShapeDtypeStruct((tokens, KV_HEADS * TILE), BF16), grad, grad],
        compiler_params=params(1),
        cost_estimate=cost(2 * tokens * 960 * 640, 6 * tokens * 960 * 2),
        name="kv_back",
    )(my_part.reshape(1), dkv, *tables, xn4)


def final_kernel(dq_ref, kvb_ref, wq_ref, wkv_ref, hid_ref, part_ref, s1_ref, gain_ref, out_ref, gain_grad_ref):
    parts, rows, width = hid_ref.shape
    scale = s1_ref[...]
    dq = dq_ref[...]
    kvb = kvb_ref[...]
    mean = 0.0
    first = pl.program_id(0) == 0
    for d in range(parts):
        grad = dot(dq, wq_ref[d]) + dot(kvb, wkv_ref[d])
        inputs = hid_ref[d].astype(F32)
        gain_grad = jnp.sum(grad * inputs * scale, axis=0, keepdims=True)
        scaled = grad * gain_ref[d]
        out_ref[d] = scaled
        mean = mean + jnp.sum(scaled * inputs, axis=-1, keepdims=True)

        @pl.when(first)
        def _(d=d, gain_grad=gain_grad):
            gain_grad_ref[d] = gain_grad

        @pl.when(jnp.logical_not(first))
        def _(d=d, gain_grad=gain_grad):
            gain_grad_ref[d] += gain_grad

    mean = mean / (parts * width) * (scale * scale * scale)
    for d in range(parts):
        out_ref[d] = part_ref[d] + scale * out_ref[d] - hid_ref[d].astype(F32) * mean


def final_step(dq, kvb, wq_pad, wkv, hid4, part4, s1, gain):
    parts, tokens, width = hid4.shape
    rows = 128
    block = pl.BlockSpec((parts, rows, width), lambda i: (0, i, 0))
    column = pl.BlockSpec((rows, 1), lambda i: (i, 0))
    vector = whole((parts, 1, width))
    return pl.pallas_call(
        final_kernel,
        grid=(tokens // rows,),
        in_specs=[
            pl.BlockSpec((rows, dq.shape[1]), lambda i: (i, 0)),
            pl.BlockSpec((rows, kvb.shape[1]), lambda i: (i, 0)),
            whole(wq_pad.shape),
            whole(wkv.shape),
            block,
            block,
            column,
            vector,
        ],
        out_specs=[block, vector],
        out_shape=[
            jax.ShapeDtypeStruct(hid4.shape, F32),
            jax.ShapeDtypeStruct((parts, 1, width), F32),
        ],
        compiler_params=params(1),
        cost_estimate=cost(2 * tokens * 960 * 2560, 10 * tokens * 960 * 2),
        name="final_step",
    )(dq, kvb, wq_pad, wkv, hid4, part4, s1, gain)


class Net:
    def __init__(self, parts, shards):
        self.parts, self.shards = parts, shards
        self.size = parts * shards
        self.index = lax.axis_index("dp") * shards + lax.axis_index("fsdp")
        self.shard_bits = shards.bit_length() - 1
        self.part_bits = parts.bit_length() - 1

    def swap(self, array, bit):
        flip = 1 << bit
        return lax.ppermute(array, AXES, [(i, i ^ flip) for i in range(self.size)])

    def on(self, bit):
        return (self.index >> bit) & 1 == 1

    def gather(self, array):
        order = list(range(self.shard_bits - 1, -1, -1))
        order += list(range(self.size.bit_length() - 2, self.shard_bits - 1, -1))
        for bit in order:
            other = self.swap(array, bit)
            here = self.on(bit)
            array = jnp.stack([jnp.where(here, other, array), jnp.where(here, array, other)])
        bits = len(order)
        place = {bit: bits - 1 - i for i, bit in enumerate(order)}
        high_first = [place[bit] for bit in range(bits - 1, -1, -1)]
        array = jnp.transpose(array, high_first + list(range(bits, array.ndim)))
        return array.reshape((self.parts, self.shards) + array.shape[bits:])

    def add(self, mine, other, dtype=BF16):
        return (mine.astype(F32) + other.astype(F32)).astype(dtype)

    def scatter_parts(self, keep, send):
        other = self.swap(send, self.shard_bits)
        for bit in range(self.size.bit_length() - 2, self.shard_bits, -1):
            half = keep.shape[0] // 2
            send = self.add(keep[half:], other[half:])
            keep = self.add(keep[:half], other[:half])
            other = self.swap(send, bit)
        return keep[0], other[0]

    def scatter_bit(self, keep, other, bit, axis, relative):
        if relative:
            away, near = 1, 0
            pick = lambda a, i: lax.index_in_dim(a, i, axis, keepdims=False)
        else:
            near = (self.index >> bit) & 1
            away = 1 - near
            pick = lambda a, i: lax.dynamic_index_in_dim(a, i, axis, keepdims=False)
        send = self.add(pick(keep, away), pick(other, away))
        return self.add(pick(keep, near), pick(other, near)), self.swap(send, bit)

    def scatter_shards(self, keep, other, relative, bits):
        shape = keep.shape[1:]
        keep = keep.reshape((2,) * bits + shape)
        other = other.reshape((2,) * bits + shape)
        for bit in range(bits):
            keep, other = self.scatter_bit(keep, other, bit, bits - 1 - bit, relative)
        return keep, other

    def scatter(self, keep, send, rows):
        keep, other = self.scatter_parts(keep, send)
        shape = (self.shards, rows) + keep.shape[1:]
        keep, other = self.scatter_shards(keep.reshape(shape), other.reshape(shape), False, self.shard_bits)
        return self.add(keep, other, F32)

    def scatter_halves(self, keep_half, send_half):
        bits = self.shard_bits - 1
        far = self.scatter_shards(*self.scatter_parts(*send_half), True, bits)
        near = self.scatter_shards(*self.scatter_parts(*keep_half), True, bits)
        arrived = self.swap(self.add(*far), bits)
        return self.add(self.add(*near, F32), arrived, F32)


def send_down(array, moves, shards, parts):
    pairs = [(d * shards + a, d * shards + b) for d in range(parts) for a, b in moves]
    return lax.ppermute(array, AXES, pairs)


class EightShards:
    a_moves = [(2 * z, 2 * z + 1) for z in range(4)] + [(7, 6)]
    b_moves = [(2, 3), (3, 2), (4, 5), (5, 4), (6, 7), (7, 6)]
    c_moves = [(4, 5), (5, 4), (6, 7), (7, 6)]

    def __init__(self, parts):
        self.parts = parts
        self.shard = lax.axis_index("fsdp")
        self.z, self.y = self.shard // 2, self.shard % 2

    def move(self, array, moves):
        return send_down(array, moves, 8, self.parts)

    def up(self, array, lowest):
        return self.move(array, [(2 * z + y, 2 * z + y + 2) for z in range(lowest, 3) for y in range(2)])

    def down(self, array, lowest):
        return self.move(array, [(2 * z + y + 2, 2 * z + y) for z in range(lowest, 3) for y in range(2)])

    def slot_ids(self):
        shard, z, y = self.shard, self.z, self.y
        none = jnp.int32(-1)
        return jnp.stack(
            [
                shard,
                jnp.where(y == 1, shard - 1, jnp.where(z == 3, 5, none)),
                jnp.where(z >= 1, shard - 2, none),
                jnp.where(z == 3, 3 - y, jnp.where(z >= 1, 2 * (z - 1) + 1 - y, none)),
                jnp.where(z >= 2, shard - 4, none),
                jnp.where(z >= 2, 1 - y, none),
                jnp.where(z == 3, y, none),
            ]
        ).astype(jnp.int32)

    def spread(self, own):
        up1 = self.up(own, 0)
        up2 = self.up(up1, 1)
        top = self.z == 3
        a = self.move(jnp.where(top & (self.y == 1), up1, own), self.a_moves)
        b = self.move(jnp.where(top, up2, up1), self.b_moves)
        up3 = self.up(up2, 2)
        c = self.move(jnp.where(top, up3, up2), self.c_moves)
        return [own, a, up1, b, up2, c, up3]

    def collect(self, grads):
        own, a, up1, b, up2, c, up3 = grads
        back = lambda moves: [(t, s) for s, t in moves]
        top = self.z == 3
        from_c = self.move(c, back(self.c_moves)).astype(F32)
        from_b = self.move(b, back(self.b_moves)).astype(F32)
        from_a = self.move(a, back(self.a_moves)).astype(F32)
        first = self.down((up3.astype(F32) + from_c).astype(BF16), 2).astype(F32)
        level2 = up2.astype(F32) + jnp.where(top, from_b, from_c + first)
        second = self.down(level2.astype(BF16), 1).astype(F32)
        level1 = up1.astype(F32) + jnp.where(top, jnp.where(self.y == 1, from_a, 0.0), from_b + second)
        third = self.down(level1.astype(BF16), 0).astype(F32)
        keep_a = jnp.where(top & (self.y == 1), 0.0, from_a)
        return (own.astype(F32) + keep_a + third).astype(BF16)


class AnyShards:
    def __init__(self, shards):
        self.shards = shards
        self.shard = lax.axis_index("fsdp")

    def slot_ids(self):
        return (self.shard - jnp.arange(self.shards)).astype(jnp.int32)

    def spread(self, own):
        every = lax.all_gather(own, "fsdp", axis=0, tiled=False)
        place = lambda s: (self.shard - s) % self.shards
        return [own] + [
            lax.dynamic_index_in_dim(every, place(s), 0, keepdims=False) for s in range(1, self.shards)
        ]

    def collect(self, grads):
        every = jnp.stack(grads)
        place = lambda j: (self.shard - j) % self.shards
        order = [lax.dynamic_index_in_dim(every, place(j), 0, keepdims=False) for j in range(self.shards)]
        return lax.psum_scatter(jnp.stack(order), "fsdp", scatter_dimension=0, tiled=False)


def shards(
    hidden_in, segment, position, selected, gain_attn, gain_ffn, router,
    w_query, key_weight, value_weight, w_output, w_gate, w_up, w_down, cotangent,
):
    groups, rows, model = hidden_in.shape
    tokens = groups * rows
    parts, shard_count = lax.axis_size("dp"), lax.axis_size("fsdp")
    width = model // parts
    net = Net(parts, shard_count)
    my_part, my_shard = lax.axis_index("dp"), lax.axis_index("fsdp")
    ring = EightShards(parts) if shard_count == 8 else AnyShards(shard_count)

    small = jnp.concatenate([key_weight.T, value_weight.T], axis=0)
    medium = jnp.concatenate([w_query.T, w_output], axis=0)
    large = jnp.concatenate([w_gate.T, w_up.T, w_down], axis=0)
    kv_all = net.gather(small)
    qo_all = net.gather(medium)
    ffn_all = lax.all_gather(large, AXES, axis=0, tiled=False).reshape((parts, shard_count) + large.shape)

    def heads_of(array, count):
        return array.reshape(parts, count, HEAD_DIM, width)

    kv_rows = small.shape[0] // 2
    q_rows = medium.shape[0] // 2
    keys = heads_of(kv_all[:, :, :kv_rows], KV_HEADS)
    values = heads_of(kv_all[:, :, kv_rows:], KV_HEADS)
    wkv = jnp.concatenate([keys, values], axis=2).reshape(parts, KV_HEADS * TILE, width)
    queries = heads_of(qo_all[:, :, :q_rows], QUERY_HEADS)
    outputs = heads_of(qo_all[:, :, q_rows:], QUERY_HEADS)
    half = HEAD_DIM // 2
    wq_pad = jnp.concatenate([queries, queries[:, :, half:], queries[:, :, :half]], axis=2)
    wq_pad = wq_pad.reshape(parts, QUERY_HEADS * TILE, width)
    wo_pad = jnp.concatenate([jnp.zeros_like(outputs), outputs], axis=2)
    wo_pad = wo_pad.reshape(parts, QUERY_HEADS * TILE, width)

    def split(array):
        return jnp.transpose(array.reshape(tokens, parts, width), (1, 0, 2))

    def join(array):
        return jnp.transpose(array, (1, 0, 2)).reshape(groups, rows, model)

    hid4, cot4 = split(hidden_in), split(cotangent)
    vector = lambda v: v.astype(F32).reshape(parts, 1, width)
    gain_one, gain_two, route = vector(gain_attn), vector(gain_ffn), vector(router)
    chosen = selected.reshape(tokens, 1).astype(F32)

    frequency = THETA ** (-(jnp.arange(half).astype(F32) * 2.0) / HEAD_DIM)
    angles = position.reshape(tokens).astype(F32)[:, None] * frequency[None, :]
    cos, sin = jnp.cos(angles), jnp.sin(angles)
    zero, one = jnp.zeros_like(cos), jnp.ones_like(cos)
    table = lambda *four: jnp.concatenate(four, axis=1)
    kv_tables = (table(cos, cos, one, one), table(-sin, zero, zero, zero), table(zero, sin, zero, zero))
    shrink = HEAD_DIM**-0.5
    q_tables = tuple(
        shrink * t
        for t in (table(cos, cos, zero, zero), table(-sin, zero, zero, zero), table(zero, sin, zero, zero))
    )
    seg_rows = segment.astype(F32).reshape(groups, 1, rows)
    tags = jnp.where(selected == 1, segment, -1).astype(BF16).reshape(groups, rows // TILE, TILE)
    tags = jnp.pad(tags, ((0, 0), (0, 16 - rows // TILE), (0, 0)))

    xn4, s1, fg4, mix, slope = first_norm(hid4, cot4, gain_one, route, chosen)
    own_kv = kv_project(xn4, wkv, kv_tables, tags, groups)
    kvs = ring.spread(own_kv)
    q = q_project(xn4, wq_pad, q_tables[0], q_tables[1] + q_tables[2], groups)
    slot_ids = ring.slot_ids()
    o, lse = attention_forward(slot_ids, q, seg_rows, kvs)
    mid4, x24, s2 = out_project(o, wo_pad, hid4, gain_two)
    out_a, xg_a, keep_a, send_a = ffn(my_part, my_shard, 1, x24, fg4, ffn_all)
    out_b, xg_b, keep_b, send_b = ffn(my_part, my_shard, 0, x24, fg4, ffn_all)
    hidden4, part4, ag4, router_sum, gain_two_sum = middle_step(
        mid4, hid4, cot4, (out_a, out_b), (xg_a, xg_b), mix, slope, s2, gain_two, route
    )
    do, keep_o, send_o = out_back(my_part, ag4, wo_pad, o)
    dq, dkvs = attention_backward(slot_ids, q, do, o, lse, seg_rows, q_tables, kvs)
    keep_q, send_q = q_back(my_part, dq, xn4)
    dkv = ring.collect(dkvs).reshape(tokens, KV_HEADS * TILE)
    kvb, keep_kv, send_kv = kv_back(my_part, dkv, kv_tables, xn4)
    grad_in4, gain_one_sum = final_step(dq, kvb, wq_pad, wkv, hid4, part4, s1, gain_one)

    sums = lax.psum(jnp.stack([gain_one_sum, gain_two_sum, router_sum]), AXES).reshape(3, model)

    ffn_grad = net.scatter_halves((keep_b, send_b), (keep_a, send_a))
    o_grad = net.scatter(keep_o, send_o, q_rows)
    q_grad = net.scatter(keep_q, send_q, q_rows)

    def by_shard(array):
        tiles = array.reshape(array.shape[0], KV_HEADS, 2, HEAD_DIM, width)
        both = jnp.transpose(tiles, (0, 2, 1, 3, 4)).reshape(-1, 2, shard_count, kv_rows, width)
        return jnp.transpose(both, (0, 2, 1, 3, 4)).reshape(-1, 2 * shard_count * kv_rows, width)

    kv_grad = net.scatter(by_shard(keep_kv), by_shard(send_kv), 2 * kv_rows)
    third = ffn_grad.shape[0] // 3
    return (
        join(hidden4),
        join(grad_in4),
        sums[0],
        sums[1],
        sums[2],
        q_grad.T,
        kv_grad[:kv_rows].T,
        kv_grad[kv_rows:].T,
        o_grad,
        ffn_grad[:third].T,
        ffn_grad[third : 2 * third].T,
        ffn_grad[2 * third :],
    )


def solution(mesh):
    tokens = P("dp", "fsdp")
    inner_first = P("fsdp", "dp")
    return jax.shard_map(
        shards,
        mesh=mesh,
        in_specs=(P("dp", "fsdp", None),) + (tokens,) * 3 + (P(),) * 3
        + (tokens,) * 3 + (inner_first,) + (tokens,) * 2 + (inner_first, P("dp", "fsdp", None)),
        out_specs=(P("dp", "fsdp", None),) * 2 + (P(),) * 3
        + (tokens,) * 3 + (inner_first,) + (tokens,) * 2 + (inner_first,),
        check_vma=False,
    )
```

time: 1330 us -> 683 us (0.51)
  waiting for transfers between devices: 830 us -> 131 us
  starting transfers between devices: 1.45 us -> 227 us
  blocking collectives: 202 us -> 38.9 us
  Pallas kernels: 0 us -> 148 us
  matrix products: 99.8 us -> 0 us
  local copies, waits for them, and re-layouts: 92.8 us -> 40.4 us
  loops' own time: 34.8 us -> 0 us
  other arithmetic: 38.4 us -> 71.6 us
    reduce_scatter x8 -> x0, waiting for transfers between devices: 393 us -> none  [the longest x1 117 us: shards(): lax.psum_scatter(kv_acc.astype(jnp.bfloat16), 'fsdp', scatter_dimension=1...]
    unnamed x31 -> x1, waiting for transfers between devices: 330 us -> 0.02 us
    ppermute x0 -> x46, starting transfers between devices: none -> 227 us  [the longest x34 211 us: swap(): return lax.ppermute(array, AXES, [(i, i ^ flip) for i in range(self.size)])]
    all_gather x7 -> x0, blocking collectives: 162 us -> none  [the longest x1 33.5 us: gather_weights(): lax.all_gather(w_query, 'fsdp', axis=1, tiled=True)]
    pallas_call x0 -> x13, Pallas kernels: none -> 148 us  [the longest x2 54.4 us: ffn(): pl.pallas_call(ffn_kernel, grid_spec=pltpu.PrefetchScalarGridSpec(num_sca...]
    ppermute x0 -> x46, waiting for transfers between devices: none -> 131 us  [the longest x34 128 us: swap(): return lax.ppermute(array, AXES, [(i, i ^ flip) for i in range(self.size)])]
    all_gather x9 -> x1, waiting for transfers between devices: 106 us -> 0.01 us  [shards(): lax.all_gather(large, AXES, axis=0, tiled=False)]
    dot_general x30 -> x0, matrix products: 99.8 us -> none  [the longest x1 9.73 us: shards(): jnp.einsum('nd,fd->nf', ffn_grad, back_down, preferred_element_type=jnp.f...]
  transfers between devices with their start and end apart: 24 -> 47, of which waited for: 19 -> 14; matrix products, arithmetic and copies ran while one was open for 13% -> 16% of each run, Pallas kernels for 0% -> 14%
where the time goes in v1:
time: 683 us; the launch traced here: 672 us
  starting transfers between devices  227 us (33%)
  Pallas kernels  148 us (22%)
  waiting for transfers between devices  131 us (19%)
  other arithmetic  71.6 us (10%)
  local copies, waits for them, and re-layouts  40.4 us (6%)
  blocking collectives  38.9 us (6%)
  between operations  15.4 us (2%)
    ppermute x34, starting transfers between devices, swap(): return lax.ppermute(array, AXES, [(i, i ^ flip) for i in range(self.size)])  211 us
    ppermute x34, waiting for transfers between devices, swap(): return lax.ppermute(array, AXES, [(i, i ^ flip) for i in range(self.size)])  128 us
    pallas_call x2, Pallas kernels, ffn(): pl.pallas_call(ffn_kernel, grid_spec=pltpu.PrefetchScalarGridSpec(num_sca...  54.4 us
    psum x1, blocking collectives, shards(): lax.psum(jnp.stack([gain_one_sum, gain_two_sum, router_sum]), AXES)  38.9 us
    convert_element_type x24, other arithmetic, add(): return (mine.astype(F32) + other.astype(F32)).astype(dtype)  34.9 us
    pallas_call x1, Pallas kernels, attention_backward(): pl.pallas_call(backward_kernel, grid_spec=pltpu.PrefetchScalarGridSpec(nu...  16.3 us
    unnamed x90, local copies, waits for them, and re-layouts  15.9 us
    ppermute x12, starting transfers between devices, send_down(): return lax.ppermute(array, AXES, pairs)  15.9 us
  transfers between devices with their start and end apart: 47, of which 14 were waited for; matrix products, arithmetic and copies ran while one was open for 16% of the time, Pallas kernels for 14%

profile of v1, /device:TPU:0, one launch (start us, length us, event | category | flops | bytes accessed | tf_op | source)
XLA Modules:
  0.0 672.4 jit_solution(14033790795212188184)
XLA Ops:
  10.1 4.1 collective-permute-start.5
  31.1 4.6 first_norm.1
  46.7 10.1 %collective-permute-done.8 = bf16[2,2,2,80,240]{4,3,0,1,2:T(8,128)(2,1)S(1)} collective-permute-done((bf16[2,2,2,80,240]{4,3,0,1,2:T(8,128)(2,1)S(1)}, bf16[2,2,2,80,240]{4,3,0,1,2:T(8,128)(2,1)S(1)}, u32[]{:S(2)}, u32[]{:S(2)}) %collective-permute-start.8) | collective-permute-done | bytes 307232 | tf_op jit(solution)/shard_map/ppermute | solution.py:724
  58.0 5.3 collective-permute-done.2
  66.9 4.1 kv_project.1.refs_0_
  74.3 19.3 %collective-permute-done.3 = bf16[2,2,2,240,240]{4,3,0,1,2:T(8,128)(2,1)} collective-permute-done((bf16[2,2,2,240,240]{4,3,0,1,2:T(8,128)(2,1)S(1)}, bf16[2,2,2,240,240]{4,3,0,1,2:T(8,128)(2,1)}, u32[]{:S(2)}, u32[]{:S(2)}) %collective-permute-start.3) | collective-permute-done | bytes 921632 | tf_op jit(solution)/shard_map/ppermute | solution.py:724
  121.0 7.9 %q_project.1.q_ref = bf16[512,1920]{1,0:T(8,128)(2,1)} custom-call(bf16[4,512,240]{2,1,0:T(8,128)(2,1)} %get-tuple-element.53.xn_ref, bf16[4,1920,240]{2,1,0:T(8,128)(2,1)} %bitcast.267, f32[512,128]{1,0:T(8,128)} %get-tuple-element.191.cos_ref, f32[512,128]{1,0:T(8,128)} %get-tuple-element.188.sin_ref), custom_call_target="tpu_custom_call" | custom-call | flops 1887436800 | bytes 5898240 | tf_op jit(solution)/shard_map/q_project/pallas_call | solution.py:148
  130.0 12.6 %attention_forward.1 = (bf16[512,1920]{1,0:T(8,128)(2,1)}, f32[2,5,1,768]{3,2,1,0:T(1,128)}) custom-call(s32[7]{0:T(128)} %stack.153.slot_ref, bf16[512,1920]{1,0:T(8,128)(2,1)} %q_project.1.q_ref, f32[2,1,256]{2,1,0:T(1,128)} %reshape.346.seg_ref, bf16[2,272,640]{2,1,0:T(8,128)(2,1)} %kv_project.1.refs_0_, bf16[2,272,640]{2,1,0:T(8,128)(2,1)} %copy-done.36, ...), custom_call_target="tpu_custom_call" | custom-call | flops 6039797760 | bytes 7864320 | tf_op jit(solution)/shard_map/attention_forward/pallas_call | solution.py:260
  142.6 7.3 %out_project.1 = (f32[4,512,240]{2,1,0:T(8,128)}, bf16[4,512,240]{2,1,0:T(8,128)(2,1)}, f32[512,1]{1,0:T(8,128)}) custom-call(bf16[512,1920]{1,0:T(8,128)(2,1)} %get-tuple-element.54.o_ref, bf16[4,1920,240]{2,1,0:T(8,128)(2,1)} %bitcast.284, bf16[4,512,240]{2,1,0:T(8,128)(2,1)} %bitcast.272, f32[4,1,240]{2,1,0:T(1,128)} %reshape.370.gain_ref), custom_call_target="tpu_custom_call" | custom-call | flops 1887436800 | bytes 7864320 | tf_op jit(solution)/shard_map/out_project/pallas_call | solution.py:386
  149.9 27.3 %ffn.3 = (f32[4,512,240]{2,1,0:T(8,128)}, f32[4,512,240]{2,1,0:T(8,128)}, bf16[2,4,960,240]{3,2,1,0:T(8,128)(2,1)}, bf16[2,4,960,240]{3,2,1,0:T(8,128)(2,1)}) custom-call(s32[3]{0:T(128)} %pad_add_fusion.2.meta_ref, bf16[4,512,240]{2,1,0:T(8,128)(2,1)} %get-tuple-element.56.x_ref, bf16[4,512,240]{2,1,0:T(8,128)(2,1)} %get-tuple-element.57.fg_ref, ...), custom_call_target="tpu_custom_call" | custom-call | flops 11324620800 | bytes 22609920 | tf_op jit(solution)/shard_map/ffn/pallas_call | solution.py:465
  177.2 27.1 %ffn.2 = (f32[4,512,240]{2,1,0:T(8,128)}, f32[4,512,240]{2,1,0:T(8,128)}, bf16[2,4,960,240]{3,2,1,0:T(8,128)(2,1)}, bf16[2,4,960,240]{3,2,1,0:T(8,128)(2,1)}) custom-call(s32[3]{0:T(128)} %pad_add_fusion.meta_ref, bf16[4,512,240]{2,1,0:T(8,128)(2,1)} %get-tuple-element.56.x_ref, bf16[4,512,240]{2,1,0:T(8,128)(2,1)} %get-tuple-element.57.fg_ref, ...), custom_call_target="tpu_custom_call" | custom-call | flops 11324620800 | bytes 22609920 | tf_op jit(solution)/shard_map/ffn/pallas_call | solution.py:465
  204.3 8.4 %middle_step.1 = (bf16[4,512,240]{2,1,0:T(8,128)(2,1)}, f32[4,512,240]{2,1,0:T(8,128)}, bf16[4,512,240]{2,1,0:T(8,128)(2,1)}, f32[4,1,240]{2,1,0:T(1,128)}, f32[4,1,240]{2,1,0:T(1,128)}) custom-call(f32[4,512,240]{2,1,0:T(8,128)} %get-tuple-element.55.mid_ref, bf16[4,512,240]{2,1,0:T(8,128)(2,1)} %bitcast.273, bf16[4,512,240]{2,1,0:T(8,128)(2,1)} %bitcast.279, ...), custom_call_target="tpu_custom_call" | custom-call | flops 14745600 | bytes 17694720 | tf_op jit(solution)/shard_map/middle_step/pallas_call | solution.py:537
  212.7 9.5 %out_back.1 = (bf16[512,1920]{1,0:T(8,128)(2,1)}, bf16[2,960,240]{2,1,0:T(8,128)(2,1)}, bf16[2,960,240]{2,1,0:T(8,128)(2,1)}) custom-call(s32[1]{0:T(128)} %bitcast.51.meta_ref, bf16[4,512,240]{2,1,0:T(8,128)(2,1)} %get-tuple-element.66.ag_ref, bf16[4,1920,240]{2,1,0:T(8,128)(2,1)} %bitcast.285, bf16[512,1920]{1,0:T(8,128)(2,1)} %get-tuple-element.54.o_ref), custom_call_target="tpu_custom_call" | custom-call | flops 2831155200 | bytes 11796480 | tf_op jit(solution)/shard_map/out_back/pallas_call | solution.py:580
  222.2 16.3 %attention_backward.1 = (bf16[512,1920]{1,0:T(8,128)(2,1)}, bf16[2,256,640]{2,1,0:T(8,128)(2,1)}, bf16[2,256,640]{2,1,0:T(8,128)(2,1)}, bf16[2,256,640]{2,1,0:T(...) custom-call(s32[7]{0:T(128)} %stack.153.slot_ref, ...), custom_call_target="tpu_custom_call" | custom-call | flops 15099494400 | bytes 15728640 | tf_op jit(solution)/shard_map/attention_backward/pallas_call | solution.py:346
  239.9 4.5 q_back.1
  258.9 5.2 collective-permute-done.33
  267.5 6.1 collective-permute-done.23
  273.7 10.4 %collective-permute-start.34 = (bf16[2,2,120,240]{3,2,1,0:T(8,128)(2,1)}, bf16[2,2,120,240]{3,2,1,0:T(8,128)(2,1)}, u32[]{:S(2)}, u32[]{:S(2)}) collective-permute-start(bf16[2,2,120,240]{3,2,1,0:T(8,128)(2,1)} %fusion.24), channel_id=1, source_target_pairs={{0,1},{1,0},{2,3},{3,2},{4,5},{5,4},{6,7},{7,6},{8,9},{9,8},{10,11... | collective-permute-start | bytes 691208 | tf_op jit(solution)/shard_map/ppermute | solution.py:724
  292.5 91.4 %collective-permute-start.35 = (bf16[2,120,240]{2,1,0:T(8,128)(2,1)S(1)}, bf16[2,120,240]{2,1,0:T(8,128)(2,1)S(1)}, u32[]{:S(2)}, u32[]{:S(2)}) collective-permute-start(bf16[2,120,240]{2,1,0:T(8,128)(2,1)S(1)} %get-tuple-element.174), channel_id=1, source_target_pairs={{0,2},{1,3},{2,0},{3,1},{4,6},{5,7},{6,4},{7,5},{8,10},{9,11},{10,... | collective-permute-start | bytes 345608 | tf_op jit(solution)/shard_map/ppermute | solution.py:724
  387.7 64.7 %collective-permute-start.25 = (bf16[2,120,240]{1,2,0:T(8,128)(2,1)S(1)}, bf16[2,120,240]{1,2,0:T(8,128)(2,1)S(1)}, u32[]{:S(2)}, u32[]{:S(2)}) collective-permute-start(bf16[2,120,240]{1,2,0:T(8,128)(2,1)S(1)} %get-tuple-element.176), channel_id=1, source_target_pairs={{0,2},{1,3},{2,0},{3,1},{4,6},{5,7},{6,4},{7,5},{8,10},{9,11},{10,... | collective-permute-start | bytes 345608 | tf_op jit(solution)/shard_map/ppermute | solution.py:724
  454.3 7.2 %collective-permute-start.36 = (bf16[120,240]{1,0:T(8,128)(2,1)S(1)}, bf16[120,240]{1,0:T(8,128)(2,1)S(1)}, u32[]{:S(2)}, u32[]{:S(2)}) collective-permute-start(bf16[120,240]{1,0:T(8,128)(2,1)S(1)} %fusion.47), channel_id=1, source_target_pairs={{0,4},{1,5},{2,6},{3,7},{4,0},{5,1},{6,2},{7,3},{8,12},{9,13},{10,... | collective-permute-start | bytes 172808 | tf_op jit(solution)/shard_map/ppermute | solution.py:724
  461.5 7.3 %collective-permute-done.25 = bf16[2,120,240]{1,2,0:T(8,128)(2,1)S(1)} collective-permute-done((bf16[2,120,240]{1,2,0:T(8,128)(2,1)S(1)}, bf16[2,120,240]{1,2,0:T(8,128)(2,1)S(1)}, u32[]{:S(2)}, u32[]{:S(2)}) %collective-permute-start.25) | collective-permute-done | bytes 115232 | tf_op jit(solution)/shard_map/ppermute | solution.py:724
  468.8 6.0 collective-permute-start.26
  474.8 5.6 add_convert_fusion.1
  483.7 4.3 kv_back.1
  490.3 6.2 add_convert_fusion.3
  506.0 20.5 %collective-permute-done.42 = bf16[1,4,960,240]{3,2,1,0:T(8,128)(2,1)} collective-permute-done((bf16[1,4,960,240]{3,2,1,0:T(8,128)(2,1)}, bf16[1,4,960,240]{3,2,1,0:T(8,128)(2,1)}, u32[]{:S(2)}, u32[]{:S(2)}) %collective-permute-start.42) | collective-permute-done | bytes 1843232 | tf_op jit(solution)/shard_map/ppermute | solution.py:724
  532.0 37.6 %collective-permute-done.28 = bf16[1,640,240]{2,1,0:T(8,128)(2,1)S(1)} collective-permute-done((bf16[1,640,240]{2,1,0:T(8,128)(2,1)S(1)}, bf16[1,640,240]{2,1,0:T(8,128)(2,1)S(1)}, u32[]{:S(2)}, u32[]{:S(2)}) %collective-permute-start.28) | collective-permute-done | bytes 307232 | tf_op jit(solution)/shard_map/ppermute | solution.py:724
  575.0 14.3 %final_step.1 = (f32[4,512,240]{2,1,0:T(8,128)}, f32[4,1,240]{2,1,0:T(1,128)}) custom-call(bf16[512,1920]{1,0:T(8,128)(2,1)} %get-tuple-element.69.dq_ref, bf16[512,640]{1,0:T(8,128)(2,1)} %get-tuple-element.77.kvb_ref, bf16[4,1920,240]{2,1,0:T(8,128)(2,1)} %bitcast.268, bf16[4,640,240]{2,1,0:T(8,128)(2,1)} %bitcast.277, bf16[4,512,240]{2,1,0:T(8,128)(2,1)} %bitcast.274, ...), custom_call_target="tpu_custom_call" | custom-call | flops 2516582400 | bytes 9830400 | tf_op jit(solution)/shard_map/final_step/pallas_call | solution.py:690
  594.4 38.9 %psum.7 = f32[3,4,1,240]{3,2,1,0:T(1,128)S(1)} all-reduce(f32[3,4,1,240]{3,2,1,0:T(1,128)S(1)} %pad_maximum_fusion.16), channel_id=1, replica_groups=mesh['dp'=4,'fsdp'=8] {'dp','fsdp'}, use_global_device_ids=true, to_apply=%region_0.1 | all-reduce | flops 2880 | bytes 23040 | tf_op jit(solution)/shard_map/psum | solution.py:954
  653.0 5.1 collective-permute-done.40
  658.1 4.8 collective-permute-done.45
  (274 shorter events, 153.1 us)
Async XLA Ops:
  7.2 142.7 %all-gather.3.cloned.1.call-start = ((), (), s32[]{:S(2)}) async-start(), calls=%async_computation | async-start | bytes 16220160 | tf_op jit(solution)/shard_map/all_gather | solution.py:891
  16.6 21.7 %collective-permute-start = (bf16[240,240]{1,0:T(8,128)(2,1)}, bf16[240,240]{1,0:T(8,128)(2,1)}, u32[]{:S(2)}, u32[]{:S(2)}) collective-permute-start(bf16[240,240]{1,0:T(8,128)(2,1)} %pad_maximum_fusion.13), channel_id=1, source_target_pairs={{0,4},{1,5},{2,6},{3,7},{4,0},{5,1},{6,2},{7,3},{8,12},{9,13},{10,... | collective-permute-start | bytes 345608 | tf_op jit(solution)/shard_map/ppermute | solution.py:724
  46.2 17.0 %collective-permute-start.2 = (bf16[2,2,240,240]{3,2,0,1:T(8,128)(2,1)S(1)}, bf16[2,2,240,240]{3,2,0,1:T(8,128)(2,1)S(1)}, u32[]{:S(2)}, u32[]{:S(2)}) collective-permute-start(bf16[2,2,240,240]{3,2,0,1:T(8,128)(2,1)S(1)} %pad_maximum_fusion.7), channel_id=1, source_target_pairs={{0,1},{1,0},{2,3},{3,2},{4,5},{5,4},{6,7},{7,6},{8,9},{9,8},{10,11... | collective-permute-start | bytes 1382408 | tf_op jit(solution)/shard_map/ppermute | solution.py:724
  63.5 30.1 %collective-permute-start.3 = (bf16[2,2,2,240,240]{4,3,0,1,2:T(8,128)(2,1)S(1)}, bf16[2,2,2,240,240]{4,3,0,1,2:T(8,128)(2,1)}, u32[]{:S(2)}, u32[]{:S(2)}) collective-permute-start(bf16[2,2,2,240,240]{4,3,0,1,2:T(8,128)(2,1)S(1)} %pad_maximum_fusion.5), channel_id=1, source_target_pairs={{0,16},{1,17},{2,18},{3,19},{4,20},{5,21},{6,22},{7,23},{8,24},{9,... | collective-permute-start | bytes 2764808 | tf_op jit(solution)/shard_map/ppermute | solution.py:724
  71.1 29.1 %collective-permute-start.10 = (bf16[2,272,640]{2,1,0:T(8,128)(2,1)}, bf16[2,272,640]{2,1,0:T(8,128)(2,1)S(1)}, u32[]{:S(2)}, u32[]{:S(2)}) collective-permute-start(bf16[2,272,640]{2,1,0:T(8,128)(2,1)} %kv_project.1.refs_0_), channel_id=1, source_target_pairs={{0,2},{1,3},{2,4},{3,5},{4,6},{5,7},{8,10},{9,11},{10,12},{11,13},... | collective-permute-start | bytes 2088968 | tf_op jit(solution)/shard_map/ppermute | solution.py:789
  96.8 15.9 %collective-permute-start.4 = (bf16[2,2,2,2,240,240]{5,4,1,2,3,0:T(8,128)(2,1)}, bf16[2,2,2,2,240,240]{5,4,1,2,3,0:T(8,128)(2,1)}, u32[]{:S(2)}, u32[]{:S(2)}) collective-permute-start(bf16[2,2,2,2,240,240]{5,4,1,2,3,0:T(8,128)(2,1)} %pad_maximum_fusion.2), channel_id=1, source_target_pairs={{0,8},{1,9},{2,10},{3,11},{4,12},{5,13},{6,14},{7,15},{8,0},{9,1},... | collective-permute-start | bytes 5529608 | tf_op jit(solution)/shard_map/ppermute | solution.py:724
  109.0 19.9 %collective-permute-start.11 = (bf16[2,272,640]{2,1,0:T(8,128)(2,1)}, bf16[2,272,640]{2,1,0:T(8,128)(2,1)S(1)}, u32[]{:S(2)}, u32[]{:S(2)}) collective-permute-start(bf16[2,272,640]{2,1,0:T(8,128)(2,1)} %get-tuple-element.166), channel_id=1, source_target_pairs={{0,1},{2,3},{4,5},{6,7},{7,6},{8,9},{10,11},{12,13},{14,15},{15,14... | collective-permute-start | bytes 2088968 | tf_op jit(solution)/shard_map/ppermute | solution.py:789
  110.3 18.5 %collective-permute-start.13 = (bf16[2,272,640]{2,1,0:T(8,128)(2,1)}, bf16[2,272,640]{2,1,0:T(8,128)(2,1)S(1)}, u32[]{:S(2)}, u32[]{:S(2)}) collective-permute-start(bf16[2,272,640]{2,1,0:T(8,128)(2,1)} %get-tuple-element.165), channel_id=1, source_target_pairs={{2,3},{3,2},{4,5},{5,4},{6,7},{7,6},{10,11},{11,10},{12,13},{13,12... | collective-permute-start | bytes 2088968 | tf_op jit(solution)/shard_map/ppermute | solution.py:789
  111.0 17.8 %collective-permute-start.15 = (bf16[2,272,640]{2,1,0:T(8,128)(2,1)}, bf16[2,272,640]{2,1,0:T(8,128)(2,1)}, u32[]{:S(2)}, u32[]{:S(2)}) collective-permute-start(bf16[2,272,640]{2,1,0:T(8,128)(2,1)} %get-tuple-element.164), channel_id=1, source_target_pairs={{4,5},{5,4},{6,7},{7,6},{12,13},{13,12},{14,15},{15,14},{20,21},{2... | collective-permute-start | bytes 2088968 | tf_op jit(solution)/shard_map/ppermute | solution.py:789
  204.3 270.6 %collective-permute-start.41 = (bf16[2,4,960,240]{3,2,1,0:T(8,128)(2,1)}, bf16[2,4,960,240]{3,2,1,0:T(8,128)(2,1)}, u32[]{:S(2)}, u32[]{:S(2)}) collective-permute-start(bf16[2,4,960,240]{3,2,1,0:T(8,128)(2,1)} %get-tuple-element.93), channel_id=1, source_target_pairs={{0,8},{1,9},{2,10},{3,11},{4,12},{5,13},{6,14},{7,15},{8,0},{9,1},... | collective-permute-start | bytes 11059208 | tf_op jit(solution)/shard_map/ppermute | solution.py:724
  244.4 245.9 %collective-permute-start.37 = (bf16[2,4,960,240]{3,2,1,0:T(8,128)(2,1)}, bf16[2,4,960,240]{3,2,1,0:T(8,128)(2,1)}, u32[]{:S(2)}, u32[]{:S(2)}) collective-permute-start(bf16[2,4,960,240]{3,2,1,0:T(8,128)(2,1)} %get-tuple-element.91), channel_id=1, source_target_pairs={{0,8},{1,9},{2,10},{3,11},{4,12},{5,13},{6,14},{7,15},{8,0},{9,1},... | collective-permute-start | bytes 11059208 | tf_op jit(solution)/shard_map/ppermute | solution.py:724
  251.9 21.7 %collective-permute-start.23 = (bf16[1,960,240]{2,1,0:T(8,128)(2,1)}, bf16[1,960,240]{2,1,0:T(8,128)(2,1)}, u32[]{:S(2)}, u32[]{:S(2)}) collective-permute-start(bf16[1,960,240]{2,1,0:T(8,128)(2,1)} %get-tuple-element.150), channel_id=1, source_target_pairs={{0,16},{1,17},{2,18},{3,19},{4,20},{5,21},{6,22},{7,23},{8,24},{9,... | collective-permute-start | bytes 1382408 | tf_op jit(solution)/shard_map/ppermute | solution.py:724
  255.1 37.4 %collective-permute-start.16 = (bf16[2,256,640]{2,1,0:T(8,128)(2,1)}, bf16[2,256,640]{2,1,0:T(8,128)(2,1)S(1)}, u32[]{:S(2)}, u32[]{:S(2)}) collective-permute-start(bf16[2,256,640]{2,1,0:T(8,128)(2,1)} %get-tuple-element.71), channel_id=1, source_target_pairs={{1,0},{3,2},{5,4},{7,6},{6,7},{9,8},{11,10},{13,12},{15,14},{14,15... | collective-permute-start | bytes 1966088 | tf_op jit(solution)/shard_map/ppermute | solution.py:789
  264.1 119.9 %collective-permute-start.20 = (bf16[2,256,640]{2,1,0:T(8,128)(2,1)}, bf16[2,256,640]{2,1,0:T(8,128)(2,1)}, u32[]{:S(2)}, u32[]{:S(2)}) collective-permute-start(bf16[2,256,640]{2,1,0:T(8,128)(2,1)} %fusion.7), channel_id=1, source_target_pairs={{4,2},{5,3},{6,4},{7,5},{12,10},{13,11},{14,12},{15,13},{20,18},{2... | collective-permute-start | bytes 1966088 | tf_op jit(solution)/shard_map/ppermute | solution.py:789
  273.7 16.1 %collective-permute-start.34 = (bf16[2,2,120,240]{3,2,1,0:T(8,128)(2,1)}, bf16[2,2,120,240]{3,2,1,0:T(8,128)(2,1)}, u32[]{:S(2)}, u32[]{:S(2)}) collective-permute-start(bf16[2,2,120,240]{3,2,1,0:T(8,128)(2,1)} %fusion.24), channel_id=1, source_target_pairs={{0,1},{1,0},{2,3},{3,2},{4,5},{5,4},{6,7},{7,6},{8,9},{9,8},{10,11... | collective-permute-start | bytes 691208 | tf_op jit(solution)/shard_map/ppermute | solution.py:724
  289.7 97.9 %collective-permute-start.24 = (bf16[2,2,120,240]{2,3,1,0:T(8,128)(2,1)S(1)}, bf16[2,2,120,240]{2,3,1,0:T(8,128)(2,1)S(1)}, u32[]{:S(2)}, u32[]{:S(2)}) collective-permute-start(bf16[2,2,120,240]{2,3,1,0:T(8,128)(2,1)S(1)} %fusion.23), channel_id=1, source_target_pairs={{0,1},{1,0},{2,3},{3,2},{4,5},{5,4},{6,7},{7,6},{8,9},{9,8},{10,11... | collective-permute-start | bytes 691208 | tf_op jit(solution)/shard_map/ppermute | solution.py:724
  292.5 161.7 %collective-permute-start.35 = (bf16[2,120,240]{2,1,0:T(8,128)(2,1)S(1)}, bf16[2,120,240]{2,1,0:T(8,128)(2,1)S(1)}, u32[]{:S(2)}, u32[]{:S(2)}) collective-permute-start(bf16[2,120,240]{2,1,0:T(8,128)(2,1)S(1)} %get-tuple-element.174), channel_id=1, source_target_pairs={{0,2},{1,3},{2,0},{3,1},{4,6},{5,7},{6,4},{7,5},{8,10},{9,11},{10,... | collective-permute-start | bytes 345608 | tf_op jit(solution)/shard_map/ppermute | solution.py:724
  386.3 95.2 %collective-permute-start.21 = (bf16[2,256,640]{2,1,0:T(8,128)(2,1)}, bf16[2,256,640]{2,1,0:T(8,128)(2,1)}, u32[]{:S(2)}, u32[]{:S(2)}) collective-permute-start(bf16[2,256,640]{2,1,0:T(8,128)(2,1)} %fusion.5), channel_id=1, source_target_pairs={{2,0},{3,1},{4,2},{5,3},{6,4},{7,5},{10,8},{11,9},{12,10},{13,11},... | collective-permute-start | bytes 1966088 | tf_op jit(solution)/shard_map/ppermute | solution.py:789
  387.7 81.1 %collective-permute-start.25 = (bf16[2,120,240]{1,2,0:T(8,128)(2,1)S(1)}, bf16[2,120,240]{1,2,0:T(8,128)(2,1)S(1)}, u32[]{:S(2)}, u32[]{:S(2)}) collective-permute-start(bf16[2,120,240]{1,2,0:T(8,128)(2,1)S(1)} %get-tuple-element.176), channel_id=1, source_target_pairs={{0,2},{1,3},{2,0},{3,1},{4,6},{5,7},{6,4},{7,5},{8,10},{9,11},{10,... | collective-permute-start | bytes 345608 | tf_op jit(solution)/shard_map/ppermute | solution.py:724
  454.3 43.2 %collective-permute-start.36 = (bf16[120,240]{1,0:T(8,128)(2,1)S(1)}, bf16[120,240]{1,0:T(8,128)(2,1)S(1)}, u32[]{:S(2)}, u32[]{:S(2)}) collective-permute-start(bf16[120,240]{1,0:T(8,128)(2,1)S(1)} %fusion.47), channel_id=1, source_target_pairs={{0,4},{1,5},{2,6},{3,7},{4,0},{5,1},{6,2},{7,3},{8,12},{9,13},{10,... | collective-permute-start | bytes 172808 | tf_op jit(solution)/shard_map/ppermute | solution.py:724
  468.8 29.4 %collective-permute-start.26 = (bf16[120,240]{0,1:T(8,128)(2,1)S(1)}, bf16[120,240]{0,1:T(8,128)(2,1)S(1)}, u32[]{:S(2)}, u32[]{:S(2)}) collective-permute-start(bf16[120,240]{0,1:T(8,128)(2,1)S(1)} %fusion.45), channel_id=1, source_target_pairs={{0,4},{1,5},{2,6},{3,7},{4,0},{5,1},{6,2},{7,3},{8,12},{9,13},{10,... | collective-permute-start | bytes 172808 | tf_op jit(solution)/shard_map/ppermute | solution.py:724
  480.4 46.1 %collective-permute-start.42 = (bf16[1,4,960,240]{3,2,1,0:T(8,128)(2,1)}, bf16[1,4,960,240]{3,2,1,0:T(8,128)(2,1)}, u32[]{:S(2)}, u32[]{:S(2)}) collective-permute-start(bf16[1,4,960,240]{3,2,1,0:T(8,128)(2,1)} %get-tuple-element.138), channel_id=1, source_target_pairs={{0,16},{1,17},{2,18},{3,19},{4,20},{5,21},{6,22},{7,23},{8,24},{9,... | collective-permute-start | bytes 5529608 | tf_op jit(solution)/shard_map/ppermute | solution.py:724
  496.5 75.4 %collective-permute-start.38 = (bf16[1,4,960,240]{3,2,1,0:T(8,128)(2,1)}, bf16[1,4,960,240]{3,2,1,0:T(8,128)(2,1)}, u32[]{:S(2)}, u32[]{:S(2)}) collective-permute-start(bf16[1,4,960,240]{3,2,1,0:T(8,128)(2,1)} %get-tuple-element.136), channel_id=1, source_target_pairs={{0,16},{1,17},{2,18},{3,19},{4,20},{5,21},{6,22},{7,23},{8,24},{9,... | collective-permute-start | bytes 5529608 | tf_op jit(solution)/shard_map/ppermute | solution.py:724
  504.8 64.7 %collective-permute-start.28 = (bf16[1,640,240]{2,1,0:T(8,128)(2,1)S(1)}, bf16[1,640,240]{2,1,0:T(8,128)(2,1)S(1)}, u32[]{:S(2)}, u32[]{:S(2)}) collective-permute-start(bf16[1,640,240]{2,1,0:T(8,128)(2,1)S(1)} %fusion.17), channel_id=1, source_target_pairs={{0,16},{1,17},{2,18},{3,19},{4,20},{5,21},{6,22},{7,23},{8,24},{9,... | collective-permute-start | bytes 921608 | tf_op jit(solution)/shard_map/ppermute | solution.py:724
  530.0 60.4 %collective-permute-start.43 = (bf16[2,960,240]{2,1,0:T(8,128)(2,1)}, bf16[2,960,240]{2,1,0:T(8,128)(2,1)}, u32[]{:S(2)}, u32[]{:S(2)}) collective-permute-start(bf16[2,960,240]{2,1,0:T(8,128)(2,1)} %get-tuple-element.142), channel_id=1, source_target_pairs={{0,1},{1,0},{2,3},{3,2},{4,5},{5,4},{6,7},{7,6},{8,9},{9,8},{10,11... | collective-permute-start | bytes 2764808 | tf_op jit(solution)/shard_map/ppermute | solution.py:724
  569.6 19.7 %collective-permute-start.29 = (bf16[2,2,80,240]{3,2,1,0:T(8,128)(2,1)S(1)}, bf16[2,2,80,240]{3,2,1,0:T(8,128)(2,1)}, u32[]{:S(2)}, u32[]{:S(2)}) collective-permute-start(bf16[2,2,80,240]{3,2,1,0:T(8,128)(2,1)S(1)} %fusion.30), channel_id=1, source_target_pairs={{0,1},{1,0},{2,3},{3,2},{4,5},{5,4},{6,7},{7,6},{8,9},{9,8},{10,11... | collective-permute-start | bytes 460808 | tf_op jit(solution)/shard_map/ppermute | solution.py:724
  574.9 61.1 %collective-permute-start.39 = (bf16[2,960,240]{2,1,0:T(8,128)(2,1)}, bf16[2,960,240]{2,1,0:T(8,128)(2,1)S(1)}, u32[]{:S(2)}, u32[]{:S(2)}) collective-permute-start(bf16[2,960,240]{2,1,0:T(8,128)(2,1)} %get-tuple-element.140), channel_id=1, source_target_pairs={{0,1},{1,0},{2,3},{3,2},{4,5},{5,4},{6,7},{7,6},{8,9},{9,8},{10,11... | collective-permute-start | bytes 2764808 | tf_op jit(solution)/shard_map/ppermute | solution.py:724
  590.3 42.9 %collective-permute-start.30 = (bf16[2,80,240]{2,1,0:T(8,128)(2,1)S(1)}, bf16[2,80,240]{2,1,0:T(8,128)(2,1)S(1)}, u32[]{:S(2)}, u32[]{:S(2)}) collective-permute-start(bf16[2,80,240]{2,1,0:T(8,128)(2,1)S(1)} %get-tuple-element.184), channel_id=1, source_target_pairs={{0,2},{1,3},{2,0},{3,1},{4,6},{5,7},{6,4},{7,5},{8,10},{9,11},{10,... | collective-permute-start | bytes 230408 | tf_op jit(solution)/shard_map/ppermute | solution.py:724
  592.4 44.9 %collective-permute-start.44 = (bf16[960,240]{1,0:T(8,128)(2,1)}, bf16[960,240]{1,0:T(8,128)(2,1)}, u32[]{:S(2)}, u32[]{:S(2)}) collective-permute-start(bf16[960,240]{1,0:T(8,128)(2,1)} %fusion.22), channel_id=1, source_target_pairs={{0,2},{1,3},{2,0},{3,1},{4,6},{5,7},{6,4},{7,5},{8,10},{9,11},{10,... | collective-permute-start | bytes 1382408 | tf_op jit(solution)/shard_map/ppermute | solution.py:724
  633.9 17.7 %collective-permute-start.31 = (bf16[80,240]{1,0:T(8,128)(2,1)}, bf16[80,240]{1,0:T(8,128)(2,1)}, u32[]{:S(2)}, u32[]{:S(2)}) collective-permute-start(bf16[80,240]{1,0:T(8,128)(2,1)} %fusion.49), channel_id=1, source_target_pairs={{0,4},{1,5},{2,6},{3,7},{4,0},{5,1},{6,2},{7,3},{8,12},{9,13},{10,... | collective-permute-start | bytes 115208 | tf_op jit(solution)/shard_map/ppermute | solution.py:724
  637.1 21.0 %collective-permute-start.40 = (bf16[960,240]{1,0:T(8,128)(2,1)}, bf16[960,240]{1,0:T(8,128)(2,1)S(1)}, u32[]{:S(2)}, u32[]{:S(2)}) collective-permute-start(bf16[960,240]{1,0:T(8,128)(2,1)} %fusion.20), channel_id=1, source_target_pairs={{0,2},{1,3},{2,0},{3,1},{4,6},{5,7},{6,4},{7,5},{8,10},{9,11},{10,... | collective-permute-start | bytes 1382408 | tf_op jit(solution)/shard_map/ppermute | solution.py:724
  639.4 23.4 %collective-permute-start.45 = (bf16[960,240]{1,0:T(8,128)(2,1)}, bf16[960,240]{1,0:T(8,128)(2,1)}, u32[]{:S(2)}, u32[]{:S(2)}) collective-permute-start(bf16[960,240]{1,0:T(8,128)(2,1)} %fusion.12), channel_id=1, source_target_pairs={{0,4},{1,5},{2,6},{3,7},{4,0},{5,1},{6,2},{7,3},{8,12},{9,13},{10,... | collective-permute-start | bytes 1382408 | tf_op jit(solution)/shard_map/ppermute | solution.py:724
  (53 other events, 599.4 us)
Sparse Core Ops, SparseCore 0:
  10.9 123.8 all-gather.2

commit v2 on v1

v2 whole, which is shorter than its diff:
```python
import functools

import jax
import jax.numpy as jnp
from jax import lax
from jax.experimental import pallas as pl
from jax.experimental.pallas import tpu as pltpu
from jax.sharding import PartitionSpec as P

QUERY_HEADS = 15
KV_HEADS = 5
SHARE = QUERY_HEADS // KV_HEADS
HEAD_DIM = 64
TILE = 128
PROMPT = 1024
LONGEST = 192
EPSILON = 1e-05
THETA = 10000.0
MINUS_LARGE = -1e30
AXES = ("dp", "fsdp")
F32 = jnp.float32
BF16 = jnp.bfloat16
VMEM_BYTES = 60 * 1024 * 1024

NT = (((1,), (1,)), ((), ()))
NN = (((1,), (0,)), ((), ()))
TN = (((0,), (0,)), ((), ()))


def dot(a, b, dims=NN):
    return lax.dot_general(a, b, dims, preferred_element_type=F32)


def params(steps=0):
    return pltpu.CompilerParams(
        vmem_limit_bytes=VMEM_BYTES,
        dimension_semantics=("arbitrary",) * steps if steps else None,
    )


def cost(flops, moved, exps=0):
    return pl.CostEstimate(flops=int(flops), bytes_accessed=int(moved), transcendentals=int(exps))


def whole(shape):
    zeros = (0,) * len(shape)
    return pl.BlockSpec(shape, lambda *_: zeros)


def norm_kernel(hid_ref, cot_ref, gain_ref, router_ref, sel_ref, xn_ref, s1_ref, fg_ref, mix_ref, slope_ref):
    parts, _, width = hid_ref.shape
    square = 0.0
    logit = 0.0
    for d in range(parts):
        x = hid_ref[d].astype(F32)
        square = square + jnp.sum(x * x, axis=-1, keepdims=True)
        logit = logit + jnp.sum(x * router_ref[d], axis=-1, keepdims=True)
    scale = lax.rsqrt(square / (parts * width) + EPSILON)
    chance = 1.0 / (1.0 + jnp.exp(-logit))
    mix = sel_ref[...] * chance
    s1_ref[...] = scale
    mix_ref[...] = mix
    slope_ref[...] = mix * (1.0 - chance)
    for d in range(parts):
        x = hid_ref[d].astype(F32)
        xn_ref[d] = (x * scale * gain_ref[d]).astype(BF16)
        fg_ref[d] = (cot_ref[d].astype(F32) * mix).astype(BF16)


def first_norm(hid4, cot4, gain, router, chosen):
    parts, tokens, width = hid4.shape
    rows = 128
    block = pl.BlockSpec((parts, rows, width), lambda i: (0, i, 0))
    column = pl.BlockSpec((rows, 1), lambda i: (i, 0))
    vector = whole((parts, 1, width))
    return pl.pallas_call(
        norm_kernel,
        grid=(tokens // rows,),
        in_specs=[block, block, vector, vector, column],
        out_specs=[block, column, block, column, column],
        out_shape=[
            jax.ShapeDtypeStruct(hid4.shape, BF16),
            jax.ShapeDtypeStruct((tokens, 1), F32),
            jax.ShapeDtypeStruct(hid4.shape, BF16),
            jax.ShapeDtypeStruct((tokens, 1), F32),
            jax.ShapeDtypeStruct((tokens, 1), F32),
        ],
        compiler_params=params(1),
        cost_estimate=cost(tokens * 960 * 10, tokens * 960 * 8),
        name="first_norm",
    )(hid4, cot4, gain, router, chosen)


def kv_kernel(xn_ref, w_ref, cos_ref, sin1_ref, sin2_ref, tag_ref, out_ref):
    rows = xn_ref.shape[1]
    total = 0.0
    for d in range(xn_ref.shape[0]):
        total = total + dot(xn_ref[d], w_ref[d], NT)
    for h in range(KV_HEADS):
        u = total[:, h * TILE : (h + 1) * TILE]
        turned = (
            u * cos_ref[...]
            + pltpu.roll(u, TILE - HEAD_DIM // 2, 1) * sin1_ref[...]
            + pltpu.roll(u, HEAD_DIM // 2, 1) * sin2_ref[...]
        )
        out_ref[:rows, h * TILE : (h + 1) * TILE] = turned.astype(BF16)
        out_ref[rows:, h * TILE : (h + 1) * TILE] = tag_ref[0]


def kv_project(groups, xn4, wkv, tables, tags):
    parts, tokens, width = xn4.shape
    rows = tokens // groups
    table = pl.BlockSpec((rows, TILE), lambda g: (g, 0))
    return pl.pallas_call(
        kv_kernel,
        grid=(groups,),
        in_specs=[
            pl.BlockSpec((parts, rows, width), lambda g: (0, g, 0)),
            whole(wkv.shape),
            table,
            table,
            table,
            pl.BlockSpec((1, 16, TILE), lambda g: (g, 0, 0)),
        ],
        out_specs=pl.BlockSpec((None, rows + 16, KV_HEADS * TILE), lambda g: (g, 0, 0)),
        out_shape=jax.ShapeDtypeStruct((groups, rows + 16, KV_HEADS * TILE), BF16),
        compiler_params=params(1),
        cost_estimate=cost(2 * tokens * 960 * 640, 3 * tokens * 960 * 2),
        name="kv_project",
    )(xn4, wkv, *tables, tags)


def q_kernel(xn_ref, w_ref, cos_ref, sin_ref, out_ref):
    for h in range(QUERY_HEADS):
        u = 0.0
        for d in range(xn_ref.shape[0]):
            u = u + dot(xn_ref[d], w_ref[d, h * TILE : (h + 1) * TILE], NT)
        turned = u * cos_ref[...] + pltpu.roll(u, HEAD_DIM, 1) * sin_ref[...]
        out_ref[:, h * TILE : (h + 1) * TILE] = turned.astype(BF16)


def q_project(xn4, wq_pad, cos_q, sin_q, groups):
    parts, tokens, width = xn4.shape
    rows = tokens // groups
    table = pl.BlockSpec((rows, TILE), lambda g: (g, 0))
    return pl.pallas_call(
        q_kernel,
        grid=(groups,),
        in_specs=[
            pl.BlockSpec((parts, rows, width), lambda g: (0, g, 0)),
            whole(wq_pad.shape),
            table,
            table,
        ],
        out_specs=pl.BlockSpec((rows, QUERY_HEADS * TILE), lambda g: (g, 0)),
        out_shape=jax.ShapeDtypeStruct((tokens, QUERY_HEADS * TILE), BF16),
        compiler_params=params(1),
        cost_estimate=cost(2 * tokens * 960 * 1920, 6 * tokens * 960 * 2),
        name="q_project",
    )(xn4, wq_pad, cos_q, sin_q)


def slot_needed(slot_ref, s, rows):
    own = slot_ref[0]
    block = slot_ref[s]
    prompt_blocks = PROMPT // rows
    reach = -(-(LONGEST - 1) // rows)
    near = (block < prompt_blocks) | (block >= own - reach)
    return (block >= 0) & (block <= own) & near


def fill_bias(slot_ref, seg_ref, kv_refs, pair_ref, key_ref, turned):
    pairs, rows, _ = pair_ref.shape
    for s, kv_ref in enumerate(kv_refs):
        needed = slot_needed(slot_ref, s, rows)
        for i in range(rows // TILE):
            here = slice(i * TILE, (i + 1) * TILE)
            tag_row = kv_ref[rows : rows + 16, 0:TILE].astype(F32)[i : i + 1]
            tag = jnp.where(needed, jnp.broadcast_to(tag_row, (TILE, TILE)).T, -1.0)
            if s >= pairs:
                lane = lax.broadcasted_iota(jnp.int32, (TILE, TILE), 1)
                hidden = (tag != 0.0) & (lane == HEAD_DIM)
                key_ref[s - pairs, here, :] = jnp.where(hidden, MINUS_LARGE, 0.0).astype(BF16)
                continue
            for j in range(rows // TILE):
                there = slice(j * TILE, (j + 1) * TILE)
                allowed = (tag == 0.0) | (tag == seg_ref[0, :, there])
                if s == 0:
                    key_row = i * TILE + lax.broadcasted_iota(jnp.int32, (TILE, TILE), 0)
                    query_row = j * TILE + lax.broadcasted_iota(jnp.int32, (TILE, TILE), 1)
                    allowed = (allowed & (key_row <= query_row)) | (key_row == query_row)
                bias = jnp.where(allowed, 0.0, MINUS_LARGE)
                if turned:
                    pair_ref[s, there, here] = bias.T
                else:
                    pair_ref[s, here, there] = bias


def lanes_of(dtype, shape, test):
    return jnp.where(test(lax.broadcasted_iota(jnp.int32, shape, 1)), 1.0, 0.0).astype(dtype)


def load_keys(kv_refs, pair_ref, key_ref):
    pairs, rows, _ = pair_ref.shape
    kvs = [ref[:rows, :] for ref in kv_refs]
    other = lanes_of(BF16, (1, TILE), lambda lane: lane != HEAD_DIM)
    marked = [kv * other + (key_ref[s - pairs] if s >= pairs else 0.0) for s, kv in enumerate(kvs)]
    return jnp.concatenate(kvs, axis=0), jnp.concatenate([m.astype(BF16) for m in marked], axis=0)


def mark(q):
    return q + lanes_of(BF16, (1, TILE), lambda lane: lane == HEAD_DIM)


def forward_kernel(slots, slot_ref, q_ref, seg_ref, *refs):
    kv_refs = refs[:slots]
    o_ref, lse_ref, pair_ref, key_ref = refs[slots:]
    rows = q_ref.shape[0]
    pairs = pair_ref.shape[0]

    @pl.when(pl.program_id(1) == 0)
    def _():
        fill_bias(slot_ref, seg_ref, kv_refs, pair_ref, key_ref, True)

    kvs, marked = load_keys(kv_refs, pair_ref, key_ref)
    low = lanes_of(BF16, (1, TILE), lambda lane: lane < HEAD_DIM)
    counted = kvs * (1.0 - low) + low
    lane = lax.broadcasted_iota(jnp.int32, (rows, TILE), 1)
    weights, peaks = [], []
    for j in range(SHARE):
        here = slice(j * TILE, (j + 1) * TILE)
        raw = dot(mark(q_ref[:, here]), marked, NT)
        parts = [raw[:, s * rows : (s + 1) * rows] + pair_ref[s] for s in range(pairs)]
        if slots > pairs:
            parts.append(raw[:, pairs * rows :])
        score = jnp.concatenate(parts, axis=1)
        peak = score[:, :TILE]
        for t in range(1, score.shape[1] // TILE):
            peak = jnp.maximum(peak, score[:, t * TILE : (t + 1) * TILE])
        peak = jnp.max(peak, axis=1, keepdims=True)
        peaks.append(peak)
        weights.append(jnp.exp(score - peak).astype(BF16))
    accs = dot(jnp.concatenate(weights, axis=0), counted)
    for j, peak in enumerate(peaks):
        here = slice(j * TILE, (j + 1) * TILE)
        acc = accs[j * rows : (j + 1) * rows]
        total = jnp.where(lane < HEAD_DIM, acc, 1.0)
        mixed = acc * pltpu.roll(1.0 / total, HEAD_DIM, 1)
        o_ref[:, here] = jnp.where(lane >= HEAD_DIM, mixed, 0.0).astype(BF16)
        lse_ref[0, 0, :, j * rows : (j + 1) * rows] = (peak + jnp.log(total)).T[0:1]


def attention_forward(slot_ids, q, seg, kvs, pairs):
    groups, _, rows = seg.shape
    slots = len(kvs)
    tokens = groups * rows
    wide = SHARE * rows
    heads = pl.BlockSpec((rows, SHARE * TILE), lambda g, h, _: (g, h))
    return pl.pallas_call(
        functools.partial(forward_kernel, slots),
        grid_spec=pltpu.PrefetchScalarGridSpec(
            num_scalar_prefetch=1,
            grid=(groups, KV_HEADS),
            in_specs=[heads, pl.BlockSpec((1, 1, rows), lambda g, h, _: (g, 0, 0))]
            + [pl.BlockSpec((None, rows + 16, TILE), lambda g, h, _: (g, 0, h))] * slots,
            out_specs=[heads, pl.BlockSpec((1, 1, 1, wide), lambda g, h, _: (g, h, 0, 0))],
            scratch_shapes=[
                pltpu.VMEM((pairs, rows, rows), F32),
                pltpu.VMEM((max(slots - pairs, 1), rows, TILE), BF16),
            ],
        ),
        out_shape=[
            jax.ShapeDtypeStruct(q.shape, BF16),
            jax.ShapeDtypeStruct((groups, KV_HEADS, 1, wide), F32),
        ],
        compiler_params=params(2),
        cost_estimate=cost(2 * 15 * tokens * 1536 * 256, 8 * tokens * 960 * 2, 15 * tokens * 1536),
        name="attention_forward",
    )(slot_ids, q, seg, *kvs)


def backward_kernel(slots, slot_ref, q_ref, do_ref, o_ref, lse_ref, seg_ref, cos_ref, sin1_ref, sin2_ref, *refs):
    kv_refs = refs[:slots]
    dq_ref = refs[slots]
    dkv_refs = refs[slots + 1 : -2]
    pair_ref, key_ref = refs[-2:]
    rows = q_ref.shape[0]

    @pl.when(pl.program_id(1) == 0)
    def _():
        fill_bias(slot_ref, seg_ref, kv_refs, pair_ref, key_ref, False)

    kvs, marked = load_keys(kv_refs, pair_ref, key_ref)
    pairs = pair_ref.shape[0]
    left, right = [], []
    for j in range(SHARE):
        here = slice(j * TILE, (j + 1) * TILE)
        q, do = q_ref[:, here], do_ref[:, here]
        delta = jnp.sum((do.astype(F32) * o_ref[:, here].astype(F32)).T, axis=0, keepdims=True)
        raw = dot(marked, mark(q), NT)
        parts = [raw[s * rows : (s + 1) * rows] + pair_ref[s] for s in range(pairs)]
        if slots > pairs:
            parts.append(raw[pairs * rows :])
        prob = jnp.exp(jnp.concatenate(parts, axis=0) - lse_ref[0, 0, :, j * rows : (j + 1) * rows])
        slope = (prob * (dot(kvs, do, NT) - delta)).astype(BF16)
        left += [slope, prob.astype(BF16)]
        right += [q, do]
        part = dot(slope, kvs, TN)
        back = (
            part * cos_ref[...]
            - pltpu.roll(part, TILE - HEAD_DIM // 2, 1) * sin1_ref[...]
            - pltpu.roll(part, HEAD_DIM // 2, 1) * sin2_ref[...]
        )
        dq_ref[:, here] = back.astype(BF16)
    right = jnp.concatenate(right, axis=0)
    for s in range(slots):
        band = jnp.concatenate([part[s * rows : (s + 1) * rows] for part in left], axis=1)
        dkv_refs[s][...] = dot(band, right).astype(BF16)


def attention_backward(slot_ids, q, do, o, lse, seg, tables, kvs, pairs):
    groups, _, rows = seg.shape
    slots = len(kvs)
    heads = pl.BlockSpec((rows, SHARE * TILE), lambda g, h, _: (g, h))
    seg_spec = pl.BlockSpec((1, 1, rows), lambda g, h, _: (g, 0, 0))
    kv_spec = pl.BlockSpec((None, rows + 16, TILE), lambda g, h, _: (g, 0, h))
    lse_spec = pl.BlockSpec((1, 1, 1, SHARE * rows), lambda g, h, _: (g, h, 0, 0))
    table = pl.BlockSpec((rows, TILE), lambda g, h, _: (g, 0))
    grad = pl.BlockSpec((None, rows, TILE), lambda g, h, _: (g, 0, h))
    tokens = groups * rows
    out = pl.pallas_call(
        functools.partial(backward_kernel, slots),
        grid_spec=pltpu.PrefetchScalarGridSpec(
            num_scalar_prefetch=1,
            grid=(groups, KV_HEADS),
            in_specs=[heads, heads, heads, lse_spec, seg_spec, table, table, table] + [kv_spec] * slots,
            out_specs=[heads] + [grad] * slots,
            scratch_shapes=[
                pltpu.VMEM((pairs, rows, rows), F32),
                pltpu.VMEM((max(slots - pairs, 1), rows, TILE), BF16),
            ],
        ),
        out_shape=[jax.ShapeDtypeStruct(q.shape, BF16)]
        + [jax.ShapeDtypeStruct((groups, rows, KV_HEADS * TILE), BF16)] * slots,
        compiler_params=params(2),
        cost_estimate=cost(5 * 15 * tokens * 1536 * 256, 16 * tokens * 960 * 2, 15 * tokens * 1536),
        name="attention_backward",
    )(slot_ids, q, do, o, lse, seg, *tables, *kvs)
    return out[0], out[1:]


def out_kernel(o_ref, w_ref, hid_ref, gain_ref, mid_ref, x2_ref, s2_ref):
    parts, _, width = hid_ref.shape
    o = o_ref[...]
    square = 0.0
    for d in range(parts):
        middle = hid_ref[d].astype(F32) + dot(o, w_ref[d])
        mid_ref[d] = middle
        square = square + jnp.sum(middle * middle, axis=-1, keepdims=True)
    scale = lax.rsqrt(square / (parts * width) + EPSILON)
    s2_ref[...] = scale
    for d in range(parts):
        x2_ref[d] = (mid_ref[d] * scale * gain_ref[d]).astype(BF16)


def out_project(o, wo_pad, hid4, gain):
    parts, tokens, width = hid4.shape
    rows = 128
    block = pl.BlockSpec((parts, rows, width), lambda i: (0, i, 0))
    column = pl.BlockSpec((rows, 1), lambda i: (i, 0))
    return pl.pallas_call(
        out_kernel,
        grid=(tokens // rows,),
        in_specs=[
            pl.BlockSpec((rows, o.shape[1]), lambda i: (i, 0)),
            whole(wo_pad.shape),
            block,
            whole((parts, 1, width)),
        ],
        out_specs=[block, block, column],
        out_shape=[
            jax.ShapeDtypeStruct(hid4.shape, F32),
            jax.ShapeDtypeStruct(hid4.shape, BF16),
            jax.ShapeDtypeStruct((tokens, 1), F32),
        ],
        compiler_params=params(1),
        cost_estimate=cost(2 * tokens * 960 * 1920, 8 * tokens * 960 * 2),
        name="out_project",
    )(o, wo_pad, hid4, gain)


def ffn_kernel(meta_ref, x_ref, fg_ref, w_ref, out_ref, xg_ref, keep_ref, send_ref):
    parts = x_ref.shape[0]
    count = w_ref.shape[1]
    rows = w_ref.shape[2] // 3
    width = w_ref.shape[3]
    my_part, my_place = meta_ref[0], meta_ref[2]
    bits = count.bit_length() - 1
    turn_bits = [sum((i >> b & 1) << (bits - 1 - b) for b in range(bits)) for i in range(count)]

    def tokens_of(ref, e):
        return ref[pl.ds(my_part ^ e, 1)].reshape(ref.shape[1:])

    def weight(e, which):
        part = pl.ds(my_part ^ e, 1)
        band = slice(which * rows, (which + 1) * rows)
        pieces = [w_ref[part, pl.ds(my_place ^ i, 1), band, :].reshape(rows, width) for i in turn_bits]
        return jnp.concatenate(pieces, axis=0)

    gate = 0.0
    up = 0.0
    hidden_grad = 0.0
    for e in range(parts):
        x = tokens_of(x_ref, e)
        gate = gate + dot(x, weight(e, 0), NT)
        up = up + dot(x, weight(e, 1), NT)
        hidden_grad = hidden_grad + dot(tokens_of(fg_ref, e), weight(e, 2), NT)
    chance = 1.0 / (1.0 + jnp.exp(-gate))
    silu = gate * chance
    hidden = (silu * up).astype(BF16)
    up_grad = (hidden_grad * silu).astype(BF16)
    gate_grad = (hidden_grad * up * chance * (1.0 + gate * (1.0 - chance))).astype(BF16)

    first = pl.program_id(0) == 0
    for e in range(parts):
        place = pl.ds(my_part ^ e, 1)
        out = dot(hidden, weight(e, 2))[None]
        back = (dot(gate_grad, weight(e, 0)) + dot(up_grad, weight(e, 1)))[None]

        @pl.when(first)
        def _(place=place, out=out, back=back):
            out_ref[place] = out
            xg_ref[place] = back

        @pl.when(jnp.logical_not(first))
        def _(place=place, out=out, back=back):
            out_ref[place] += out
            xg_ref[place] += back

    turned = (gate_grad.T, up_grad.T, hidden.T)
    for e in range(parts):
        target = send_ref if e % 2 else keep_ref
        for which in range(3):
            right = tokens_of(fg_ref if which == 2 else x_ref, e)
            grad = dot(turned[which], right).astype(BF16)
            for i in range(count):
                target[e // 2, i, which * rows : (which + 1) * rows, :] = grad[i * rows : (i + 1) * rows]


def ffn(my_part, my_shard, rows3, x4, fg4, weights, shard_first):
    parts, tokens, width = x4.shape
    half = weights.shape[1]
    block = pl.BlockSpec((parts, half, None, rows3, width), lambda j, m: (0, 0, m[1] ^ j, 0, 0))
    if shard_first:
        grad_block = pl.BlockSpec((None, parts // 2, half, rows3, width), lambda j, m: (j, 0, 0, 0, 0))
        grad = jax.ShapeDtypeStruct((2, parts // 2, half, rows3, width), BF16)
    else:
        grad_block = pl.BlockSpec((parts // 2, None, half, rows3, width), lambda j, m: (0, j, 0, 0, 0))
        grad = jax.ShapeDtypeStruct((parts // 2, 2, half, rows3, width), BF16)
    meta = jnp.stack([my_part, my_shard % 2, my_shard // 2]).astype(jnp.int32)
    return pl.pallas_call(
        ffn_kernel,
        grid_spec=pltpu.PrefetchScalarGridSpec(
            num_scalar_prefetch=1,
            grid=(2,),
            in_specs=[whole(x4.shape), whole(x4.shape), block],
            out_specs=[whole(x4.shape), whole(x4.shape), grad_block, grad_block],
        ),
        out_shape=[jax.ShapeDtypeStruct(x4.shape, F32)] * 2 + [grad, grad],
        compiler_params=params(1),
        cost_estimate=cost(12 * tokens * 960 * rows3 * half, 8 * tokens * 960 * 2 + 8 * 960 * rows3 * half),
        name="ffn",
    )(meta, x4, fg4, weights)


def middle_kernel(
    mid_ref, hid_ref, cot_ref, out_a_ref, out_b_ref, xg_a_ref, xg_b_ref, mix_ref, slope_ref, s2_ref, gain_ref, router_ref,
    hidden_ref, part_ref, ag_ref, router_grad_ref, gain_grad_ref,
):
    parts, rows, width = mid_ref.shape
    mix = mix_ref[...]
    scale = s2_ref[...]
    inner = 0.0
    mean = 0.0
    for d in range(parts):
        middle = mid_ref[d]
        inputs = hid_ref[d].astype(F32)
        branch = (middle - inputs) + (out_a_ref[d] + out_b_ref[d])
        upstream = cot_ref[d].astype(F32)
        inner = inner + jnp.sum(upstream * branch, axis=-1, keepdims=True)
        hidden_ref[d] = (inputs + mix * branch).astype(BF16)
        mean = mean + jnp.sum((xg_a_ref[d] + xg_b_ref[d]) * gain_ref[d] * middle, axis=-1, keepdims=True)
    logit_grad = slope_ref[...] * inner
    mean = mean / (parts * width) * (scale * scale * scale)
    first = pl.program_id(0) == 0
    for d in range(parts):
        middle = mid_ref[d]
        inputs = hid_ref[d].astype(F32)
        upstream = cot_ref[d].astype(F32)
        grad = xg_a_ref[d] + xg_b_ref[d]
        middle_grad = scale * (grad * gain_ref[d]) - middle * mean
        ag_ref[d] = (upstream * mix + middle_grad).astype(BF16)
        part_ref[d] = upstream + logit_grad * router_ref[d] + middle_grad
        router_grad = jnp.sum(logit_grad * inputs, axis=0, keepdims=True)
        gain_grad = jnp.sum(grad * middle * scale, axis=0, keepdims=True)

        @pl.when(first)
        def _(d=d, router_grad=router_grad, gain_grad=gain_grad):
            router_grad_ref[d] = router_grad
            gain_grad_ref[d] = gain_grad

        @pl.when(jnp.logical_not(first))
        def _(d=d, router_grad=router_grad, gain_grad=gain_grad):
            router_grad_ref[d] += router_grad
            gain_grad_ref[d] += gain_grad


def middle_step(mid4, hid4, cot4, outs, grads, mix, slope, s2, gain, router):
    parts, tokens, width = mid4.shape
    rows = 128
    block = pl.BlockSpec((parts, rows, width), lambda i: (0, i, 0))
    column = pl.BlockSpec((rows, 1), lambda i: (i, 0))
    vector = whole((parts, 1, width))
    return pl.pallas_call(
        middle_kernel,
        grid=(tokens // rows,),
        in_specs=[block] * 7 + [column] * 3 + [vector] * 2,
        out_specs=[block, block, block, vector, vector],
        out_shape=[
            jax.ShapeDtypeStruct(mid4.shape, BF16),
            jax.ShapeDtypeStruct(mid4.shape, F32),
            jax.ShapeDtypeStruct(mid4.shape, BF16),
            jax.ShapeDtypeStruct((parts, 1, width), F32),
            jax.ShapeDtypeStruct((parts, 1, width), F32),
        ],
        compiler_params=params(1),
        cost_estimate=cost(tokens * 960 * 30, tokens * 960 * 36),
        name="middle_step",
    )(mid4, hid4, cot4, *outs, *grads, mix, slope, s2, gain, router)


def compact(tile_major, upper):
    count = tile_major.shape[0] // TILE
    start = HEAD_DIM if upper else 0
    return jnp.concatenate(
        [tile_major[h * TILE + start : h * TILE + start + HEAD_DIM] for h in range(count)], axis=0
    )


def out_back_kernel(ag_ref, w_ref, do_ref):
    for h in range(QUERY_HEADS):
        total = 0.0
        for d in range(ag_ref.shape[0]):
            total = total + dot(ag_ref[d], w_ref[d, h * TILE : (h + 1) * TILE], NT)
        do_ref[:, h * TILE : (h + 1) * TILE] = total.astype(BF16)


def out_back(ag4, wo_pad):
    parts, tokens, width = ag4.shape
    rows = 256
    return pl.pallas_call(
        out_back_kernel,
        grid=(tokens // rows,),
        in_specs=[pl.BlockSpec((parts, rows, width), lambda i: (0, i, 0)), whole(wo_pad.shape)],
        out_specs=pl.BlockSpec((rows, wo_pad.shape[1]), lambda i: (i, 0)),
        out_shape=jax.ShapeDtypeStruct((tokens, wo_pad.shape[1]), BF16),
        compiler_params=params(1),
        cost_estimate=cost(2 * tokens * 960 * 1920, 6 * tokens * 960 * 2),
        name="out_back",
    )(ag4, wo_pad)


def qo_back_kernel(meta_ref, dq_ref, xn_ref, w_ref, o_ref, ag_ref, keep_ref, send_ref, xg_ref):
    parts = xn_ref.shape[0]
    sides = ((compact(dq_ref[...].T, False), xn_ref), (compact(o_ref[...].T, True), ag_ref))
    for e in range(parts):
        target = send_ref if e % 2 else keep_ref
        for i, (left, ref) in enumerate(sides):
            right = ref[pl.ds(meta_ref[0] ^ e, 1)].reshape(ref.shape[1:])
            target[e // 2, i] = dot(left, right).astype(BF16)
    for d in range(parts):
        xg_ref[d] = dot(dq_ref[...], w_ref[d])


def qo_back(my_part, dq, xn4, wq_pad, o, ag4):
    parts, tokens, width = xn4.shape
    grad = jax.ShapeDtypeStruct((parts // 2, 2, QUERY_HEADS * HEAD_DIM, width), BF16)
    return pl.pallas_call(
        qo_back_kernel,
        grid_spec=pltpu.PrefetchScalarGridSpec(
            num_scalar_prefetch=1,
            grid=(1,),
            in_specs=[whole(a.shape) for a in (dq, xn4, wq_pad, o, ag4)],
            out_specs=[whole(grad.shape), whole(grad.shape), whole(xn4.shape)],
        ),
        out_shape=[grad, grad, jax.ShapeDtypeStruct(xn4.shape, F32)],
        compiler_params=params(1),
        cost_estimate=cost(2 * tokens * 960 * 3840, 14 * tokens * 960 * 2),
        name="qo_back",
    )(my_part.reshape(1), dq, xn4, wq_pad, o, ag4)


def kv_back_kernel(meta_ref, dkv_ref, cos_ref, sin1_ref, sin2_ref, xn_ref, back_ref, keep_ref, send_ref):
    for h in range(KV_HEADS):
        u = dkv_ref[:, h * TILE : (h + 1) * TILE].astype(F32)
        back = (
            u * cos_ref[...]
            - pltpu.roll(u, TILE - HEAD_DIM // 2, 1) * sin1_ref[...]
            - pltpu.roll(u, HEAD_DIM // 2, 1) * sin2_ref[...]
        )
        back_ref[:, h * TILE : (h + 1) * TILE] = back.astype(BF16)
    turned = back_ref[...].T
    for e in range(xn_ref.shape[0]):
        x = xn_ref[pl.ds(meta_ref[0] ^ e, 1)].reshape(xn_ref.shape[1:])
        target = send_ref if e % 2 else keep_ref
        target[e // 2] = dot(turned, x).astype(BF16)


def kv_back(my_part, dkv, tables, xn4):
    parts, tokens, width = xn4.shape
    grad = jax.ShapeDtypeStruct((parts // 2, KV_HEADS * TILE, width), BF16)
    table = whole((tokens, TILE))
    return pl.pallas_call(
        kv_back_kernel,
        grid_spec=pltpu.PrefetchScalarGridSpec(
            num_scalar_prefetch=1,
            grid=(1,),
            in_specs=[whole(dkv.shape), table, table, table, whole(xn4.shape)],
            out_specs=[whole((tokens, KV_HEADS * TILE)), whole(grad.shape), whole(grad.shape)],
        ),
        out_shape=[jax.ShapeDtypeStruct((tokens, KV_HEADS * TILE), BF16), grad, grad],
        compiler_params=params(1),
        cost_estimate=cost(2 * tokens * 960 * 640, 6 * tokens * 960 * 2),
        name="kv_back",
    )(my_part.reshape(1), dkv, *tables, xn4)


def final_kernel(xg_ref, kvb_ref, wkv_ref, hid_ref, part_ref, s1_ref, gain_ref, out_ref, gain_grad_ref):
    parts, rows, width = hid_ref.shape
    scale = s1_ref[...]
    kvb = kvb_ref[...]
    mean = 0.0
    first = pl.program_id(0) == 0
    for d in range(parts):
        grad = xg_ref[d] + dot(kvb, wkv_ref[d])
        inputs = hid_ref[d].astype(F32)
        gain_grad = jnp.sum(grad * inputs * scale, axis=0, keepdims=True)
        scaled = grad * gain_ref[d]
        out_ref[d] = scaled
        mean = mean + jnp.sum(scaled * inputs, axis=-1, keepdims=True)

        @pl.when(first)
        def _(d=d, gain_grad=gain_grad):
            gain_grad_ref[d] = gain_grad

        @pl.when(jnp.logical_not(first))
        def _(d=d, gain_grad=gain_grad):
            gain_grad_ref[d] += gain_grad

    mean = mean / (parts * width) * (scale * scale * scale)
    for d in range(parts):
        out_ref[d] = part_ref[d] + scale * out_ref[d] - hid_ref[d].astype(F32) * mean


def final_step(xg4, kvb, wkv, hid4, part4, s1, gain):
    parts, tokens, width = hid4.shape
    rows = 128
    block = pl.BlockSpec((parts, rows, width), lambda i: (0, i, 0))
    column = pl.BlockSpec((rows, 1), lambda i: (i, 0))
    vector = whole((parts, 1, width))
    return pl.pallas_call(
        final_kernel,
        grid=(tokens // rows,),
        in_specs=[
            block,
            pl.BlockSpec((rows, kvb.shape[1]), lambda i: (i, 0)),
            whole(wkv.shape),
            block,
            block,
            column,
            vector,
        ],
        out_specs=[block, vector],
        out_shape=[
            jax.ShapeDtypeStruct(hid4.shape, F32),
            jax.ShapeDtypeStruct((parts, 1, width), F32),
        ],
        compiler_params=params(1),
        cost_estimate=cost(2 * tokens * 960 * 640, 10 * tokens * 960 * 2),
        name="final_step",
    )(xg4, kvb, wkv, hid4, part4, s1, gain)


class Clock:
    def __init__(self):
        self.token = jnp.zeros((8, TILE), F32)

    def at(self, *values):
        out = lax.optimization_barrier(values + (self.token,))
        self.token = out[-1]
        return out[0] if len(values) == 1 else out[:-1]

    def after(self, value):
        return lax.optimization_barrier((value, self.token))[0]


def add(mine, other, dtype=BF16):
    return (mine.astype(F32) + other.astype(F32)).astype(dtype)


class Net:
    def __init__(self, clock, parts, shards):
        self.clock = clock
        self.parts, self.shards = parts, shards
        self.size = parts * shards
        self.index = lax.axis_index("dp") * shards + lax.axis_index("fsdp")
        self.bits = self.size.bit_length() - 1
        self.core = shards.bit_length() - 1
        self.order = list(range(self.core - 1, -1, -1)) + list(range(self.core + 1, self.bits)) + [self.core]

    def swap(self, array, bit):
        flip = 1 << bit
        return lax.ppermute(self.clock.at(array), AXES, [(i, i ^ flip) for i in range(self.size)])

    def on(self, bit):
        return (self.index >> bit) & 1 == 1


class Gather:
    def __init__(self, net, array):
        self.net = net
        self.shape = array.shape
        self.array = array
        self.left = list(net.order)
        self.other = None

    def step(self):
        net = self.net
        if self.other is not None:
            bit = self.left.pop(0)
            other = net.clock.at(self.other)
            here = net.on(bit)
            self.array = jnp.stack([jnp.where(here, other, self.array), jnp.where(here, self.array, other)])
        if self.left:
            self.other = net.swap(self.array, self.left[0])

    def finish(self):
        while self.left:
            self.step()
        net = self.net
        place = {bit: net.bits - 1 - i for i, bit in enumerate(net.order)}
        high_first = [place[bit] for bit in range(net.bits - 1, -1, -1)]
        array = jnp.transpose(self.array, high_first + list(range(net.bits, self.array.ndim)))
        return array.reshape((net.parts, net.shards) + self.shape)


class Scatter:
    def __init__(self, net, keep, send, sections, rows, by_distance=None):
        self.net, self.relative = net, by_distance is not None
        self.left = [net.core] + (by_distance or list(reversed(net.order[:-1])))
        width = keep.shape[-1]
        if self.relative:
            shape = (-1, rows, width)
        else:
            shape = (net.parts // 2, sections, net.shards, rows, width)
        self.keep, self.other = keep.reshape(shape), net.swap(send, self.left.pop(0)).reshape(shape)

    def halves(self, array, bit):
        if self.relative or bit > self.net.core:
            half = array.shape[0] // 2
            return array[:half], array[half:]
        if array.ndim == 5:
            array = array[0]
        pairs = array.reshape((array.shape[0], -1, 2) + array.shape[2:])
        on = (self.net.index >> bit) & 1
        pick = lambda i: lax.dynamic_index_in_dim(pairs, i, 2, keepdims=False)
        return pick(on), pick(1 - on)

    def land(self):
        self.other = self.net.clock.at(self.other)

    def send(self):
        bit = self.left.pop(0)
        keep, send = self.halves(self.keep, bit)
        other_keep, other_send = self.halves(self.other, bit)
        self.keep = add(keep, other_keep)
        self.other = self.net.swap(add(send, other_send), bit)

    def step(self):
        if self.left:
            self.land()
            self.send()

    def result(self):
        while self.left:
            self.step()
        grad = add(self.keep, self.net.clock.at(self.other), F32)
        return grad[0] if self.relative else grad.reshape((grad.shape[-4],) + grad.shape[-2:])


class SumAll:
    def __init__(self, net, array):
        self.net, self.array = net, array
        self.left = list(reversed(net.order))
        self.other = None

    def step(self):
        if self.other is not None:
            self.array = self.array + self.net.clock.at(self.other)
            self.other = None
        if self.left:
            self.other = self.net.swap(self.array, self.left.pop(0))

    def result(self):
        while self.left or self.other is not None:
            self.step()
        return self.array


class EightShards:
    a_moves = [(2 * z, 2 * z + 1) for z in range(4)] + [(7, 6)]
    b_moves = [(2, 3), (3, 2), (4, 5), (5, 4), (6, 7), (7, 6)]
    c_moves = [(4, 5), (5, 4), (6, 7), (7, 6)]

    def __init__(self, clock, parts, shards):
        self.clock, self.parts, self.shards = clock, parts, shards
        self.shard = lax.axis_index("fsdp")
        self.z, self.y = self.shard // 2, self.shard % 2
        self.top, self.odd = self.z == 3, self.y == 1

    def move(self, array, moves):
        pairs = [(d * self.shards + a, d * self.shards + b) for d in range(self.parts) for a, b in moves]
        return lax.ppermute(self.clock.at(array), AXES, pairs)

    def up(self, array, lowest):
        return self.move(array, [(2 * z + y, 2 * z + y + 2) for z in range(lowest, 3) for y in range(2)])

    def down(self, array, lowest):
        return self.move(array, [(2 * z + y + 2, 2 * z + y) for z in range(lowest, 3) for y in range(2)])

    def slot_ids(self):
        shard, z, y = self.shard, self.z, self.y
        none = jnp.int32(-1)
        return jnp.stack(
            [
                shard,
                jnp.where(y == 1, shard - 1, jnp.where(z == 3, 5, none)),
                jnp.where(z == 3, 3 - y, jnp.where(z >= 1, 2 * (z - 1) + 1 - y, none)),
                jnp.where(z >= 2, shard - 4, none),
                jnp.where(z >= 2, 1 - y, none),
                jnp.where(z == 3, y, jnp.where(z >= 1, shard - 2, none)),
            ]
        ).astype(jnp.int32)

    def spread(self, own):
        at = self.clock.at
        up1 = self.up(own, 0)
        yield
        up1 = at(up1)
        up2 = self.up(up1, 1)
        a = self.move(jnp.where(self.top & self.odd, up1, own), self.a_moves)
        yield
        up2, a = at(up2, a)
        up3 = self.up(up2, 2)
        b = self.move(jnp.where(self.top, up2, up1), self.b_moves)
        yield
        up3, b = at(up3, b)
        c = self.move(jnp.where(self.top, up3, up2), self.c_moves)
        yield
        last = jnp.where(self.top, up3, up1)
        c = at(c)
        yield [own, a, b, up2, c, last]

    pairs = 2

    def collect(self, grads):
        at = self.clock.at
        own, a, b, up2, c, last = grads
        back = lambda moves: [(t, s) for s, t in moves]
        wide = lambda array: array.astype(F32)
        from_c, from_b = self.move(c, back(self.c_moves)), self.move(b, back(self.b_moves))
        yield
        from_c = wide(at(from_c))
        first = self.down((wide(last) + from_c).astype(BF16), 2)
        from_a = self.move(a, back(self.a_moves))
        yield
        from_b, first = at(from_b, first)
        from_b, first = wide(from_b), wide(first)
        second = self.down((wide(up2) + jnp.where(self.top, from_b, from_c + first)).astype(BF16), 1)
        yield
        from_a, second = at(from_a, second)
        from_a, second = wide(from_a), wide(second)
        late = self.top & self.odd
        level = jnp.where(self.top, jnp.where(self.odd, from_a, 0.0), wide(last) + from_b + second)
        third = self.down(level.astype(BF16), 0)
        yield
        third = wide(at(third))
        yield (wide(own) + jnp.where(late, 0.0, from_a) + third).astype(BF16)


class AnyShards:
    def __init__(self, clock, parts, shards):
        self.shards = shards
        self.pairs = shards
        self.shard = lax.axis_index("fsdp")

    def slot_ids(self):
        return (self.shard - jnp.arange(self.shards)).astype(jnp.int32)

    def pick(self, array, s):
        return lax.dynamic_index_in_dim(array, (self.shard - s) % self.shards, 0, keepdims=False)

    def spread(self, own):
        every = lax.all_gather(own, "fsdp", axis=0, tiled=False)
        yield from (None,) * 4
        yield [own] + [self.pick(every, s) for s in range(1, self.shards)]

    def collect(self, grads):
        every = jnp.stack(grads)
        order = jnp.stack([self.pick(every, s) for s in range(self.shards)])
        yield from (None,) * 4
        yield lax.psum_scatter(order, "fsdp", scatter_dimension=0, tiled=False)


def shards(
    hidden_in, segment, position, selected, gain_attn, gain_ffn, router,
    w_query, key_weight, value_weight, w_output, w_gate, w_up, w_down, cotangent,
):
    groups, rows, model = hidden_in.shape
    tokens = groups * rows
    parts, shard_count = lax.axis_size("dp"), lax.axis_size("fsdp")
    width = model // parts
    clock = Clock()
    at = clock.at
    net = Net(clock, parts, shard_count)
    my_part, my_shard = lax.axis_index("dp"), lax.axis_index("fsdp")
    ring = (EightShards if shard_count == 8 else AnyShards)(clock, parts, shard_count)

    small = jnp.concatenate([key_weight.T, value_weight.T, w_query.T], axis=0)
    kv_rows, q_rows = key_weight.shape[1], w_query.shape[1]
    gate_rows, up_rows = w_gate.T, w_up.T
    chunk_rows = w_down.shape[0] // 2
    large = [w[c * chunk_rows : (c + 1) * chunk_rows] for c in range(2) for w in (gate_rows, up_rows, w_down)]
    large = [jnp.concatenate(large[:3] + [w_output], axis=0), jnp.concatenate(large[3:], axis=0)]

    def heads_of(array, count):
        return array.reshape(parts, count, HEAD_DIM, width)

    def split(array):
        return jnp.transpose(array.reshape(tokens, parts, width), (1, 0, 2))

    def join(array):
        return jnp.transpose(array, (1, 0, 2)).reshape(groups, rows, model)

    half = HEAD_DIM // 2
    frequency = THETA ** (-(jnp.arange(half).astype(F32) * 2.0) / HEAD_DIM)
    angles = position.reshape(tokens).astype(F32)[:, None] * frequency[None, :]
    cos, sin = jnp.cos(angles), jnp.sin(angles)
    zero, one = jnp.zeros_like(cos), jnp.ones_like(cos)
    table = lambda *four: jnp.concatenate(four, axis=1)
    kv_tables = (table(cos, cos, one, one), table(-sin, zero, zero, zero), table(zero, sin, zero, zero))
    shrink = HEAD_DIM**-0.5
    q_tables = tuple(
        shrink * t
        for t in (table(cos, cos, zero, zero), table(-sin, zero, zero, zero), table(zero, sin, zero, zero))
    )
    seg_rows = segment.astype(F32).reshape(groups, 1, rows)
    tags = jnp.where(selected == 1, segment, -1).astype(BF16).reshape(groups, rows // TILE, TILE)
    tags = jnp.pad(tags, ((0, 0), (0, 16 - rows // TILE), (0, 0)))
    hid4, cot4 = split(hidden_in), split(cotangent)
    vector = lambda v: v.astype(F32).reshape(parts, 1, width)
    gain_one, gain_two, route = vector(gain_attn), vector(gain_ffn), vector(router)
    chosen = selected.reshape(tokens, 1).astype(F32)

    small_gather = Gather(net, small)
    small_gather.step()
    small_gather.step()
    small_gather.step()
    xn4, s1, fg4, mix, slope = first_norm(hid4, cot4, gain_one, route, chosen)
    xn4 = at(xn4)
    small_gather.step()
    first_all = lax.all_gather(clock.after(large[0]), AXES, axis=0, tiled=False)
    small_all = small_gather.finish()
    keys = heads_of(small_all[:, :, :kv_rows], KV_HEADS)
    values = heads_of(small_all[:, :, kv_rows : 2 * kv_rows], KV_HEADS)
    wkv = jnp.concatenate([keys, values], axis=2).reshape(parts, KV_HEADS * TILE, width)
    spread = ring.spread(kv_project(groups, xn4, wkv, kv_tables, tags))
    next(spread)
    queries = heads_of(small_all[:, :, 2 * kv_rows :], QUERY_HEADS)
    wq_pad = jnp.concatenate([queries, queries[:, :, half:], queries[:, :, :half]], axis=2)
    wq_pad = wq_pad.reshape(parts, QUERY_HEADS * TILE, width)
    q = at(q_project(xn4, wq_pad, q_tables[0], q_tables[1] + q_tables[2], groups))
    next(spread)
    second_all = lax.all_gather(clock.after(large[1]), AXES, axis=0, tiled=False)
    next(spread)
    next(spread)
    slot_ids = ring.slot_ids()
    kvs = next(spread)
    o, lse = at(*attention_forward(slot_ids, q, seg_rows, kvs, ring.pairs))
    outputs = heads_of(first_all[:, 3 * chunk_rows :], QUERY_HEADS)
    wo_pad = jnp.concatenate([jnp.zeros_like(outputs), outputs], axis=2)
    wo_pad = wo_pad.reshape(parts, QUERY_HEADS * TILE, width)
    mid4, x24, s2 = out_project(o, wo_pad, hid4, gain_two)
    x24 = at(x24)

    ffn_all = [a.reshape((parts, shard_count // 2, 2) + a.shape[1:]) for a in (first_all, second_all)]
    bits = net.order[:-1][::-1]
    parts_bits = [bit for bit in bits if bit > net.core]
    shards_bits = [bit for bit in bits if bit < net.core]
    out_a, xg_a, keep_a, send_a = ffn(my_part, my_shard, 3 * chunk_rows, x24, fg4, ffn_all[0], False)
    scatter_a = Scatter(net, keep_a, send_a, 1, 3 * chunk_rows, parts_bits + shards_bits)
    out_b, xg_b, keep_b, send_b = ffn(my_part, my_shard, 3 * chunk_rows, x24, fg4, ffn_all[1], True)
    scatter_b = Scatter(net, keep_b, send_b, 1, 3 * chunk_rows, shards_bits[:1] + parts_bits + shards_bits[1:])
    scatter_a.step()
    out_b = at(out_b)
    hidden4, part4, ag4, router_sum, gain_two_sum = middle_step(
        mid4, hid4, cot4, (out_a, out_b), (xg_a, xg_b), mix, slope, s2, gain_two, route
    )
    ag4 = at(ag4)
    scatter_b.step()
    do = at(out_back(ag4, wo_pad))
    dq, dkvs = attention_backward(slot_ids, q, do, o, lse, seg_rows, q_tables, kvs, ring.pairs)
    dq = at(dq)
    scatter_b.land()
    scatter_a.land()
    collect = ring.collect(dkvs)
    next(collect)
    scatter_b.send()
    keep_qo, send_qo, xg_q = qo_back(my_part, dq, xn4, wq_pad, o, ag4)
    xg_q = at(xg_q)
    next(collect)
    scatter_qo = Scatter(net, keep_qo, send_qo, 2, q_rows)
    next(collect)
    scatter_a.send()
    scatter_qo.step()
    next(collect)
    scatter_b.step()
    dkv = next(collect).reshape(tokens, KV_HEADS * TILE)
    kvb, keep_kv, send_kv = kv_back(my_part, dkv, kv_tables, xn4)

    def by_kind(array):
        tiles = array.reshape(array.shape[0], KV_HEADS, 2, HEAD_DIM, width)
        return jnp.transpose(tiles, (0, 2, 1, 3, 4))

    scatter_kv = Scatter(net, by_kind(keep_kv), by_kind(send_kv), 2, kv_rows)
    kvb = at(kvb)
    grad_in4, gain_one_sum = final_step(xg_q, kvb, wkv, hid4, part4, s1, gain_one)
    scatter_kv.step()
    scatter_a.step()
    scatter_qo.step()
    scatter_b.step()
    sums = SumAll(net, jnp.stack([gain_one_sum, gain_two_sum, router_sum]))
    sums.step()
    for _ in range(net.bits):
        scatter_kv.step()
        sums.step()
        scatter_qo.step()
        scatter_a.step()
        scatter_b.step()
    kv_grad = scatter_kv.result()
    sums = sums.result().reshape(3, model)
    q_grad, o_grad = scatter_qo.result()
    grads = [s.result().reshape(3, chunk_rows, width) for s in (scatter_a, scatter_b)]
    gate_grad, up_grad, down_grad = jnp.concatenate(grads, axis=1)
    return (
        join(hidden4),
        join(grad_in4),
        sums[0],
        sums[1],
        sums[2],
        q_grad.T,
        kv_grad[0].T,
        kv_grad[1].T,
        o_grad,
        gate_grad.T,
        up_grad.T,
        down_grad,
    )


def solution(mesh):
    tokens = P("dp", "fsdp")
    inner_first = P("fsdp", "dp")
    return jax.shard_map(
        shards,
        mesh=mesh,
        in_specs=(P("dp", "fsdp", None),) + (tokens,) * 3 + (P(),) * 3
        + (tokens,) * 3 + (inner_first,) + (tokens,) * 2 + (inner_first, P("dp", "fsdp", None)),
        out_specs=(P("dp", "fsdp", None),) * 2 + (P(),) * 3
        + (tokens,) * 3 + (inner_first,) + (tokens,) * 2 + (inner_first,),
        check_vma=False,
    )
```

time: 683 us -> 556 us (0.81)
  starting transfers between devices: 227 us -> 103 us
  blocking collectives: 38.9 us -> 0 us
  Pallas kernels: 148 us -> 184 us
  other arithmetic: 71.6 us -> 53.6 us
  waiting for transfers between devices: 131 us -> 144 us
  local copies, waits for them, and re-layouts: 40.4 us -> 48.1 us
    ppermute x46 -> x42, starting transfers between devices: 227 us -> 102 us  [the longest x30 86.1 us: swap(): lax.ppermute(self.clock.at(array), AXES, [(i, i ^ flip) for i in range(se...]
    psum x1 -> x0, blocking collectives: 38.9 us -> none  [shards(): lax.psum(jnp.stack([gain_one_sum, gain_two_sum, router_sum]), AXES)]
    pallas_call x5, Pallas kernels: 57.2 us -> 85.1 us  [the longest x1 37.5 us: attention_backward(): pl.pallas_call(functools.partial(backward_kernel, slots), grid_spec=pltpu...]
    all_gather x1 -> x2, waiting for transfers between devices: 0.01 us -> 22.1 us  [the longest x1 22.1 us: shards(): lax.all_gather(clock.after(large[1]), AXES, axis=0, tiled=False)]
    ppermute x46 -> x42, waiting for transfers between devices: 131 us -> 121 us  [the longest x30 85.8 us: swap(): lax.ppermute(self.clock.at(array), AXES, [(i, i ^ flip) for i in range(se...]
    pallas_call x2, Pallas kernels: 54.4 us -> 62.5 us  [ffn(): pl.pallas_call(ffn_kernel, grid_spec=pltpu.PrefetchScalarGridSpec(num_sca...]
    convert_element_type x24 -> x18, other arithmetic: 34.9 us -> 27.1 us  [add(): return (mine.astype(F32) + other.astype(F32)).astype(dtype)]
    unnamed x90 -> x83, local copies, waits for them, and re-layouts: 15.9 us -> 15.1 us
  transfers between devices with their start and end apart: 47 -> 44, of which waited for: 14 -> 17; matrix products, arithmetic and copies ran while one was open for 16% -> 16% of each run, Pallas kernels for 14% -> 34%
where the time goes in v2:
time: 556 us; the launch traced here: 547 us
  Pallas kernels  184 us (33%)
  waiting for transfers between devices  144 us (26%)
  starting transfers between devices  103 us (19%)
  other arithmetic  53.6 us (10%)
  local copies, waits for them, and re-layouts  48.1 us (9%)
  between operations  15.3 us (3%)
    ppermute x30, starting transfers between devices, swap(): lax.ppermute(self.clock.at(array), AXES, [(i, i ^ flip) for i in range(se...  86.1 us
    ppermute x30, waiting for transfers between devices, swap(): lax.ppermute(self.clock.at(array), AXES, [(i, i ^ flip) for i in range(se...  85.8 us
    pallas_call x2, Pallas kernels, ffn(): pl.pallas_call(ffn_kernel, grid_spec=pltpu.PrefetchScalarGridSpec(num_sca...  62.5 us
    pallas_call x1, Pallas kernels, attention_backward(): pl.pallas_call(functools.partial(backward_kernel, slots), grid_spec=pltpu...  37.5 us
    ppermute x12, waiting for transfers between devices, move(): return lax.ppermute(self.clock.at(array), AXES, pairs)  35.6 us
    convert_element_type x18, other arithmetic, add(): return (mine.astype(F32) + other.astype(F32)).astype(dtype)  27.1 us
    all_gather x1, waiting for transfers between devices, shards(): lax.all_gather(clock.after(large[1]), AXES, axis=0, tiled=False)  22.1 us
    pallas_call x1, Pallas kernels, attention_forward(): pl.pallas_call(functools.partial(forward_kernel, slots), grid_spec=pltpu....  20.8 us
  transfers between devices with their start and end apart: 44, of which 17 were waited for; matrix products, arithmetic and copies ran while one was open for 16% of the time, Pallas kernels for 34%

profile of v2, /device:TPU:0, one launch (start us, length us, event | category | flops | bytes accessed | tf_op | source)
XLA Modules:
  0.0 547.4 jit_solution(4869388199155783048)
XLA Ops:
  9.0 4.1 collective-permute-start
  13.1 5.1 collective-permute-done
  20.8 4.6 collective-permute-done.1
  36.2 4.5 first_norm.1
  43.5 19.0 %collective-permute-done.3 = bf16[2,2,2,200,240]{4,3,0,1,2:T(8,128)(2,1)S(1)} collective-permute-done((bf16[2,2,2,200,240]{4,3,0,1,2:T(8,128)(2,1)S(1)}, bf16[2,2,2,200,240]{4,3,0,1,2:T(8,128)(2,1)S(1)}, u32[]{:S(2)}, u32[]{:S(2)}) %collective-permute-start.3) | collective-permute-done | bytes 768032 | tf_op jit(solution)/shard_map/ppermute | solution.py:723
  72.0 4.1 kv_project.1.refs_0_
  76.1 4.7 collective-permute-start.5
  83.3 8.0 %q_project.1.q_ref = bf16[512,1920]{1,0:T(8,128)(2,1)} custom-call(bf16[4,512,240]{2,1,0:T(8,128)(2,1)} %get-tuple-element.217.xn_ref, bf16[4,1920,240]{2,1,0:T(8,128)(2,1)} %bitcast.179, f32[512,128]{1,0:T(8,128)} %get-tuple-element.484.cos_ref, f32[512,128]{1,0:T(8,128)} %get-tuple-element.481.sin_ref), custom_call_target="tpu_custom_call" | custom-call | flops 1887436800 | bytes 5898240 | tf_op jit(solution)/shard_map/q_project/pallas_call | solution.py:146
  91.3 14.4 %collective-permute-done.5 = bf16[2,272,640]{2,1,0:T(8,128)(2,1)S(1)} collective-permute-done((bf16[2,272,640]{2,1,0:T(8,128)(2,1)}, bf16[2,272,640]{2,1,0:T(8,128)(2,1)S(1)}, u32[]{:S(2)}, u32[]{:S(2)}) %collective-permute-start.5) | collective-permute-done | bytes 696352 | tf_op jit(solution)/shard_map/ppermute | solution.py:833
  108.8 21.2 %collective-permute-done.7.refs_1_ = bf16[2,272,640]{2,1,0:T(8,128)(2,1)S(1)} collective-permute-done((bf16[2,272,640]{2,1,0:T(8,128)(2,1)S(1)}, bf16[2,272,640]{2,1,0:T(8,128)(2,1)S(1)}, u32[]{:S(2)}, u32[]{:S(2)}) %collective-permute-start.7) | collective-permute-done | bytes 696352 | tf_op jit(solution)/shard_map/ppermute | solution.py:833
  137.8 20.8 %attention_forward.1 = (bf16[512,1920]{1,0:T(8,128)(2,1)}, f32[2,5,1,768]{3,2,1,0:T(1,128)}) custom-call(s32[6]{0:T(128)} %stack.100.slot_ref, bf16[512,1920]{1,0:T(8,128)(2,1)} %q_project.1.q_ref, f32[2,1,256]{2,1,0:T(1,128)} %reshape.347.seg_ref, bf16[2,272,640]{2,1,0:T(8,128)(2,1)} %kv_project.1.refs_0_, bf16[2,272,640]{2,1,0:T(8,128)(2,1)} %copy-done.33, ...), custom_call_target="tpu_custom_call" | custom-call | flops 6039797760 | bytes 7864320 | tf_op jit(solution)/shard_map/attention_forward/pallas_call | solution.py:259
  162.9 7.3 %out_project.1 = (f32[4,512,240]{2,1,0:T(8,128)}, bf16[4,512,240]{2,1,0:T(8,128)(2,1)}, f32[512,1]{1,0:T(8,128)}) custom-call(bf16[512,1920]{1,0:T(8,128)(2,1)} %get-tuple-element.255.o_ref, bf16[4,1920,240]{2,1,0:T(8,128)(2,1)} %bitcast.189, bf16[4,512,240]{2,1,0:T(8,128)(2,1)} %bitcast.176, f32[4,1,240]{2,1,0:T(1,128)} %reshape.370.gain_ref), custom_call_target="tpu_custom_call" | custom-call | flops 1887436800 | bytes 7864320 | tf_op jit(solution)/shard_map/out_project/pallas_call | solution.py:371
  170.2 27.1 %ffn.2 = (f32[4,512,240]{2,1,0:T(8,128)}, f32[4,512,240]{2,1,0:T(8,128)}, bf16[2,2,4,480,240]{4,3,2,1,0:T(8,128)(2,1)}, bf16[2,2,4,480,240]{4,3,2,1,0:T(8,128)(2,1)}) custom-call(s32[3]{0:T(128)} %pad_add_fusion.meta_ref, bf16[4,512,240]{2,1,0:T(8,128)(2,1)} %get-tuple-element.260.x_ref, bf16[4,512,240]{2,1,0:T(8,128)(2,1)} %get-tuple-element.261.fg_ref, ...), custom_call_target="tpu_custom_call" | custom-call | flops 11324620800 | bytes 22609920 | tf_op jit(solution)/shard_map/ffn/pallas_call | solution.py:461
  197.3 22.1 %all-gather.7.cloned.1.call-done = bf16[15360,240]{1,0:T(8,128)(2,1)} async-done(((bf16[480,240]{1,0:T(8,128)(2,1)}), bf16[15360,240]{1,0:T(8,128)(2,1)}) %all-gather.7.cloned.1.call-update) | async-done | bytes 7372816 | tf_op jit(solution)/shard_map/all_gather | solution.py:994
  219.4 35.4 %ffn.3 = (f32[4,512,240]{2,1,0:T(8,128)}, f32[4,512,240]{2,1,0:T(8,128)}, bf16[2,2,4,480,240]{4,3,2,1,0:T(8,128)(2,1)}, bf16[2,2,4,480,240]{4,3,2,1,0:T(8,128)(2,1)}) custom-call(s32[3]{0:T(128)} %pad_add_fusion.meta_ref, bf16[4,512,240]{2,1,0:T(8,128)(2,1)} %get-tuple-element.260.x_ref, bf16[4,512,240]{2,1,0:T(8,128)(2,1)} %get-tuple-element.261.fg_ref, ...), custom_call_target="tpu_custom_call" | custom-call | flops 11324620800 | bytes 22609920 | tf_op jit(solution)/shard_map/ffn/pallas_call | solution.py:461
  259.3 4.7 fusion
  264.1 8.3 %middle_step.1 = (bf16[4,512,240]{2,1,0:T(8,128)(2,1)}, f32[4,512,240]{2,1,0:T(8,128)}, bf16[4,512,240]{2,1,0:T(8,128)(2,1)}, f32[4,1,240]{2,1,0:T(1,128)}, f32[4,1,240]{2,1,0:T(1,128)}) custom-call(f32[4,512,240]{2,1,0:T(8,128)} %get-tuple-element.257.mid_ref, bf16[4,512,240]{2,1,0:T(8,128)(2,1)} %bitcast.177, bf16[4,512,240]{2,1,0:T(8,128)(2,1)} %bitcast.186, ...), custom_call_target="tpu_custom_call" | custom-call | flops 14745600 | bytes 17694720 | tf_op jit(solution)/shard_map/middle_step/pallas_call | solution.py:524
  272.4 5.9 %fusion.1 = (bf16[8,480,240]{2,1,0:T(8,128)(2,1)S(1)}, bf16[8,480,240]{2,1,0:T(8,128)(2,1)}) fusion(bf16[1,2,4,480,240]{4,3,2,1,0:T(8,128)(2,1)} %get-tuple-element.441, bf16[16,480,240]{2,1,0:T(8,128)(2,1)} %bitcast.46, bf16[1,2,4,480,240]{4,3,2,1,0:T(8,128)(2,1)} %get-tuple-element.442), kind=kLoop, calls=%fused_computation.4 | loop fusion | flops 7372800 | bytes 11059200 | tf_op jit(solution)/shard_map/convert_element_type | solution.py:708
  280.4 7.6 %out_back.1.do_ref = bf16[512,1920]{1,0:T(8,128)(2,1)} custom-call(bf16[4,512,240]{2,1,0:T(8,128)(2,1)} %get-tuple-element.284.ag_ref, bf16[4,1920,240]{2,1,0:T(8,128)(2,1)} %bitcast.190), custom_call_target="tpu_custom_call" | custom-call | flops 1887436800 | bytes 5898240 | tf_op jit(solution)/shard_map/out_back/pallas_call | solution.py:561
  288.0 37.5 %attention_backward.1 = (bf16[512,1920]{1,0:T(8,128)(2,1)}, bf16[2,256,640]{2,1,0:T(8,128)(2,1)}, bf16[2,256,640]{2,1,0:T(8,128)(2,1)}, bf16[2,256,640]{2,1,0:T(...) custom-call(s32[6]{0:T(128)} %stack.100.slot_ref, ...), custom_call_target="tpu_custom_call" | custom-call | flops 15099494400 | bytes 15728640 | tf_op jit(solution)/shard_map/attention_backward/pallas_call | solution.py:331
  327.0 10.4 %qo_back.1 = (bf16[2,2,960,240]{3,2,1,0:T(8,128)(2,1)}, bf16[2,2,960,240]{3,2,1,0:T(8,128)(2,1)}, f32[4,512,240]{2,1,0:T(8,128)}) custom-call(s32[1]{0:T(128)} %bitcast.37.meta_ref, bf16[512,1920]{1,0:T(8,128)(2,1)} %get-tuple-element.295.dq_ref, bf16[4,512,240]{2,1,0:T(8,128)(2,1)} %get-tuple-element.217.xn_ref, bf16[4,1920,240]{2,1,0:T(8,128)(2,1)} %bitcast.180, ...), custom_call_target="tpu_custom_call" | custom-call | flops 3774873600 | bytes 13762560 | tf_op jit(solution)/shard_map/qo_back/pallas_call | solution.py:588
  337.4 3.4 add_convert_fusion.1
  354.9 19.0 %collective-permute-done.25 = bf16[4,480,240]{2,1,0:T(8,128)(2,1)S(1)} collective-permute-done((bf16[4,480,240]{2,1,0:T(8,128)(2,1)}, bf16[4,480,240]{2,1,0:T(8,128)(2,1)S(1)}, u32[]{:S(2)}, u32[]{:S(2)}) %collective-permute-start.25) | collective-permute-done | bytes 921632 | tf_op jit(solution)/shard_map/ppermute | solution.py:723
  375.0 24.8 %collective-permute-start.31 = (bf16[2,480,240]{2,1,0:T(8,128)(2,1)}, bf16[2,480,240]{2,1,0:T(8,128)(2,1)}, u32[]{:S(2)}, u32[]{:S(2)}) collective-permute-start(bf16[2,480,240]{2,1,0:T(8,128)(2,1)} %get-tuple-element.385), channel_id=1, source_target_pairs={{0,2},{1,3},{2,0},{3,1},{4,6},{5,7},{6,4},{7,5},{8,10},{9,11},{10,... | collective-permute-start | bytes 1382408 | tf_op jit(solution)/shard_map/ppermute | solution.py:723
  411.3 34.8 %collective-permute-start.40 = (bf16[1,480,240]{2,1,0:T(8,128)(2,1)S(1)}, bf16[1,480,240]{2,1,0:T(8,128)(2,1)S(1)}, u32[]{:S(2)}, u32[]{:S(2)}) collective-permute-start(bf16[1,480,240]{2,1,0:T(8,128)(2,1)S(1)} %add_convert_fusion.13), channel_id=1, source_target_pairs={{0,4},{1,5},{2,6},{3,7},{4,0},{5,1},{6,2},{7,3},{8,12},{9,13},{10,... | collective-permute-start | bytes 691208 | tf_op jit(solution)/shard_map/ppermute | solution.py:723
  452.8 10.2 %collective-permute-done.40 = bf16[1,480,240]{2,1,0:T(8,128)(2,1)S(1)} collective-permute-done((bf16[1,480,240]{2,1,0:T(8,128)(2,1)S(1)}, bf16[1,480,240]{2,1,0:T(8,128)(2,1)S(1)}, u32[]{:S(2)}, u32[]{:S(2)}) %collective-permute-start.40) | collective-permute-done | bytes 230432 | tf_op jit(solution)/shard_map/ppermute | solution.py:723
  465.3 4.3 kv_back.1
  471.7 8.8 %final_step.1 = (f32[4,512,240]{2,1,0:T(8,128)}, f32[4,1,240]{2,1,0:T(1,128)}) custom-call(f32[4,512,240]{2,1,0:T(8,128)} %get-tuple-element.308.xg_ref, bf16[512,640]{1,0:T(8,128)(2,1)} %get-tuple-element.350.kvb_ref, bf16[4,640,240]{2,1,0:T(8,128)(2,1)} %bitcast.184, bf16[4,512,240]{2,1,0:T(8,128)(2,1)} %bitcast.178, ...), custom_call_target="tpu_custom_call" | custom-call | flops 629145600 | bytes 9830400 | tf_op jit(solution)/shard_map/final_step/pallas_call | solution.py:671
  507.0 7.3 %collective-permute-done.32 = bf16[2,4,120,240]{3,2,0,1:T(8,128)(2,1)S(1)} collective-permute-done((bf16[2,4,120,240]{3,2,0,1:T(8,128)(2,1)S(1)}, bf16[2,4,120,240]{3,2,0,1:T(8,128)(2,1)S(1)}, u32[]{:S(2)}, u32[]{:S(2)}) %collective-permute-start.32) | collective-permute-done | bytes 460832 | tf_op jit(solution)/shard_map/ppermute | solution.py:723
  520.8 3.7 collective-permute-start.37
  524.7 3.4 collective-permute-done.37
  530.1 4.4 collective-permute-done.38
  (255 shorter events, 130.9 us)
Async XLA Ops:
  7.2 151.4 %all-gather.5.cloned.1.call-start = ((), (), s32[]{:S(2)}) async-start(), calls=%async_computation | async-start | bytes 10137600 | tf_op jit(solution)/shard_map/all_gather | solution.py:982
  9.0 9.2 %collective-permute-start = (bf16[200,240]{1,0:T(8,128)(2,1)S(1)}, bf16[200,240]{1,0:T(8,128)(2,1)S(1)}, u32[]{:S(2)}, u32[]{:S(2)}) collective-permute-start(bf16[200,240]{1,0:T(8,128)(2,1)S(1)} %pad_maximum_fusion.11), channel_id=1, source_target_pairs={{0,4},{1,5},{2,6},{3,7},{4,0},{5,1},{6,2},{7,3},{8,12},{9,13},{10,... | collective-permute-start | bytes 288008 | tf_op jit(solution)/shard_map/ppermute | solution.py:723
  19.1 6.3 %collective-permute-start.1 = (bf16[2,200,240]{2,1,0:T(8,128)(2,1)S(1)}, bf16[2,200,240]{2,1,0:T(8,128)(2,1)S(1)}, u32[]{:S(2)}, u32[]{:S(2)}) collective-permute-start(bf16[2,200,240]{2,1,0:T(8,128)(2,1)S(1)} %pad_maximum_fusion.10), channel_id=1, source_target_pairs={{0,2},{1,3},{2,0},{3,1},{4,6},{5,7},{6,4},{7,5},{8,10},{9,11},{10,... | collective-permute-start | bytes 576008 | tf_op jit(solution)/shard_map/ppermute | solution.py:723
  25.5 16.1 %collective-permute-start.2 = (bf16[2,2,200,240]{3,2,0,1:T(8,128)(2,1)S(1)}, bf16[2,2,200,240]{3,2,0,1:T(8,128)(2,1)S(1)}, u32[]{:S(2)}, u32[]{:S(2)}) collective-permute-start(bf16[2,2,200,240]{3,2,0,1:T(8,128)(2,1)S(1)} %pad_maximum_fusion.5), channel_id=1, source_target_pairs={{0,1},{1,0},{2,3},{3,2},{4,5},{5,4},{6,7},{7,6},{8,9},{9,8},{10,11... | collective-permute-start | bytes 1152008 | tf_op jit(solution)/shard_map/ppermute | solution.py:723
  41.9 177.6 %all-gather.7.cloned.1.call-start = ((), (), s32[]{:S(2)}) async-start(), calls=%async_computation.1 | async-start | bytes 8110080 | tf_op jit(solution)/shard_map/all_gather | solution.py:994
  41.9 20.6 %collective-permute-start.3 = (bf16[2,2,2,200,240]{4,3,0,1,2:T(8,128)(2,1)S(1)}, bf16[2,2,2,200,240]{4,3,0,1,2:T(8,128)(2,1)S(1)}, u32[]{:S(2)}, u32[]{:S(2)}) collective-permute-start(bf16[2,2,2,200,240]{4,3,0,1,2:T(8,128)(2,1)S(1)} %pad_maximum_fusion.4), channel_id=1, source_target_pairs={{0,16},{1,17},{2,18},{3,19},{4,20},{5,21},{6,22},{7,23},{8,24},{9,... | collective-permute-start | bytes 2304008 | tf_op jit(solution)/shard_map/ppermute | solution.py:723
  76.1 29.6 %collective-permute-start.5 = (bf16[2,272,640]{2,1,0:T(8,128)(2,1)}, bf16[2,272,640]{2,1,0:T(8,128)(2,1)S(1)}, u32[]{:S(2)}, u32[]{:S(2)}) collective-permute-start(bf16[2,272,640]{2,1,0:T(8,128)(2,1)} %kv_project.1.refs_0_), channel_id=1, source_target_pairs={{0,2},{1,3},{2,4},{3,5},{4,6},{5,7},{8,10},{9,11},{10,12},{11,13},... | collective-permute-start | bytes 2088968 | tf_op jit(solution)/shard_map/ppermute | solution.py:833
  105.8 24.2 %collective-permute-start.7 = (bf16[2,272,640]{2,1,0:T(8,128)(2,1)S(1)}, bf16[2,272,640]{2,1,0:T(8,128)(2,1)S(1)}, u32[]{:S(2)}, u32[]{:S(2)}) collective-permute-start(bf16[2,272,640]{2,1,0:T(8,128)(2,1)S(1)} %broadcast_select_fusion.3), channel_id=1, source_target_pairs={{0,1},{2,3},{4,5},{6,7},{7,6},{8,9},{10,11},{12,13},{14,15},{15,14... | collective-permute-start | bytes 2088968 | tf_op jit(solution)/shard_map/ppermute | solution.py:833
  108.1 21.9 %collective-permute-start.6 = (bf16[2,272,640]{2,1,0:T(8,128)(2,1)S(1)}, bf16[2,272,640]{2,1,0:T(8,128)(2,1)S(1)}, u32[]{:S(2)}, u32[]{:S(2)}) collective-permute-start(bf16[2,272,640]{2,1,0:T(8,128)(2,1)S(1)} %collective-permute-done.5), channel_id=1, source_target_pairs={{2,4},{3,5},{4,6},{5,7},{10,12},{11,13},{12,14},{13,15},{18,20},{1... | collective-permute-start | bytes 2088968 | tf_op jit(solution)/shard_map/ppermute | solution.py:833
  197.3 62.0 %collective-permute-start.11 = (bf16[2,2,4,480,240]{4,3,2,1,0:T(8,128)(2,1)}, bf16[2,2,4,480,240]{4,3,2,1,0:T(8,128)(2,1)}, u32[]{:S(2)}, u32[]{:S(2)}) collective-permute-start(bf16[2,2,4,480,240]{4,3,2,1,0:T(8,128)(2,1)} %get-tuple-element.268), channel_id=1, source_target_pairs={{0,8},{1,9},{2,10},{3,11},{4,12},{5,13},{6,14},{7,15},{8,0},{9,1},... | collective-permute-start | bytes 11059208 | tf_op jit(solution)/shard_map/ppermute | solution.py:723
  254.8 17.6 %collective-permute-start.12 = (bf16[2,2,4,480,240]{4,3,2,1,0:T(8,128)(2,1)}, bf16[2,2,4,480,240]{4,3,2,1,0:T(8,128)(2,1)}, u32[]{:S(2)}, u32[]{:S(2)}) collective-permute-start(bf16[2,2,4,480,240]{4,3,2,1,0:T(8,128)(2,1)} %get-tuple-element.286), channel_id=1, source_target_pairs={{0,8},{1,9},{2,10},{3,11},{4,12},{5,13},{6,14},{7,15},{8,0},{9,1},... | collective-permute-start | bytes 11059208 | tf_op jit(solution)/shard_map/ppermute | solution.py:723
  278.3 47.1 %collective-permute-start.13 = (bf16[8,480,240]{2,1,0:T(8,128)(2,1)}, bf16[8,480,240]{2,1,0:T(8,128)(2,1)}, u32[]{:S(2)}, u32[]{:S(2)}) collective-permute-start(bf16[8,480,240]{2,1,0:T(8,128)(2,1)} %get-tuple-element.297), channel_id=1, source_target_pairs={{0,1},{1,0},{2,3},{3,2},{4,5},{5,4},{6,7},{7,6},{8,9},{9,8},{10,11... | collective-permute-start | bytes 5529608 | tf_op jit(solution)/shard_map/ppermute | solution.py:723
  279.8 45.7 %collective-permute-start.14 = (bf16[8,480,240]{2,1,0:T(8,128)(2,1)}, bf16[8,480,240]{2,1,0:T(8,128)(2,1)}, u32[]{:S(2)}, u32[]{:S(2)}) collective-permute-start(bf16[8,480,240]{2,1,0:T(8,128)(2,1)} %get-tuple-element.302), channel_id=1, source_target_pairs={{0,16},{1,17},{2,18},{3,19},{4,20},{5,21},{6,22},{7,23},{8,24},{9,... | collective-permute-start | bytes 5529608 | tf_op jit(solution)/shard_map/ppermute | solution.py:723
  325.5 16.1 %collective-permute-start.15 = (bf16[2,256,640]{2,1,0:T(8,128)(2,1)}, bf16[2,256,640]{2,1,0:T(8,128)(2,1)}, u32[]{:S(2)}, u32[]{:S(2)}) collective-permute-start(bf16[2,256,640]{2,1,0:T(8,128)(2,1)} %get-tuple-element.312), channel_id=1, source_target_pairs={{5,4},{4,5},{7,6},{6,7},{13,12},{12,13},{15,14},{14,15},{21,20},{2... | collective-permute-start | bytes 1966088 | tf_op jit(solution)/shard_map/ppermute | solution.py:833
  343.8 55.9 %collective-permute-start.20 = (bf16[2,2,960,240]{3,2,1,0:T(8,128)(2,1)}, bf16[2,2,960,240]{3,2,1,0:T(8,128)(2,1)}, u32[]{:S(2)}, u32[]{:S(2)}) collective-permute-start(bf16[2,2,960,240]{3,2,1,0:T(8,128)(2,1)} %get-tuple-element.329), channel_id=1, source_target_pairs={{0,8},{1,9},{2,10},{3,11},{4,12},{5,13},{6,14},{7,15},{8,0},{9,1},... | collective-permute-start | bytes 5529608 | tf_op jit(solution)/shard_map/ppermute | solution.py:723
  349.2 24.8 %collective-permute-start.25 = (bf16[4,480,240]{2,1,0:T(8,128)(2,1)}, bf16[4,480,240]{2,1,0:T(8,128)(2,1)S(1)}, u32[]{:S(2)}, u32[]{:S(2)}) collective-permute-start(bf16[4,480,240]{2,1,0:T(8,128)(2,1)} %get-tuple-element.359), channel_id=1, source_target_pairs={{0,1},{1,0},{2,3},{3,2},{4,5},{5,4},{6,7},{7,6},{8,9},{9,8},{10,11... | collective-permute-start | bytes 2764808 | tf_op jit(solution)/shard_map/ppermute | solution.py:723
  350.6 52.2 %collective-permute-start.16 = (bf16[2,256,640]{2,1,0:T(8,128)(2,1)}, bf16[2,256,640]{2,1,0:T(8,128)(2,1)S(1)}, u32[]{:S(2)}, u32[]{:S(2)}) collective-permute-start(bf16[2,256,640]{2,1,0:T(8,128)(2,1)} %get-tuple-element.317), channel_id=1, source_target_pairs={{1,0},{3,2},{5,4},{7,6},{6,7},{9,8},{11,10},{13,12},{15,14},{14,15... | collective-permute-start | bytes 1966088 | tf_op jit(solution)/shard_map/ppermute | solution.py:833
  351.9 51.0 %collective-permute-start.19 = (bf16[2,256,640]{2,1,0:T(8,128)(2,1)}, bf16[2,256,640]{2,1,0:T(8,128)(2,1)S(1)}, u32[]{:S(2)}, u32[]{:S(2)}) collective-permute-start(bf16[2,256,640]{2,1,0:T(8,128)(2,1)} %fusion.8), channel_id=1, source_target_pairs={{4,2},{5,3},{6,4},{7,5},{12,10},{13,11},{14,12},{15,13},{20,18},{2... | collective-permute-start | bytes 1966088 | tf_op jit(solution)/shard_map/ppermute | solution.py:833
  354.2 56.1 %collective-permute-start.22 = (bf16[4,480,240]{2,1,0:T(8,128)(2,1)}, bf16[4,480,240]{2,1,0:T(8,128)(2,1)}, u32[]{:S(2)}, u32[]{:S(2)}) collective-permute-start(bf16[4,480,240]{2,1,0:T(8,128)(2,1)} %get-tuple-element.340), channel_id=1, source_target_pairs={{0,16},{1,17},{2,18},{3,19},{4,20},{5,21},{6,22},{7,23},{8,24},{9,... | collective-permute-start | bytes 2764808 | tf_op jit(solution)/shard_map/ppermute | solution.py:723
  375.0 35.3 %collective-permute-start.31 = (bf16[2,480,240]{2,1,0:T(8,128)(2,1)}, bf16[2,480,240]{2,1,0:T(8,128)(2,1)}, u32[]{:S(2)}, u32[]{:S(2)}) collective-permute-start(bf16[2,480,240]{2,1,0:T(8,128)(2,1)} %get-tuple-element.385), channel_id=1, source_target_pairs={{0,2},{1,3},{2,0},{3,1},{4,6},{5,7},{6,4},{7,5},{8,10},{9,11},{10,... | collective-permute-start | bytes 1382408 | tf_op jit(solution)/shard_map/ppermute | solution.py:723
  404.1 58.9 %collective-permute-start.21 = (bf16[2,256,640]{2,1,0:T(8,128)(2,1)}, bf16[2,256,640]{2,1,0:T(8,128)(2,1)}, u32[]{:S(2)}, u32[]{:S(2)}) collective-permute-start(bf16[2,256,640]{2,1,0:T(8,128)(2,1)} %fusion.11), channel_id=1, source_target_pairs={{2,0},{3,1},{4,2},{5,3},{6,4},{7,5},{10,8},{11,9},{12,10},{13,11},... | collective-permute-start | bytes 1966088 | tf_op jit(solution)/shard_map/ppermute | solution.py:833
  411.3 51.7 %collective-permute-start.40 = (bf16[1,480,240]{2,1,0:T(8,128)(2,1)S(1)}, bf16[1,480,240]{2,1,0:T(8,128)(2,1)S(1)}, u32[]{:S(2)}, u32[]{:S(2)}) collective-permute-start(bf16[1,480,240]{2,1,0:T(8,128)(2,1)S(1)} %add_convert_fusion.13), channel_id=1, source_target_pairs={{0,4},{1,5},{2,6},{3,7},{4,0},{5,1},{6,2},{7,3},{8,12},{9,13},{10,... | collective-permute-start | bytes 691208 | tf_op jit(solution)/shard_map/ppermute | solution.py:723
  448.4 34.8 %collective-permute-start.23 = (bf16[2,480,240]{2,1,0:T(8,128)(2,1)}, bf16[2,480,240]{2,1,0:T(8,128)(2,1)S(1)}, u32[]{:S(2)}, u32[]{:S(2)}) collective-permute-start(bf16[2,480,240]{2,1,0:T(8,128)(2,1)} %get-tuple-element.357), channel_id=1, source_target_pairs={{0,2},{1,3},{2,0},{3,1},{4,6},{5,7},{6,4},{7,5},{8,10},{9,11},{10,... | collective-permute-start | bytes 1382408 | tf_op jit(solution)/shard_map/ppermute | solution.py:723
  451.3 49.3 %collective-permute-start.24 = (bf16[1,2,8,120,240]{4,3,2,1,0:T(8,128)(2,1)}, bf16[1,2,8,120,240]{4,3,2,1,0:T(8,128)(2,1)}, u32[]{:S(2)}, u32[]{:S(2)}) collective-permute-start(bf16[1,2,8,120,240]{4,3,2,1,0:T(8,128)(2,1)} %get-tuple-element.358), channel_id=1, source_target_pairs={{0,16},{1,17},{2,18},{3,19},{4,20},{5,21},{6,22},{7,23},{8,24},{9,... | collective-permute-start | bytes 2764808 | tf_op jit(solution)/shard_map/ppermute | solution.py:723
  485.4 14.2 %collective-permute-start.41 = (bf16[1,480,240]{2,1,0:T(8,128)(2,1)}, bf16[1,480,240]{2,1,0:T(8,128)(2,1)S(1)}, u32[]{:S(2)}, u32[]{:S(2)}) collective-permute-start(bf16[1,480,240]{2,1,0:T(8,128)(2,1)} %add_convert_fusion.15), channel_id=1, source_target_pairs={{0,4},{1,5},{2,6},{3,7},{4,0},{5,1},{6,2},{7,3},{8,12},{9,13},{10,... | collective-permute-start | bytes 691208 | tf_op jit(solution)/shard_map/ppermute | solution.py:723
  485.4 18.8 %collective-permute-start.26 = (bf16[2,2,5,64,240]{4,3,2,1,0:T(8,128)(2,1)}, bf16[2,2,5,64,240]{4,3,2,1,0:T(8,128)(2,1)}, u32[]{:S(2)}, u32[]{:S(2)}) collective-permute-start(bf16[2,2,5,64,240]{4,3,2,1,0:T(8,128)(2,1)} %bitcast.172), channel_id=1, source_target_pairs={{0,8},{1,9},{2,10},{3,11},{4,12},{5,13},{6,14},{7,15},{8,0},{9,1},... | collective-permute-start | bytes 1843208 | tf_op jit(solution)/shard_map/ppermute | solution.py:723
  487.7 8.3 %collective-permute-start.33 = (f32[3,4,1,240]{3,2,1,0:T(1,128)S(1)}, f32[3,4,1,240]{3,2,1,0:T(1,128)S(1)}, u32[]{:S(2)}, u32[]{:S(2)}) collective-permute-start(f32[3,4,1,240]{3,2,1,0:T(1,128)S(1)} %fusion.45), channel_id=1, source_target_pairs={{0,1},{1,0},{2,3},{3,2},{4,5},{5,4},{6,7},{7,6},{8,9},{9,8},{10,11... | collective-permute-start | bytes 34568 | tf_op jit(solution)/shard_map/ppermute | solution.py:723
  499.9 16.2 %collective-permute-start.35 = (f32[3,4,1,240]{3,2,1,0:T(1,128)S(1)}, f32[3,4,1,240]{3,2,1,0:T(1,128)S(1)}, u32[]{:S(2)}, u32[]{:S(2)}) collective-permute-start(f32[3,4,1,240]{3,2,1,0:T(1,128)S(1)} %add.274), channel_id=1, source_target_pairs={{0,4},{1,5},{2,6},{3,7},{4,0},{5,1},{6,2},{7,3},{8,12},{9,13},{10,... | collective-permute-start | bytes 34568 | tf_op jit(solution)/shard_map/ppermute | solution.py:723
  502.0 12.3 %collective-permute-start.32 = (bf16[2,4,120,240]{3,2,0,1:T(8,128)(2,1)S(1)}, bf16[2,4,120,240]{3,2,0,1:T(8,128)(2,1)S(1)}, u32[]{:S(2)}, u32[]{:S(2)}) collective-permute-start(bf16[2,4,120,240]{3,2,0,1:T(8,128)(2,1)S(1)} %fusion.17), channel_id=1, source_target_pairs={{0,1},{1,0},{2,3},{3,2},{4,5},{5,4},{6,7},{7,6},{8,9},{9,8},{10,11... | collective-permute-start | bytes 1382408 | tf_op jit(solution)/shard_map/ppermute | solution.py:723
  505.5 12.6 %collective-permute-start.28 = (bf16[1,2,8,40,240]{4,3,2,1,0:T(8,128)(2,1)S(1)}, bf16[1,2,8,40,240]{4,3,2,1,0:T(8,128)(2,1)S(1)}, u32[]{:S(2)}, u32[]{:S(2)}) collective-permute-start(bf16[1,2,8,40,240]{4,3,2,1,0:T(8,128)(2,1)S(1)} %get-tuple-element.376), channel_id=1, source_target_pairs={{0,16},{1,17},{2,18},{3,19},{4,20},{5,21},{6,22},{7,23},{8,24},{9,... | collective-permute-start | bytes 921608 | tf_op jit(solution)/shard_map/ppermute | solution.py:723
  514.5 6.3 %collective-permute-start.36 = (bf16[2,2,120,240]{3,2,1,0:T(8,128)(2,1)S(1)}, bf16[2,2,120,240]{3,2,1,0:T(8,128)(2,1)S(1)}, u32[]{:S(2)}, u32[]{:S(2)}) collective-permute-start(bf16[2,2,120,240]{3,2,1,0:T(8,128)(2,1)S(1)} %copy.55), channel_id=1, source_target_pairs={{0,2},{1,3},{2,0},{3,1},{4,6},{5,7},{6,4},{7,5},{8,10},{9,11},{10,... | collective-permute-start | bytes 691208 | tf_op jit(solution)/shard_map/ppermute | solution.py:723
  520.8 7.3 %collective-permute-start.37 = (bf16[2,1,120,240]{3,2,1,0:T(8,128)(2,1)S(1)}, bf16[2,1,120,240]{3,2,1,0:T(8,128)(2,1)S(1)}, u32[]{:S(2)}, u32[]{:S(2)}) collective-permute-start(bf16[2,1,120,240]{3,2,1,0:T(8,128)(2,1)S(1)} %fusion.24), channel_id=1, source_target_pairs={{0,4},{1,5},{2,6},{3,7},{4,0},{5,1},{6,2},{7,3},{8,12},{9,13},{10,... | collective-permute-start | bytes 345608 | tf_op jit(solution)/shard_map/ppermute | solution.py:723
  (49 other events, 368.1 us)
Sparse Core Ops, SparseCore 0:
  42.0 89.0 all-gather.4
  134.0 85.4 all-gather.6

commit v3 on v2

--- a/solution.py
+++ b/solution.py
@@ -7,6 +7,7 @@
 from jax.experimental.pallas import tpu as pltpu
 from jax.sharding import PartitionSpec as P
 
+MODEL_DIM = 960
 QUERY_HEADS = 15
 KV_HEADS = 5
 SHARE = QUERY_HEADS // KV_HEADS
@@ -47,6 +48,19 @@
     return pl.BlockSpec(shape, lambda *_: zeros)
 
 
+def side_by_side(ref):
+    return jnp.concatenate([ref[d] for d in range(ref.shape[0])], axis=1)
+
+
+def by_distance(ref, my_part):
+    parts = ref.shape[0]
+    return jnp.concatenate([ref[pl.ds(my_part ^ e, 1)].reshape(ref.shape[1:]) for e in range(parts)], axis=1)
+
+
+def whole_rows(pieces):
+    return jnp.concatenate([piece[:, : MODEL_DIM // len(pieces)] for piece in pieces], axis=1)
+
+
 def norm_kernel(hid_ref, cot_ref, gain_ref, router_ref, sel_ref, xn_ref, s1_ref, fg_ref, mix_ref, slope_ref):
     parts, _, width = hid_ref.shape
     square = 0.0
@@ -55,7 +69,7 @@
         x = hid_ref[d].astype(F32)
         square = square + jnp.sum(x * x, axis=-1, keepdims=True)
         logit = logit + jnp.sum(x * router_ref[d], axis=-1, keepdims=True)
-    scale = lax.rsqrt(square / (parts * width) + EPSILON)
+    scale = lax.rsqrt(square / MODEL_DIM + EPSILON)
     chance = 1.0 / (1.0 + jnp.exp(-logit))
     mix = sel_ref[...] * chance
     s1_ref[...] = scale
@@ -93,9 +107,7 @@
 
 def kv_kernel(xn_ref, w_ref, cos_ref, sin1_ref, sin2_ref, tag_ref, out_ref):
     rows = xn_ref.shape[1]
-    total = 0.0
-    for d in range(xn_ref.shape[0]):
-        total = total + dot(xn_ref[d], w_ref[d], NT)
+    total = dot(side_by_side(xn_ref), side_by_side(w_ref), NT)
     for h in range(KV_HEADS):
         u = total[:, h * TILE : (h + 1) * TILE]
         turned = (
@@ -131,10 +143,9 @@
 
 
 def q_kernel(xn_ref, w_ref, cos_ref, sin_ref, out_ref):
+    total = dot(side_by_side(xn_ref), side_by_side(w_ref), NT)
     for h in range(QUERY_HEADS):
-        u = 0.0
-        for d in range(xn_ref.shape[0]):
-            u = u + dot(xn_ref[d], w_ref[d, h * TILE : (h + 1) * TILE], NT)
+        u = total[:, h * TILE : (h + 1) * TILE]
         turned = u * cos_ref[...] + pltpu.roll(u, HEAD_DIM, 1) * sin_ref[...]
         out_ref[:, h * TILE : (h + 1) * TILE] = turned.astype(BF16)
 
@@ -351,13 +362,13 @@
 
 def out_kernel(o_ref, w_ref, hid_ref, gain_ref, mid_ref, x2_ref, s2_ref):
     parts, _, width = hid_ref.shape
-    o = o_ref[...]
+    out = dot(o_ref[...], side_by_side(w_ref))
     square = 0.0
     for d in range(parts):
-        middle = hid_ref[d].astype(F32) + dot(o, w_ref[d])
+        middle = hid_ref[d].astype(F32) + out[:, d * width : (d + 1) * width]
         mid_ref[d] = middle
         square = square + jnp.sum(middle * middle, axis=-1, keepdims=True)
-    scale = lax.rsqrt(square / (parts * width) + EPSILON)
+    scale = lax.rsqrt(square / MODEL_DIM + EPSILON)
     s2_ref[...] = scale
     for d in range(parts):
         x2_ref[d] = (mid_ref[d] * scale * gain_ref[d]).astype(BF16)
@@ -365,7 +376,7 @@
 
 def out_project(o, wo_pad, hid4, gain):
     parts, tokens, width = hid4.shape
-    rows = 128
+    rows = 256
     block = pl.BlockSpec((parts, rows, width), lambda i: (0, i, 0))
     column = pl.BlockSpec((rows, 1), lambda i: (i, 0))
     return pl.pallas_call(
@@ -390,31 +401,23 @@
 
 
 def ffn_kernel(meta_ref, x_ref, fg_ref, w_ref, out_ref, xg_ref, keep_ref, send_ref):
-    parts = x_ref.shape[0]
-    count = w_ref.shape[1]
-    rows = w_ref.shape[2] // 3
-    width = w_ref.shape[3]
+    parts, count, rows3, width = w_ref.shape
+    rows = rows3 // 3
     my_part, my_place = meta_ref[0], meta_ref[2]
     bits = count.bit_length() - 1
     turn_bits = [sum((i >> b & 1) << (bits - 1 - b) for b in range(bits)) for i in range(count)]
 
-    def tokens_of(ref, e):
-        return ref[pl.ds(my_part ^ e, 1)].reshape(ref.shape[1:])
-
-    def weight(e, which):
-        part = pl.ds(my_part ^ e, 1)
+    def weight(which):
         band = slice(which * rows, (which + 1) * rows)
-        pieces = [w_ref[part, pl.ds(my_place ^ i, 1), band, :].reshape(rows, width) for i in turn_bits]
-        return jnp.concatenate(pieces, axis=0)
-
-    gate = 0.0
-    up = 0.0
-    hidden_grad = 0.0
-    for e in range(parts):
-        x = tokens_of(x_ref, e)
-        gate = gate + dot(x, weight(e, 0), NT)
-        up = up + dot(x, weight(e, 1), NT)
-        hidden_grad = hidden_grad + dot(tokens_of(fg_ref, e), weight(e, 2), NT)
+        block = lambda d, i: w_ref[d, pl.ds(my_place ^ i, 1), band, :].reshape(rows, width)
+        lines = [jnp.concatenate([block(d, i) for d in range(parts)], axis=1) for i in turn_bits]
+        return jnp.concatenate(lines, axis=0)
+
+    w_gate, w_up, w_down = (weight(which) for which in range(3))
+    x, fg = side_by_side(x_ref), side_by_side(fg_ref)
+    gate = dot(x, w_gate, NT)
+    up = dot(x, w_up, NT)
+    hidden_grad = dot(fg, w_down, NT)
     chance = 1.0 / (1.0 + jnp.exp(-gate))
     silu = gate * chance
     hidden = (silu * up).astype(BF16)
@@ -422,29 +425,29 @@
     gate_grad = (hidden_grad * up * chance * (1.0 + gate * (1.0 - chance))).astype(BF16)
 
     first = pl.program_id(0) == 0
-    for e in range(parts):
-        place = pl.ds(my_part ^ e, 1)
-        out = dot(hidden, weight(e, 2))[None]
-        back = (dot(gate_grad, weight(e, 0)) + dot(up_grad, weight(e, 1)))[None]
+    out = dot(hidden, w_down)
+    back = dot(jnp.concatenate([gate_grad, up_grad], axis=1), jnp.concatenate([w_gate, w_up], axis=0))
+    for d in range(parts):
+        here = slice(d * width, (d + 1) * width)
 
         @pl.when(first)
-        def _(place=place, out=out, back=back):
-            out_ref[place] = out
-            xg_ref[place] = back
+        def _(d=d, here=here):
+            out_ref[d] = out[:, here]
+            xg_ref[d] = back[:, here]
 
         @pl.when(jnp.logical_not(first))
-        def _(place=place, out=out, back=back):
-            out_ref[place] += out
-            xg_ref[place] += back
-
-    turned = (gate_grad.T, up_grad.T, hidden.T)
-    for e in range(parts):
-        target = send_ref if e % 2 else keep_ref
-        for which in range(3):
-            right = tokens_of(fg_ref if which == 2 else x_ref, e)
-            grad = dot(turned[which], right).astype(BF16)
-            for i in range(count):
-                target[e // 2, i, which * rows : (which + 1) * rows, :] = grad[i * rows : (i + 1) * rows]
+        def _(d=d, here=here):
+            out_ref[d] += out[:, here]
+            xg_ref[d] += back[:, here]
+
+    x, fg = by_distance(x_ref, my_part), by_distance(fg_ref, my_part)
+    for which, left in enumerate((gate_grad, up_grad, hidden)):
+        left, right = left.T, fg if which == 2 else x
+        for i in range(count):
+            grad = dot(left[i * rows : (i + 1) * rows], right).astype(BF16)
+            for e in range(parts):
+                target = send_ref if e % 2 else keep_ref
+                target[e // 2, i, which * rows : (which + 1) * rows, :] = grad[:, e * width : (e + 1) * width]
 
 
 def ffn(my_part, my_shard, rows3, x4, fg4, weights, shard_first):
@@ -482,16 +485,18 @@
     scale = s2_ref[...]
     inner = 0.0
     mean = 0.0
+    rows_out = []
     for d in range(parts):
         middle = mid_ref[d]
         inputs = hid_ref[d].astype(F32)
         branch = (middle - inputs) + (out_a_ref[d] + out_b_ref[d])
         upstream = cot_ref[d].astype(F32)
         inner = inner + jnp.sum(upstream * branch, axis=-1, keepdims=True)
-        hidden_ref[d] = (inputs + mix * branch).astype(BF16)
+        rows_out.append(inputs + mix * branch)
         mean = mean + jnp.sum((xg_a_ref[d] + xg_b_ref[d]) * gain_ref[d] * middle, axis=-1, keepdims=True)
+    hidden_ref[...] = whole_rows(rows_out).astype(BF16)
     logit_grad = slope_ref[...] * inner
-    mean = mean / (parts * width) * (scale * scale * scale)
+    mean = mean / MODEL_DIM * (scale * scale * scale)
     first = pl.program_id(0) == 0
     for d in range(parts):
         middle = mid_ref[d]
@@ -525,9 +530,9 @@
         middle_kernel,
         grid=(tokens // rows,),
         in_specs=[block] * 7 + [column] * 3 + [vector] * 2,
-        out_specs=[block, block, block, vector, vector],
+        out_specs=[pl.BlockSpec((rows, MODEL_DIM), lambda i: (i, 0)), block, block, vector, vector],
         out_shape=[
-            jax.ShapeDtypeStruct(mid4.shape, BF16),
+            jax.ShapeDtypeStruct((tokens, MODEL_DIM), BF16),
             jax.ShapeDtypeStruct(mid4.shape, F32),
             jax.ShapeDtypeStruct(mid4.shape, BF16),
             jax.ShapeDtypeStruct((parts, 1, width), F32),
@@ -548,11 +553,7 @@
 
 
 def out_back_kernel(ag_ref, w_ref, do_ref):
-    for h in range(QUERY_HEADS):
-        total = 0.0
-        for d in range(ag_ref.shape[0]):
-            total = total + dot(ag_ref[d], w_ref[d, h * TILE : (h + 1) * TILE], NT)
-        do_ref[:, h * TILE : (h + 1) * TILE] = total.astype(BF16)
+    do_ref[...] = dot(side_by_side(ag_ref), side_by_side(w_ref), NT).astype(BF16)
 
 
 def out_back(ag4, wo_pad):
@@ -570,16 +571,25 @@
     )(ag4, wo_pad)
 
 
+def part_grads(left, ref, my_part, targets):
+    parts, _, width = ref.shape
+    right = by_distance(ref, my_part)
+    rows = left.shape[0]
+    step = rows // 4
+    for r in range(0, rows, step):
+        grad = dot(left[r : r + step], right).astype(BF16)
+        for e in range(parts):
+            targets[e % 2][e // 2, r : r + step] = grad[:, e * width : (e + 1) * width]
+
+
 def qo_back_kernel(meta_ref, dq_ref, xn_ref, w_ref, o_ref, ag_ref, keep_ref, send_ref, xg_ref):
-    parts = xn_ref.shape[0]
+    parts, _, width = xn_ref.shape
     sides = ((compact(dq_ref[...].T, False), xn_ref), (compact(o_ref[...].T, True), ag_ref))
-    for e in range(parts):
-        target = send_ref if e % 2 else keep_ref
-        for i, (left, ref) in enumerate(sides):
-            right = ref[pl.ds(meta_ref[0] ^ e, 1)].reshape(ref.shape[1:])
-            target[e // 2, i] = dot(left, right).astype(BF16)
+    for i, (left, ref) in enumerate(sides):
+        part_grads(left, ref, meta_ref[0], (keep_ref.at[:, i], send_ref.at[:, i]))
+    back = dot(dq_ref[...], side_by_side(w_ref))
     for d in range(parts):
-        xg_ref[d] = dot(dq_ref[...], w_ref[d])
+        xg_ref[d] = back[:, d * width : (d + 1) * width]
 
 
 def qo_back(my_part, dq, xn4, wq_pad, o, ag4):
@@ -609,11 +619,7 @@
             - pltpu.roll(u, HEAD_DIM // 2, 1) * sin2_ref[...]
         )
         back_ref[:, h * TILE : (h + 1) * TILE] = back.astype(BF16)
-    turned = back_ref[...].T
-    for e in range(xn_ref.shape[0]):
-        x = xn_ref[pl.ds(meta_ref[0] ^ e, 1)].reshape(xn_ref.shape[1:])
-        target = send_ref if e % 2 else keep_ref
-        target[e // 2] = dot(turned, x).astype(BF16)
+    part_grads(back_ref[...].T, xn_ref, meta_ref[0], (keep_ref, send_ref))
 
 
 def kv_back(my_part, dkv, tables, xn4):
@@ -638,15 +644,16 @@
 def final_kernel(xg_ref, kvb_ref, wkv_ref, hid_ref, part_ref, s1_ref, gain_ref, out_ref, gain_grad_ref):
     parts, rows, width = hid_ref.shape
     scale = s1_ref[...]
-    kvb = kvb_ref[...]
+    back = dot(kvb_ref[...], side_by_side(wkv_ref))
+    scaled_rows = []
     mean = 0.0
     first = pl.program_id(0) == 0
     for d in range(parts):
-        grad = xg_ref[d] + dot(kvb, wkv_ref[d])
+        grad = xg_ref[d] + back[:, d * width : (d + 1) * width]
         inputs = hid_ref[d].astype(F32)
         gain_grad = jnp.sum(grad * inputs * scale, axis=0, keepdims=True)
         scaled = grad * gain_ref[d]
-        out_ref[d] = scaled
+        scaled_rows.append(scaled)
         mean = mean + jnp.sum(scaled * inputs, axis=-1, keepdims=True)
 
         @pl.when(first)
@@ -657,14 +664,15 @@
         def _(d=d, gain_grad=gain_grad):
             gain_grad_ref[d] += gain_grad
 
-    mean = mean / (parts * width) * (scale * scale * scale)
-    for d in range(parts):
-        out_ref[d] = part_ref[d] + scale * out_ref[d] - hid_ref[d].astype(F32) * mean
+    mean = mean / MODEL_DIM * (scale * scale * scale)
+    out_ref[...] = whole_rows(
+        [part_ref[d] + scale * scaled_rows[d] - hid_ref[d].astype(F32) * mean for d in range(parts)]
+    )
 
 
 def final_step(xg4, kvb, wkv, hid4, part4, s1, gain):
     parts, tokens, width = hid4.shape
-    rows = 128
+    rows = 256
     block = pl.BlockSpec((parts, rows, width), lambda i: (0, i, 0))
     column = pl.BlockSpec((rows, 1), lambda i: (i, 0))
     vector = whole((parts, 1, width))
@@ -680,9 +688,9 @@
             column,
             vector,
         ],
-        out_specs=[block, vector],
+        out_specs=[pl.BlockSpec((rows, MODEL_DIM), lambda i: (i, 0)), vector],
         out_shape=[
-            jax.ShapeDtypeStruct(hid4.shape, F32),
+            jax.ShapeDtypeStruct((tokens, MODEL_DIM), F32),
             jax.ShapeDtypeStruct((parts, 1, width), F32),
         ],
         compiler_params=params(1),
@@ -929,28 +937,27 @@
     groups, rows, model = hidden_in.shape
     tokens = groups * rows
     parts, shard_count = lax.axis_size("dp"), lax.axis_size("fsdp")
-    width = model // parts
+    columns = model // parts
+    width = -(-columns // TILE) * TILE
+    fill = lambda array: jnp.pad(array, ((0, 0),) * (array.ndim - 1) + ((0, width - columns),))
     clock = Clock()
     at = clock.at
     net = Net(clock, parts, shard_count)
     my_part, my_shard = lax.axis_index("dp"), lax.axis_index("fsdp")
     ring = (EightShards if shard_count == 8 else AnyShards)(clock, parts, shard_count)
 
-    small = jnp.concatenate([key_weight.T, value_weight.T, w_query.T], axis=0)
+    small = fill(jnp.concatenate([key_weight.T, value_weight.T, w_query.T], axis=0))
     kv_rows, q_rows = key_weight.shape[1], w_query.shape[1]
     gate_rows, up_rows = w_gate.T, w_up.T
     chunk_rows = w_down.shape[0] // 2
     large = [w[c * chunk_rows : (c + 1) * chunk_rows] for c in range(2) for w in (gate_rows, up_rows, w_down)]
-    large = [jnp.concatenate(large[:3] + [w_output], axis=0), jnp.concatenate(large[3:], axis=0)]
+    large = [fill(jnp.concatenate(large[:3] + [w_output], axis=0)), fill(jnp.concatenate(large[3:], axis=0))]
 
     def heads_of(array, count):
         return array.reshape(parts, count, HEAD_DIM, width)
 
     def split(array):
-        return jnp.transpose(array.reshape(tokens, parts, width), (1, 0, 2))
-
-    def join(array):
-        return jnp.transpose(array, (1, 0, 2)).reshape(groups, rows, model)
+        return fill(jnp.transpose(array.reshape(tokens, parts, columns), (1, 0, 2)))
 
     half = HEAD_DIM // 2
     frequency = THETA ** (-(jnp.arange(half).astype(F32) * 2.0) / HEAD_DIM)
@@ -968,7 +975,7 @@
     tags = jnp.where(selected == 1, segment, -1).astype(BF16).reshape(groups, rows // TILE, TILE)
     tags = jnp.pad(tags, ((0, 0), (0, 16 - rows // TILE), (0, 0)))
     hid4, cot4 = split(hidden_in), split(cotangent)
-    vector = lambda v: v.astype(F32).reshape(parts, 1, width)
+    vector = lambda v: fill(v.astype(F32).reshape(parts, 1, columns))
     gain_one, gain_two, route = vector(gain_attn), vector(gain_ffn), vector(router)
     chosen = selected.reshape(tokens, 1).astype(F32)
 
@@ -1013,7 +1020,7 @@
     scatter_b = Scatter(net, keep_b, send_b, 1, 3 * chunk_rows, shards_bits[:1] + parts_bits + shards_bits[1:])
     scatter_a.step()
     out_b = at(out_b)
-    hidden4, part4, ag4, router_sum, gain_two_sum = middle_step(
+    hidden_out, part4, ag4, router_sum, gain_two_sum = middle_step(
         mid4, hid4, cot4, (out_a, out_b), (xg_a, xg_b), mix, slope, s2, gain_two, route
     )
     ag4 = at(ag4)
@@ -1035,6 +1042,7 @@
     scatter_qo.step()
     next(collect)
     scatter_b.step()
+    scatter_qo.step()
     dkv = next(collect).reshape(tokens, KV_HEADS * TILE)
     kvb, keep_kv, send_kv = kv_back(my_part, dkv, kv_tables, xn4)
 
@@ -1044,27 +1052,33 @@
 
     scatter_kv = Scatter(net, by_kind(keep_kv), by_kind(send_kv), 2, kv_rows)
     kvb = at(kvb)
-    grad_in4, gain_one_sum = final_step(xg_q, kvb, wkv, hid4, part4, s1, gain_one)
-    scatter_kv.step()
+    scatter_b.step()
     scatter_a.step()
     scatter_qo.step()
-    scatter_b.step()
+    grad_in, gain_one_sum = final_step(xg_q, kvb, wkv, hid4, part4, s1, gain_one)
+    scatter_kv.step()
     sums = SumAll(net, jnp.stack([gain_one_sum, gain_two_sum, router_sum]))
     sums.step()
+    scatter_b.land()
+    scatter_a.step()
+    scatter_qo.step()
+    scatter_kv.step()
+    sums.step()
+    scatter_a.land()
+    scatter_qo.land()
     for _ in range(net.bits):
         scatter_kv.step()
         sums.step()
-        scatter_qo.step()
-        scatter_a.step()
-        scatter_b.step()
     kv_grad = scatter_kv.result()
-    sums = sums.result().reshape(3, model)
-    q_grad, o_grad = scatter_qo.result()
-    grads = [s.result().reshape(3, chunk_rows, width) for s in (scatter_a, scatter_b)]
+    sums = sums.result()[..., :columns].reshape(3, model)
+    kv_grad = kv_grad[..., :columns]
+    q_grad, o_grad = scatter_qo.result()[..., :columns]
+    grads = [s.result().reshape(3, chunk_rows, width)[..., :columns] for s in (scatter_a, scatter_b)]
     gate_grad, up_grad, down_grad = jnp.concatenate(grads, axis=1)
+    sums = sums + clock.token[0, 0]
     return (
-        join(hidden4),
-        join(grad_in4),
+        hidden_out.reshape(groups, rows, model),
+        grad_in.reshape(groups, rows, model),
         sums[0],
         sums[1],
         sums[2],

time: 556 us -> 522 us (0.939)
  Pallas kernels: 184 us -> 157 us
  local copies, waits for them, and re-layouts: 48.1 us -> 38.9 us
  starting transfers between devices: 103 us -> 95.8 us
  other arithmetic: 53.6 us -> 59.9 us
    ppermute x30, waiting for transfers between devices: 85.8 us -> 65 us  [swap(): lax.ppermute(self.clock.at(array), AXES, [(i, i ^ flip) for i in range(se...]
    pallas_call x2, Pallas kernels: 62.5 us -> 43.2 us  [ffn(): pl.pallas_call(ffn_kernel, grid_spec=pltpu.PrefetchScalarGridSpec(num_sca...]
    ppermute x12, waiting for transfers between devices: 35.6 us -> 52.8 us  [move(): return lax.ppermute(self.clock.at(array), AXES, pairs)]
    ppermute x30, starting transfers between devices: 86.1 us -> 78.6 us  [swap(): lax.ppermute(self.clock.at(array), AXES, [(i, i ^ flip) for i in range(se...]
    all_gather x1, waiting for transfers between devices: 22.1 us -> 27.9 us  [shards(): lax.all_gather(clock.after(large[1]), AXES, axis=0, tiled=False)]
    reshape x9 -> x7, local copies, waits for them, and re-layouts: 9.58 us -> 3.92 us  [the longest x4 2.29 us: split(): return fill(jnp.transpose(array.reshape(tokens, parts, columns), (1, 0, 2)))]
    unnamed x83 -> x93, local copies, waits for them, and re-layouts: 15.1 us -> 12.7 us
  transfers between devices with their start and end apart: 44 -> 44, of which waited for: 17 -> 20; matrix products, arithmetic and copies ran while one was open for 16% -> 14% of each run, Pallas kernels for 34% -> 31%
where the time goes in v3:
time: 522 us; the launch traced here: 513 us
  Pallas kernels  157 us (30%)
  waiting for transfers between devices  146 us (28%)
  starting transfers between devices  95.8 us (18%)
  other arithmetic  59.9 us (11%)
  local copies, waits for them, and re-layouts  38.9 us (7%)
  between operations  15.3 us (3%)
    ppermute x30, starting transfers between devices, swap(): lax.ppermute(self.clock.at(array), AXES, [(i, i ^ flip) for i in range(se...  78.6 us
    ppermute x30, waiting for transfers between devices, swap(): lax.ppermute(self.clock.at(array), AXES, [(i, i ^ flip) for i in range(se...  65 us
    ppermute x12, waiting for transfers between devices, move(): return lax.ppermute(self.clock.at(array), AXES, pairs)  52.8 us
    pallas_call x2, Pallas kernels, ffn(): pl.pallas_call(ffn_kernel, grid_spec=pltpu.PrefetchScalarGridSpec(num_sca...  43.2 us
    pallas_call x1, Pallas kernels, attention_backward(): pl.pallas_call(functools.partial(backward_kernel, slots), grid_spec=pltpu...  37.5 us
    convert_element_type x18, other arithmetic, add(): return (mine.astype(F32) + other.astype(F32)).astype(dtype)  28 us
    all_gather x1, waiting for transfers between devices, shards(): lax.all_gather(clock.after(large[1]), AXES, axis=0, tiled=False)  27.9 us
    pallas_call x1, Pallas kernels, attention_forward(): pl.pallas_call(functools.partial(forward_kernel, slots), grid_spec=pltpu....  20.8 us
  transfers between devices with their start and end apart: 44, of which 20 were waited for; matrix products, arithmetic and copies ran while one was open for 14% of the time, Pallas kernels for 31%

profile of v3, /device:TPU:0, one launch (start us, length us, event | category | flops | bytes accessed | tf_op | source)
XLA Modules:
  0.0 512.5 jit_solution(10281639479998904438)
XLA Ops:
  9.0 4.1 collective-permute-start
  20.6 4.8 collective-permute-done.1
  35.6 4.6 first_norm.1
  44.5 19.0 %collective-permute-done.3 = bf16[2,2,2,200,256]{4,3,0,1,2:T(8,128)(2,1)S(1)} collective-permute-done((bf16[2,2,2,200,256]{4,3,0,1,2:T(8,128)(2,1)S(1)}, bf16[2,2,2,200,256]{4,3,0,1,2:T(8,128)(2,1)S(1)}, u32[]{:S(2)}, u32[]{:S(2)}) %collective-permute-start.3) | collective-permute-done | bytes 819232 | tf_op jit(solution)/shard_map/ppermute | solution.py:731
  73.5 4.0 kv_project.1.refs_0_
  77.5 4.4 collective-permute-start.5
  84.3 6.2 %q_project.1.q_ref = bf16[512,1920]{1,0:T(8,128)(2,1)} custom-call(bf16[4,512,256]{2,1,0:T(8,128)(2,1)} %get-tuple-element.252.xn_ref, bf16[4,1920,256]{2,1,0:T(8,128)(2,1)} %bitcast.168, f32[512,128]{1,0:T(8,128)} %get-tuple-element.554.cos_ref, f32[512,128]{1,0:T(8,128)} %get-tuple-element.551.sin_ref), custom_call_target="tpu_custom_call" | custom-call | flops 1887436800 | bytes 5898240 | tf_op jit(solution)/shard_map/q_project/pallas_call | solution.py:157
  90.5 16.6 %collective-permute-done.5 = bf16[2,272,640]{2,1,0:T(8,128)(2,1)S(1)} collective-permute-done((bf16[2,272,640]{2,1,0:T(8,128)(2,1)}, bf16[2,272,640]{2,1,0:T(8,128)(2,1)S(1)}, u32[]{:S(2)}, u32[]{:S(2)}) %collective-permute-start.5) | collective-permute-done | bytes 696352 | tf_op jit(solution)/shard_map/ppermute | solution.py:841
  110.1 21.0 %collective-permute-done.7.refs_1_ = bf16[2,272,640]{2,1,0:T(8,128)(2,1)S(1)} collective-permute-done((bf16[2,272,640]{2,1,0:T(8,128)(2,1)S(1)}, bf16[2,272,640]{2,1,0:T(8,128)(2,1)S(1)}, u32[]{:S(2)}, u32[]{:S(2)}) %collective-permute-start.7) | collective-permute-done | bytes 696352 | tf_op jit(solution)/shard_map/ppermute | solution.py:841
  139.2 20.8 %attention_forward.1 = (bf16[512,1920]{1,0:T(8,128)(2,1)}, f32[2,5,1,768]{3,2,1,0:T(1,128)}) custom-call(s32[6]{0:T(128)} %stack.100.slot_ref, bf16[512,1920]{1,0:T(8,128)(2,1)} %q_project.1.q_ref, f32[2,1,256]{2,1,0:T(1,128)} %reshape.340.seg_ref, bf16[2,272,640]{2,1,0:T(8,128)(2,1)} %kv_project.1.refs_0_, bf16[2,272,640]{2,1,0:T(8,128)(2,1)} %copy-done.38, ...), custom_call_target="tpu_custom_call" | custom-call | flops 6039797760 | bytes 7864320 | tf_op jit(solution)/shard_map/attention_forward/pallas_call | solution.py:270
  164.0 6.6 %out_project.1 = (f32[4,512,256]{2,1,0:T(8,128)}, bf16[4,512,256]{2,1,0:T(8,128)(2,1)}, f32[512,1]{1,0:T(8,128)}) custom-call(bf16[512,1920]{1,0:T(8,128)(2,1)} %get-tuple-element.290.o_ref, bf16[4,1920,256]{2,1,0:T(8,128)(2,1)} %bitcast.178, bf16[4,512,256]{2,1,0:T(8,128)(2,1)} %pad.41.hid_ref, f32[4,1,256]{2,1,0:T(1,128)} %pad_convert_fusion.gain_ref), custom_call_target="tpu_custom_call" | custom-call | flops 1887436800 | bytes 7864320 | tf_op jit(solution)/shard_map/out_project/pallas_call | solution.py:382
  170.6 21.6 %ffn.2 = (f32[4,512,256]{2,1,0:T(8,128)}, f32[4,512,256]{2,1,0:T(8,128)}, bf16[2,2,4,480,256]{4,3,2,1,0:T(8,128)(2,1)}, bf16[2,2,4,480,256]{4,3,2,1,0:T(8,128)(2,1)}) custom-call(s32[3]{0:T(128)} %pad_add_fusion.meta_ref, bf16[4,512,256]{2,1,0:T(8,128)(2,1)} %get-tuple-element.295.x_ref, bf16[4,512,256]{2,1,0:T(8,128)(2,1)} %get-tuple-element.296.fg_ref, ...), custom_call_target="tpu_custom_call" | custom-call | flops 11324620800 | bytes 22609920 | tf_op jit(solution)/shard_map/ffn/pallas_call | solution.py:464
  192.2 27.9 %all-gather.7.cloned.1.call-done = bf16[15360,256]{1,0:T(8,128)(2,1)} async-done(((bf16[480,256]{1,0:T(8,128)(2,1)}), bf16[15360,256]{1,0:T(8,128)(2,1)}) %all-gather.7.cloned.1.call-update) | async-done | bytes 7864336 | tf_op jit(solution)/shard_map/all_gather | solution.py:1001
  220.1 21.6 %ffn.3 = (f32[4,512,256]{2,1,0:T(8,128)}, f32[4,512,256]{2,1,0:T(8,128)}, bf16[2,2,4,480,256]{4,3,2,1,0:T(8,128)(2,1)}, bf16[2,2,4,480,256]{4,3,2,1,0:T(8,128)(2,1)}) custom-call(s32[3]{0:T(128)} %pad_add_fusion.meta_ref, bf16[4,512,256]{2,1,0:T(8,128)(2,1)} %get-tuple-element.295.x_ref, bf16[4,512,256]{2,1,0:T(8,128)(2,1)} %get-tuple-element.296.fg_ref, ...), custom_call_target="tpu_custom_call" | custom-call | flops 11324620800 | bytes 22609920 | tf_op jit(solution)/shard_map/ffn/pallas_call | solution.py:464
  246.2 4.8 fusion
  250.9 8.3 %middle_step.1 = (bf16[512,960]{1,0:T(8,128)(2,1)}, f32[4,512,256]{2,1,0:T(8,128)}, bf16[4,512,256]{2,1,0:T(8,128)(2,1)}, f32[4,1,256]{2,1,0:T(1,128)}, f32[4,1,256]{2,1,0:T(1,128)}) custom-call(f32[4,512,256]{2,1,0:T(8,128)} %get-tuple-element.292.mid_ref, bf16[4,512,256]{2,1,0:T(8,128)(2,1)} %pad.41.hid_ref, bf16[4,512,256]{2,1,0:T(8,128)(2,1)} %pad.42.cot_ref, ...), custom_call_target="tpu_custom_call" | custom-call | flops 14745600 | bytes 17694720 | tf_op jit(solution)/shard_map/middle_step/pallas_call | solution.py:529
  259.3 5.8 %fusion.1 = (bf16[8,480,256]{2,1,0:T(8,128)(2,1)S(1)}, bf16[8,480,256]{2,1,0:T(8,128)(2,1)}) fusion(bf16[1,2,4,480,256]{4,3,2,1,0:T(8,128)(2,1)} %get-tuple-element.511, bf16[16,480,256]{2,1,0:T(8,128)(2,1)} %bitcast.46, bf16[1,2,4,480,256]{4,3,2,1,0:T(8,128)(2,1)} %get-tuple-element.512), kind=kLoop, calls=%fused_computation.4 | loop fusion | flops 7864320 | bytes 11796480 | tf_op jit(solution)/shard_map/convert_element_type | solution.py:716
  267.2 6.1 %out_back.1.do_ref = bf16[512,1920]{1,0:T(8,128)(2,1)} custom-call(bf16[4,512,256]{2,1,0:T(8,128)(2,1)} %get-tuple-element.319.ag_ref, bf16[4,1920,256]{2,1,0:T(8,128)(2,1)} %bitcast.179), custom_call_target="tpu_custom_call" | custom-call | flops 1887436800 | bytes 5898240 | tf_op jit(solution)/shard_map/out_back/pallas_call | solution.py:562
  273.2 37.5 %attention_backward.1 = (bf16[512,1920]{1,0:T(8,128)(2,1)}, bf16[2,256,640]{2,1,0:T(8,128)(2,1)}, bf16[2,256,640]{2,1,0:T(8,128)(2,1)}, bf16[2,256,640]{2,1,0:T(...) custom-call(s32[6]{0:T(128)} %stack.100.slot_ref, ...), custom_call_target="tpu_custom_call" | custom-call | flops 15099494400 | bytes 15728640 | tf_op jit(solution)/shard_map/attention_backward/pallas_call | solution.py:342
  313.1 9.6 %qo_back.1 = (bf16[2,2,960,256]{3,2,1,0:T(8,128)(2,1)}, bf16[2,2,960,256]{3,2,1,0:T(8,128)(2,1)}, f32[4,512,256]{2,1,0:T(8,128)}) custom-call(s32[1]{0:T(128)} %bitcast.37.meta_ref, bf16[512,1920]{1,0:T(8,128)(2,1)} %get-tuple-element.330.dq_ref, bf16[4,512,256]{2,1,0:T(8,128)(2,1)} %get-tuple-element.252.xn_ref, bf16[4,1920,256]{2,1,0:T(8,128)(2,1)} %bitcast.169, ...), custom_call_target="tpu_custom_call" | custom-call | flops 3774873600 | bytes 13762560 | tf_op jit(solution)/shard_map/qo_back/pallas_call | solution.py:598
  322.7 3.4 add_convert_fusion.1
  341.1 3.5 collective-permute-start.26
  344.5 5.1 collective-permute-done.16
  357.9 48.6 %collective-permute-start.27 = (bf16[2,480,256]{2,1,0:T(8,128)(2,1)}, bf16[2,480,256]{2,1,0:T(8,128)(2,1)S(1)}, u32[]{:S(2)}, u32[]{:S(2)}) collective-permute-start(bf16[2,480,256]{2,1,0:T(8,128)(2,1)} %get-tuple-element.400), channel_id=1, source_target_pairs={{0,2},{1,3},{2,0},{3,1},{4,6},{5,7},{6,4},{7,5},{8,10},{9,11},{10,... | collective-permute-start | bytes 1474568 | tf_op jit(solution)/shard_map/ppermute | solution.py:731
  409.5 10.1 %collective-permute-done.21 = bf16[2,256,640]{2,1,0:T(8,128)(2,1)S(1)} collective-permute-done((bf16[2,256,640]{2,1,0:T(8,128)(2,1)S(1)}, bf16[2,256,640]{2,1,0:T(8,128)(2,1)S(1)}, u32[]{:S(2)}, u32[]{:S(2)}) %collective-permute-start.21) | collective-permute-done | bytes 655392 | tf_op jit(solution)/shard_map/ppermute | solution.py:841
  421.8 3.9 kv_back.1
  435.1 6.1 %final_step.1 = (f32[512,960]{1,0:T(8,128)}, f32[4,1,256]{2,1,0:T(1,128)}) custom-call(f32[4,512,256]{2,1,0:T(8,128)} %get-tuple-element.343.xg_ref, bf16[512,640]{1,0:T(8,128)(2,1)} %get-tuple-element.389.kvb_ref, bf16[4,640,256]{2,1,0:T(8,128)(2,1)} %bitcast.173, bf16[4,512,256]{2,1,0:T(8,128)(2,1)} %pad.41.hid_ref, ...), custom_call_target="tpu_custom_call" | custom-call | flops 629145600 | bytes 9830400 | tf_op jit(solution)/shard_map/final_step/pallas_call | solution.py:679
  446.6 7.9 %collective-permute-done.31 = bf16[2,480,256]{2,1,0:T(8,128)(2,1)S(1)} collective-permute-done((bf16[2,480,256]{2,1,0:T(8,128)(2,1)}, bf16[2,480,256]{2,1,0:T(8,128)(2,1)S(1)}, u32[]{:S(2)}, u32[]{:S(2)}) %collective-permute-start.31) | collective-permute-done | bytes 491552 | tf_op jit(solution)/shard_map/ppermute | solution.py:731
  455.3 3.7 collective-permute-done.30
  459.2 3.6 collective-permute-done.29
  464.2 7.8 %collective-permute-done.36 = bf16[1,480,256]{2,1,0:T(8,128)(2,1)S(1)} collective-permute-done((bf16[1,480,256]{2,1,0:T(8,128)(2,1)S(1)}, bf16[1,480,256]{2,1,0:T(8,128)(2,1)S(1)}, u32[]{:S(2)}, u32[]{:S(2)}) %collective-permute-start.36) | collective-permute-done | bytes 245792 | tf_op jit(solution)/shard_map/ppermute | solution.py:731
  488.8 3.0 collective-permute-start.40
  (268 shorter events, 135.3 us)
Async XLA Ops:
  7.2 152.8 %all-gather.5.cloned.1.call-start = ((), (), s32[]{:S(2)}) async-start(), calls=%async_computation | async-start | bytes 10137600 | tf_op jit(solution)/shard_map/all_gather | solution.py:989
  9.0 9.2 %collective-permute-start = (bf16[200,256]{1,0:T(8,128)(2,1)S(1)}, bf16[200,256]{1,0:T(8,128)(2,1)S(1)}, u32[]{:S(2)}, u32[]{:S(2)}) collective-permute-start(bf16[200,256]{1,0:T(8,128)(2,1)S(1)} %fusion.44), channel_id=1, source_target_pairs={{0,4},{1,5},{2,6},{3,7},{4,0},{5,1},{6,2},{7,3},{8,12},{9,13},{10,... | collective-permute-start | bytes 307208 | tf_op jit(solution)/shard_map/ppermute | solution.py:731
  26.2 15.5 %collective-permute-start.2 = (bf16[2,2,200,256]{3,2,0,1:T(8,128)(2,1)}, bf16[2,2,200,256]{3,2,0,1:T(8,128)(2,1)}, u32[]{:S(2)}, u32[]{:S(2)}) collective-permute-start(bf16[2,2,200,256]{3,2,0,1:T(8,128)(2,1)} %pad_maximum_fusion.5), channel_id=1, source_target_pairs={{0,1},{1,0},{2,3},{3,2},{4,5},{5,4},{6,7},{7,6},{8,9},{9,8},{10,11... | collective-permute-start | bytes 1228808 | tf_op jit(solution)/shard_map/ppermute | solution.py:731
  42.9 177.2 %all-gather.7.cloned.1.call-start = ((), (), s32[]{:S(2)}) async-start(), calls=%async_computation.1 | async-start | bytes 8110080 | tf_op jit(solution)/shard_map/all_gather | solution.py:1001
  42.9 20.6 %collective-permute-start.3 = (bf16[2,2,2,200,256]{4,3,0,1,2:T(8,128)(2,1)S(1)}, bf16[2,2,2,200,256]{4,3,0,1,2:T(8,128)(2,1)S(1)}, u32[]{:S(2)}, u32[]{:S(2)}) collective-permute-start(bf16[2,2,2,200,256]{4,3,0,1,2:T(8,128)(2,1)S(1)} %pad_maximum_fusion.4), channel_id=1, source_target_pairs={{0,16},{1,17},{2,18},{3,19},{4,20},{5,21},{6,22},{7,23},{8,24},{9,... | collective-permute-start | bytes 2457608 | tf_op jit(solution)/shard_map/ppermute | solution.py:731
  77.5 29.7 %collective-permute-start.5 = (bf16[2,272,640]{2,1,0:T(8,128)(2,1)}, bf16[2,272,640]{2,1,0:T(8,128)(2,1)S(1)}, u32[]{:S(2)}, u32[]{:S(2)}) collective-permute-start(bf16[2,272,640]{2,1,0:T(8,128)(2,1)} %kv_project.1.refs_0_), channel_id=1, source_target_pairs={{0,2},{1,3},{2,4},{3,5},{4,6},{5,7},{8,10},{9,11},{10,12},{11,13},... | collective-permute-start | bytes 2088968 | tf_op jit(solution)/shard_map/ppermute | solution.py:841
  107.3 23.8 %collective-permute-start.7 = (bf16[2,272,640]{2,1,0:T(8,128)(2,1)S(1)}, bf16[2,272,640]{2,1,0:T(8,128)(2,1)S(1)}, u32[]{:S(2)}, u32[]{:S(2)}) collective-permute-start(bf16[2,272,640]{2,1,0:T(8,128)(2,1)S(1)} %broadcast_select_fusion.3), channel_id=1, source_target_pairs={{0,1},{2,3},{4,5},{6,7},{7,6},{8,9},{10,11},{12,13},{14,15},{15,14... | collective-permute-start | bytes 2088968 | tf_op jit(solution)/shard_map/ppermute | solution.py:841
  109.3 21.7 %collective-permute-start.6 = (bf16[2,272,640]{2,1,0:T(8,128)(2,1)S(1)}, bf16[2,272,640]{2,1,0:T(8,128)(2,1)S(1)}, u32[]{:S(2)}, u32[]{:S(2)}) collective-permute-start(bf16[2,272,640]{2,1,0:T(8,128)(2,1)S(1)} %collective-permute-done.5), channel_id=1, source_target_pairs={{2,4},{3,5},{4,6},{5,7},{10,12},{11,13},{12,14},{13,15},{18,20},{1... | collective-permute-start | bytes 2088968 | tf_op jit(solution)/shard_map/ppermute | solution.py:841
  192.2 54.0 %collective-permute-start.11 = (bf16[2,2,4,480,256]{4,3,2,1,0:T(8,128)(2,1)}, bf16[2,2,4,480,256]{4,3,2,1,0:T(8,128)(2,1)}, u32[]{:S(2)}, u32[]{:S(2)}) collective-permute-start(bf16[2,2,4,480,256]{4,3,2,1,0:T(8,128)(2,1)} %get-tuple-element.303), channel_id=1, source_target_pairs={{0,8},{1,9},{2,10},{3,11},{4,12},{5,13},{6,14},{7,15},{8,0},{9,1},... | collective-permute-start | bytes 11796488 | tf_op jit(solution)/shard_map/ppermute | solution.py:731
  241.7 17.6 %collective-permute-start.12 = (bf16[2,2,4,480,256]{4,3,2,1,0:T(8,128)(2,1)}, bf16[2,2,4,480,256]{4,3,2,1,0:T(8,128)(2,1)}, u32[]{:S(2)}, u32[]{:S(2)}) collective-permute-start(bf16[2,2,4,480,256]{4,3,2,1,0:T(8,128)(2,1)} %get-tuple-element.321), channel_id=1, source_target_pairs={{0,8},{1,9},{2,10},{3,11},{4,12},{5,13},{6,14},{7,15},{8,0},{9,1},... | collective-permute-start | bytes 11796488 | tf_op jit(solution)/shard_map/ppermute | solution.py:731
  265.1 45.6 %collective-permute-start.13 = (bf16[8,480,256]{2,1,0:T(8,128)(2,1)}, bf16[8,480,256]{2,1,0:T(8,128)(2,1)}, u32[]{:S(2)}, u32[]{:S(2)}) collective-permute-start(bf16[8,480,256]{2,1,0:T(8,128)(2,1)} %get-tuple-element.332), channel_id=1, source_target_pairs={{0,1},{1,0},{2,3},{3,2},{4,5},{5,4},{6,7},{7,6},{8,9},{9,8},{10,11... | collective-permute-start | bytes 5898248 | tf_op jit(solution)/shard_map/ppermute | solution.py:731
  266.6 45.0 %collective-permute-start.14 = (bf16[8,480,256]{2,1,0:T(8,128)(2,1)}, bf16[8,480,256]{2,1,0:T(8,128)(2,1)}, u32[]{:S(2)}, u32[]{:S(2)}) collective-permute-start(bf16[8,480,256]{2,1,0:T(8,128)(2,1)} %get-tuple-element.337), channel_id=1, source_target_pairs={{0,16},{1,17},{2,18},{3,19},{4,20},{5,21},{6,22},{7,23},{8,24},{9,... | collective-permute-start | bytes 5898248 | tf_op jit(solution)/shard_map/ppermute | solution.py:731
  311.6 14.5 %collective-permute-start.15 = (bf16[2,256,640]{2,1,0:T(8,128)(2,1)}, bf16[2,256,640]{2,1,0:T(8,128)(2,1)}, u32[]{:S(2)}, u32[]{:S(2)}) collective-permute-start(bf16[2,256,640]{2,1,0:T(8,128)(2,1)} %get-tuple-element.347), channel_id=1, source_target_pairs={{5,4},{4,5},{7,6},{6,7},{13,12},{12,13},{15,14},{14,15},{21,20},{2... | collective-permute-start | bytes 1966088 | tf_op jit(solution)/shard_map/ppermute | solution.py:841
  327.5 10.6 %collective-permute-start.20 = (bf16[2,2,960,256]{3,2,1,0:T(8,128)(2,1)S(1)}, bf16[2,2,960,256]{3,2,1,0:T(8,128)(2,1)S(1)}, u32[]{:S(2)}, u32[]{:S(2)}) collective-permute-start(bf16[2,2,960,256]{3,2,1,0:T(8,128)(2,1)S(1)} %copy-done.37), channel_id=1, source_target_pairs={{0,8},{1,9},{2,10},{3,11},{4,12},{5,13},{6,14},{7,15},{8,0},{9,1},... | collective-permute-start | bytes 5898248 | tf_op jit(solution)/shard_map/ppermute | solution.py:731
  329.2 24.9 %collective-permute-start.23 = (bf16[4,480,256]{2,1,0:T(8,128)(2,1)}, bf16[4,480,256]{2,1,0:T(8,128)(2,1)}, u32[]{:S(2)}, u32[]{:S(2)}) collective-permute-start(bf16[4,480,256]{2,1,0:T(8,128)(2,1)} %get-tuple-element.376), channel_id=1, source_target_pairs={{0,16},{1,17},{2,18},{3,19},{4,20},{5,21},{6,22},{7,23},{8,24},{9,... | collective-permute-start | bytes 2949128 | tf_op jit(solution)/shard_map/ppermute | solution.py:731
  329.8 19.8 %collective-permute-start.16 = (bf16[2,256,640]{2,1,0:T(8,128)(2,1)}, bf16[2,256,640]{2,1,0:T(8,128)(2,1)}, u32[]{:S(2)}, u32[]{:S(2)}) collective-permute-start(bf16[2,256,640]{2,1,0:T(8,128)(2,1)} %get-tuple-element.352), channel_id=1, source_target_pairs={{1,0},{3,2},{5,4},{7,6},{6,7},{9,8},{11,10},{13,12},{15,14},{14,15... | collective-permute-start | bytes 1966088 | tf_op jit(solution)/shard_map/ppermute | solution.py:841
  333.7 15.9 %collective-permute-start.19 = (bf16[2,256,640]{2,1,0:T(8,128)(2,1)}, bf16[2,256,640]{2,1,0:T(8,128)(2,1)}, u32[]{:S(2)}, u32[]{:S(2)}) collective-permute-start(bf16[2,256,640]{2,1,0:T(8,128)(2,1)} %fusion.8), channel_id=1, source_target_pairs={{4,2},{5,3},{6,4},{7,5},{12,10},{13,11},{14,12},{15,13},{20,18},{2... | collective-permute-start | bytes 1966088 | tf_op jit(solution)/shard_map/ppermute | solution.py:841
  339.6 67.7 %collective-permute-start.22 = (bf16[1,2,8,120,256]{4,3,2,1,0:T(8,128)(2,1)}, bf16[1,2,8,120,256]{4,3,2,1,0:T(8,128)(2,1)}, u32[]{:S(2)}, u32[]{:S(2)}) collective-permute-start(bf16[1,2,8,120,256]{4,3,2,1,0:T(8,128)(2,1)} %get-tuple-element.375), channel_id=1, source_target_pairs={{0,16},{1,17},{2,18},{3,19},{4,20},{5,21},{6,22},{7,23},{8,24},{9,... | collective-permute-start | bytes 2949128 | tf_op jit(solution)/shard_map/ppermute | solution.py:731
  341.1 88.1 %collective-permute-start.26 = (bf16[4,480,256]{2,1,0:T(8,128)(2,1)}, bf16[4,480,256]{2,1,0:T(8,128)(2,1)}, u32[]{:S(2)}, u32[]{:S(2)}) collective-permute-start(bf16[4,480,256]{2,1,0:T(8,128)(2,1)} %get-tuple-element.399), channel_id=1, source_target_pairs={{0,1},{1,0},{2,3},{3,2},{4,5},{5,4},{6,7},{7,6},{8,9},{9,8},{10,11... | collective-permute-start | bytes 2949128 | tf_op jit(solution)/shard_map/ppermute | solution.py:731
  354.1 65.5 %collective-permute-start.21 = (bf16[2,256,640]{2,1,0:T(8,128)(2,1)S(1)}, bf16[2,256,640]{2,1,0:T(8,128)(2,1)S(1)}, u32[]{:S(2)}, u32[]{:S(2)}) collective-permute-start(bf16[2,256,640]{2,1,0:T(8,128)(2,1)S(1)} %fusion.11), channel_id=1, source_target_pairs={{2,0},{3,1},{4,2},{5,3},{6,4},{7,5},{10,8},{11,9},{12,10},{13,11},... | collective-permute-start | bytes 1966088 | tf_op jit(solution)/shard_map/ppermute | solution.py:841
  357.9 70.4 %collective-permute-start.27 = (bf16[2,480,256]{2,1,0:T(8,128)(2,1)}, bf16[2,480,256]{2,1,0:T(8,128)(2,1)S(1)}, u32[]{:S(2)}, u32[]{:S(2)}) collective-permute-start(bf16[2,480,256]{2,1,0:T(8,128)(2,1)} %get-tuple-element.400), channel_id=1, source_target_pairs={{0,2},{1,3},{2,0},{3,1},{4,6},{5,7},{6,4},{7,5},{8,10},{9,11},{10,... | collective-permute-start | bytes 1474568 | tf_op jit(solution)/shard_map/ppermute | solution.py:731
  429.2 12.9 %collective-permute-start.25 = (bf16[2,4,120,256]{3,2,0,1:T(8,128)(2,1)}, bf16[2,4,120,256]{3,2,0,1:T(8,128)(2,1)}, u32[]{:S(2)}, u32[]{:S(2)}) collective-permute-start(bf16[2,4,120,256]{3,2,0,1:T(8,128)(2,1)} %fusion.21), channel_id=1, source_target_pairs={{0,1},{1,0},{2,3},{3,2},{4,5},{5,4},{6,7},{7,6},{8,9},{9,8},{10,11... | collective-permute-start | bytes 1474568 | tf_op jit(solution)/shard_map/ppermute | solution.py:731
  430.0 15.3 %collective-permute-start.24 = (bf16[2,2,5,64,256]{4,3,2,1,0:T(8,128)(2,1)}, bf16[2,2,5,64,256]{4,3,2,1,0:T(8,128)(2,1)}, u32[]{:S(2)}, u32[]{:S(2)}) collective-permute-start(bf16[2,2,5,64,256]{4,3,2,1,0:T(8,128)(2,1)} %bitcast.163), channel_id=1, source_target_pairs={{0,8},{1,9},{2,10},{3,11},{4,12},{5,13},{6,14},{7,15},{8,0},{9,1},... | collective-permute-start | bytes 1966088 | tf_op jit(solution)/shard_map/ppermute | solution.py:731
  432.3 14.2 %collective-permute-start.32 = (bf16[1,480,256]{2,1,0:T(8,128)(2,1)}, bf16[1,480,256]{2,1,0:T(8,128)(2,1)}, u32[]{:S(2)}, u32[]{:S(2)}) collective-permute-start(bf16[1,480,256]{2,1,0:T(8,128)(2,1)} %add_convert_fusion.15), channel_id=1, source_target_pairs={{0,4},{1,5},{2,6},{3,7},{4,0},{5,1},{6,2},{7,3},{8,12},{9,13},{10,... | collective-permute-start | bytes 737288 | tf_op jit(solution)/shard_map/ppermute | solution.py:731
  435.1 19.4 %collective-permute-start.31 = (bf16[2,480,256]{2,1,0:T(8,128)(2,1)}, bf16[2,480,256]{2,1,0:T(8,128)(2,1)S(1)}, u32[]{:S(2)}, u32[]{:S(2)}) collective-permute-start(bf16[2,480,256]{2,1,0:T(8,128)(2,1)} %get-tuple-element.417), channel_id=1, source_target_pairs={{0,2},{1,3},{2,0},{3,1},{4,6},{5,7},{6,4},{7,5},{8,10},{9,11},{10,... | collective-permute-start | bytes 1474568 | tf_op jit(solution)/shard_map/ppermute | solution.py:731
  443.2 15.8 %collective-permute-start.30 = (bf16[2,2,120,256]{3,2,0,1:T(8,128)(2,1)S(1)}, bf16[2,2,120,256]{3,2,0,1:T(8,128)(2,1)S(1)}, u32[]{:S(2)}, u32[]{:S(2)}) collective-permute-start(bf16[2,2,120,256]{3,2,0,1:T(8,128)(2,1)S(1)} %get-tuple-element.416), channel_id=1, source_target_pairs={{0,2},{1,3},{2,0},{3,1},{4,6},{5,7},{6,4},{7,5},{8,10},{9,11},{10,... | collective-permute-start | bytes 737288 | tf_op jit(solution)/shard_map/ppermute | solution.py:731
  454.5 8.3 %collective-permute-start.29 = (bf16[1,2,8,40,256]{4,3,2,1,0:T(8,128)(2,1)S(1)}, bf16[1,2,8,40,256]{4,3,2,1,0:T(8,128)(2,1)S(1)}, u32[]{:S(2)}, u32[]{:S(2)}) collective-permute-start(bf16[1,2,8,40,256]{4,3,2,1,0:T(8,128)(2,1)S(1)} %get-tuple-element.415), channel_id=1, source_target_pairs={{0,16},{1,17},{2,18},{3,19},{4,20},{5,21},{6,22},{7,23},{8,24},{9,... | collective-permute-start | bytes 983048 | tf_op jit(solution)/shard_map/ppermute | solution.py:731
  455.2 7.8 %collective-permute-start.28 = (f32[3,4,1,256]{3,2,1,0:T(1,128)S(1)}, f32[3,4,1,256]{3,2,1,0:T(1,128)S(1)}, u32[]{:S(2)}, u32[]{:S(2)}) collective-permute-start(f32[3,4,1,256]{3,2,1,0:T(1,128)S(1)} %pad_maximum_fusion.9), channel_id=1, source_target_pairs={{0,8},{1,9},{2,10},{3,11},{4,12},{5,13},{6,14},{7,15},{8,0},{9,1},... | collective-permute-start | bytes 36872 | tf_op jit(solution)/shard_map/ppermute | solution.py:731
  455.3 16.8 %collective-permute-start.36 = (bf16[1,480,256]{2,1,0:T(8,128)(2,1)S(1)}, bf16[1,480,256]{2,1,0:T(8,128)(2,1)S(1)}, u32[]{:S(2)}, u32[]{:S(2)}) collective-permute-start(bf16[1,480,256]{2,1,0:T(8,128)(2,1)S(1)} %add_convert_fusion.12), channel_id=1, source_target_pairs={{0,4},{1,5},{2,6},{3,7},{4,0},{5,1},{6,2},{7,3},{8,12},{9,13},{10,... | collective-permute-start | bytes 737288 | tf_op jit(solution)/shard_map/ppermute | solution.py:731
  459.1 15.5 %collective-permute-start.35 = (bf16[2,1,120,256]{3,2,0,1:T(8,128)(2,1)S(1)}, bf16[2,1,120,256]{3,2,0,1:T(8,128)(2,1)S(1)}, u32[]{:S(2)}, u32[]{:S(2)}) collective-permute-start(bf16[2,1,120,256]{3,2,0,1:T(8,128)(2,1)S(1)} %fusion.37), channel_id=1, source_target_pairs={{0,4},{1,5},{2,6},{3,7},{4,0},{5,1},{6,2},{7,3},{8,12},{9,13},{10,... | collective-permute-start | bytes 368648 | tf_op jit(solution)/shard_map/ppermute | solution.py:731
  463.0 13.1 %collective-permute-start.34 = (bf16[2,4,40,256]{3,2,1,0:T(8,128)(2,1)S(1)}, bf16[2,4,40,256]{3,2,1,0:T(8,128)(2,1)S(1)}, u32[]{:S(2)}, u32[]{:S(2)}) collective-permute-start(bf16[2,4,40,256]{3,2,1,0:T(8,128)(2,1)S(1)} %get-tuple-element.433), channel_id=1, source_target_pairs={{0,1},{1,0},{2,3},{3,2},{4,5},{5,4},{6,7},{7,6},{8,9},{9,8},{10,11... | collective-permute-start | bytes 491528 | tf_op jit(solution)/shard_map/ppermute | solution.py:731
  481.3 14.5 %collective-permute-start.41 = (bf16[2,1,40,256]{3,2,0,1:T(8,128)(2,1)}, bf16[2,1,40,256]{3,2,0,1:T(8,128)(2,1)}, u32[]{:S(2)}, u32[]{:S(2)}) collective-permute-start(bf16[2,1,40,256]{3,2,0,1:T(8,128)(2,1)} %fusion.48), channel_id=1, source_target_pairs={{0,4},{1,5},{2,6},{3,7},{4,0},{5,1},{6,2},{7,3},{8,12},{9,13},{10,... | collective-permute-start | bytes 122888 | tf_op jit(solution)/shard_map/ppermute | solution.py:731
  (54 other events, 417.2 us)
Sparse Core Ops, SparseCore 0:
  43.0 88.9 all-gather.4
  134.9 85.1 all-gather.6

commit v4 on v3

--- a/solution.py
+++ b/solution.py
@@ -450,10 +450,10 @@
                 target[e // 2, i, which * rows : (which + 1) * rows, :] = grad[:, e * width : (e + 1) * width]
 
 
-def ffn(my_part, my_shard, rows3, x4, fg4, weights, shard_first):
+def ffn(my_part, my_shard, chunk, rows3, x4, fg4, weights, shard_first):
     parts, tokens, width = x4.shape
     half = weights.shape[1]
-    block = pl.BlockSpec((parts, half, None, rows3, width), lambda j, m: (0, 0, m[1] ^ j, 0, 0))
+    block = pl.BlockSpec((parts, half, None, rows3, width), lambda j, m: (0, 0, m[1] ^ j, chunk, 0))
     if shard_first:
         grad_block = pl.BlockSpec((None, parts // 2, half, rows3, width), lambda j, m: (j, 0, 0, 0, 0))
         grad = jax.ShapeDtypeStruct((2, parts // 2, half, rows3, width), BF16)
@@ -946,12 +946,13 @@
     my_part, my_shard = lax.axis_index("dp"), lax.axis_index("fsdp")
     ring = (EightShards if shard_count == 8 else AnyShards)(clock, parts, shard_count)
 
-    small = fill(jnp.concatenate([key_weight.T, value_weight.T, w_query.T], axis=0))
+    small = fill(jnp.concatenate([key_weight.T, value_weight.T], axis=0))
+    medium = fill(jnp.concatenate([w_query.T, w_output], axis=0))
     kv_rows, q_rows = key_weight.shape[1], w_query.shape[1]
     gate_rows, up_rows = w_gate.T, w_up.T
     chunk_rows = w_down.shape[0] // 2
     large = [w[c * chunk_rows : (c + 1) * chunk_rows] for c in range(2) for w in (gate_rows, up_rows, w_down)]
-    large = [fill(jnp.concatenate(large[:3] + [w_output], axis=0)), fill(jnp.concatenate(large[3:], axis=0))]
+    large = fill(jnp.concatenate(large, axis=0))
 
     def heads_of(array, count):
         return array.reshape(parts, count, HEAD_DIM, width)
@@ -980,43 +981,43 @@
     chosen = selected.reshape(tokens, 1).astype(F32)
 
     small_gather = Gather(net, small)
+    medium_all = lax.all_gather(medium, AXES, axis=0, tiled=False)
     small_gather.step()
     small_gather.step()
     small_gather.step()
     xn4, s1, fg4, mix, slope = first_norm(hid4, cot4, gain_one, route, chosen)
     xn4 = at(xn4)
     small_gather.step()
-    first_all = lax.all_gather(clock.after(large[0]), AXES, axis=0, tiled=False)
     small_all = small_gather.finish()
     keys = heads_of(small_all[:, :, :kv_rows], KV_HEADS)
-    values = heads_of(small_all[:, :, kv_rows : 2 * kv_rows], KV_HEADS)
+    values = heads_of(small_all[:, :, kv_rows:], KV_HEADS)
     wkv = jnp.concatenate([keys, values], axis=2).reshape(parts, KV_HEADS * TILE, width)
     spread = ring.spread(kv_project(groups, xn4, wkv, kv_tables, tags))
     next(spread)
-    queries = heads_of(small_all[:, :, 2 * kv_rows :], QUERY_HEADS)
+    large_all = lax.all_gather(clock.after(large), AXES, axis=0, tiled=False)
+    next(spread)
+    queries = heads_of(medium_all[:, :q_rows], QUERY_HEADS)
     wq_pad = jnp.concatenate([queries, queries[:, :, half:], queries[:, :, :half]], axis=2)
     wq_pad = wq_pad.reshape(parts, QUERY_HEADS * TILE, width)
     q = at(q_project(xn4, wq_pad, q_tables[0], q_tables[1] + q_tables[2], groups))
-    next(spread)
-    second_all = lax.all_gather(clock.after(large[1]), AXES, axis=0, tiled=False)
     next(spread)
     next(spread)
     slot_ids = ring.slot_ids()
     kvs = next(spread)
     o, lse = at(*attention_forward(slot_ids, q, seg_rows, kvs, ring.pairs))
-    outputs = heads_of(first_all[:, 3 * chunk_rows :], QUERY_HEADS)
+    outputs = heads_of(medium_all[:, q_rows:], QUERY_HEADS)
     wo_pad = jnp.concatenate([jnp.zeros_like(outputs), outputs], axis=2)
     wo_pad = wo_pad.reshape(parts, QUERY_HEADS * TILE, width)
     mid4, x24, s2 = out_project(o, wo_pad, hid4, gain_two)
     x24 = at(x24)
 
-    ffn_all = [a.reshape((parts, shard_count // 2, 2) + a.shape[1:]) for a in (first_all, second_all)]
+    ffn_all = large_all.reshape((parts, shard_count // 2, 2) + large.shape)
     bits = net.order[:-1][::-1]
     parts_bits = [bit for bit in bits if bit > net.core]
     shards_bits = [bit for bit in bits if bit < net.core]
-    out_a, xg_a, keep_a, send_a = ffn(my_part, my_shard, 3 * chunk_rows, x24, fg4, ffn_all[0], False)
+    out_a, xg_a, keep_a, send_a = ffn(my_part, my_shard, 0, 3 * chunk_rows, x24, fg4, ffn_all, False)
     scatter_a = Scatter(net, keep_a, send_a, 1, 3 * chunk_rows, parts_bits + shards_bits)
-    out_b, xg_b, keep_b, send_b = ffn(my_part, my_shard, 3 * chunk_rows, x24, fg4, ffn_all[1], True)
+    out_b, xg_b, keep_b, send_b = ffn(my_part, my_shard, 1, 3 * chunk_rows, x24, fg4, ffn_all, True)
     scatter_b = Scatter(net, keep_b, send_b, 1, 3 * chunk_rows, shards_bits[:1] + parts_bits + shards_bits[1:])
     scatter_a.step()
     out_b = at(out_b)
@@ -1052,16 +1053,20 @@
 
     scatter_kv = Scatter(net, by_kind(keep_kv), by_kind(send_kv), 2, kv_rows)
     kvb = at(kvb)
+    grad_in, gain_one_sum = final_step(xg_q, kvb, wkv, hid4, part4, s1, gain_one)
+    scatter_kv.step()
     scatter_b.step()
     scatter_a.step()
     scatter_qo.step()
-    grad_in, gain_one_sum = final_step(xg_q, kvb, wkv, hid4, part4, s1, gain_one)
-    scatter_kv.step()
     sums = SumAll(net, jnp.stack([gain_one_sum, gain_two_sum, router_sum]))
     sums.step()
-    scatter_b.land()
+    scatter_kv.step()
+    sums.step()
     scatter_a.step()
     scatter_qo.step()
+    scatter_kv.step()
+    sums.step()
+    scatter_b.land()
     scatter_kv.step()
     sums.step()
     scatter_a.land()

time: 522 us -> 517 us (level)
  waiting for transfers between devices: 146 us -> 135 us
  local copies, waits for them, and re-layouts: 38.9 us -> 48.9 us
    all_gather x2, waiting for transfers between devices: 27.9 us -> 54 us  [the longest x1 53.9 us: shards(): large_all = lax.all_gather(clock.after(large), AXES, axis=0, tiled=False)]
    ppermute x30, waiting for transfers between devices: 65 us -> 40.8 us  [swap(): lax.ppermute(self.clock.at(array), AXES, [(i, i ^ flip) for i in range(se...]
    ppermute x12, waiting for transfers between devices: 52.8 us -> 40.7 us  [move(): return lax.ppermute(self.clock.at(array), AXES, pairs)]
    unnamed x93 -> x74, local copies, waits for them, and re-layouts: 12.7 us -> 21.8 us
  transfers between devices with their start and end apart: 44 -> 44, of which waited for: 20 -> 17; matrix products, arithmetic and copies ran while one was open for 14% -> 16% of each run, Pallas kernels for 31% -> 27%
where the time goes in v4:
time: 517 us; the launch traced here: 507 us
  Pallas kernels  156 us (30%)
  waiting for transfers between devices  135 us (26%)
  starting transfers between devices  93.3 us (18%)
  other arithmetic  57.8 us (11%)
  local copies, waits for them, and re-layouts  48.9 us (9%)
  between operations  15.3 us (3%)
    ppermute x30, starting transfers between devices, swap(): lax.ppermute(self.clock.at(array), AXES, [(i, i ^ flip) for i in range(se...  76.5 us
    all_gather x1, waiting for transfers between devices, shards(): large_all = lax.all_gather(clock.after(large), AXES, axis=0, tiled=False)  53.9 us
    pallas_call x2, Pallas kernels, ffn(): pl.pallas_call(ffn_kernel, grid_spec=pltpu.PrefetchScalarGridSpec(num_sca...  42.8 us
    ppermute x30, waiting for transfers between devices, swap(): lax.ppermute(self.clock.at(array), AXES, [(i, i ^ flip) for i in range(se...  40.8 us
    ppermute x12, waiting for transfers between devices, move(): return lax.ppermute(self.clock.at(array), AXES, pairs)  40.7 us
    pallas_call x1, Pallas kernels, attention_backward(): pl.pallas_call(functools.partial(backward_kernel, slots), grid_spec=pltpu...  37.5 us
    convert_element_type x18, other arithmetic, add(): return (mine.astype(F32) + other.astype(F32)).astype(dtype)  27.6 us
    unnamed x74, local copies, waits for them, and re-layouts  21.8 us
  transfers between devices with their start and end apart: 44, of which 17 were waited for; matrix products, arithmetic and copies ran while one was open for 16% of the time, Pallas kernels for 27%

profile of v4, /device:TPU:0, one launch (start us, length us, event | category | flops | bytes accessed | tf_op | source)
XLA Modules:
  0.0 507.2 jit_solution(3381166930333089560)
XLA Ops:
  10.5 4.1 collective-permute-start
  34.3 4.6 first_norm.1
  41.1 5.0 collective-permute-done.2
  50.3 4.9 collective-permute-done.3
  60.0 4.0 kv_project.1.refs_0_
  65.7 20.4 %collective-permute-done.5 = bf16[2,272,640]{2,1,0:T(8,128)(2,1)S(1)} collective-permute-done((bf16[2,272,640]{2,1,0:T(8,128)(2,1)}, bf16[2,272,640]{2,1,0:T(8,128)(2,1)S(1)}, u32[]{:S(2)}, u32[]{:S(2)}) %collective-permute-start.5) | collective-permute-done | bytes 696352 | tf_op jit(solution)/shard_map/ppermute | solution.py:841
  88.1 4.4 collective-permute-start.7
  97.9 6.1 %q_project.1.q_ref = bf16[512,1920]{1,0:T(8,128)(2,1)} custom-call(bf16[4,512,256]{2,1,0:T(8,128)(2,1)} %get-tuple-element.251.xn_ref, bf16[4,1920,256]{2,1,0:T(8,128)(2,1)} %bitcast.167, f32[512,128]{1,0:T(8,128)} %get-tuple-element.552.cos_ref, f32[512,128]{1,0:T(8,128)} %get-tuple-element.549.sin_ref), custom_call_target="tpu_custom_call" | custom-call | flops 1887436800 | bytes 5898240 | tf_op jit(solution)/shard_map/q_project/pallas_call | solution.py:157
  104.0 3.7 collective-permute-done.7.refs_1_
  118.5 20.8 %attention_forward.1 = (bf16[512,1920]{1,0:T(8,128)(2,1)}, f32[2,5,1,768]{3,2,1,0:T(1,128)}) custom-call(s32[6]{0:T(128)} %stack.100.slot_ref, bf16[512,1920]{1,0:T(8,128)(2,1)} %q_project.1.q_ref, f32[2,1,256]{2,1,0:T(1,128)} %reshape.337.seg_ref, bf16[2,272,640]{2,1,0:T(8,128)(2,1)} %kv_project.1.refs_0_, ...), custom_call_target="tpu_custom_call" | custom-call | flops 6039797760 | bytes 7864320 | tf_op jit(solution)/shard_map/attention_forward/pallas_call | solution.py:270
  139.3 6.6 %out_project.1 = (f32[4,512,256]{2,1,0:T(8,128)}, bf16[4,512,256]{2,1,0:T(8,128)(2,1)}, f32[512,1]{1,0:T(8,128)}) custom-call(bf16[512,1920]{1,0:T(8,128)(2,1)} %get-tuple-element.289.o_ref, bf16[4,1920,256]{2,1,0:T(8,128)(2,1)} %bitcast.177, bf16[4,512,256]{2,1,0:T(8,128)(2,1)} %pad.41.hid_ref, f32[4,1,256]{2,1,0:T(1,128)} %pad_convert_fusion.gain_ref), custom_call_target="tpu_custom_call" | custom-call | flops 1887436800 | bytes 7864320 | tf_op jit(solution)/shard_map/out_project/pallas_call | solution.py:382
  146.0 53.9 %all-gather.7.cloned.1.call-done = bf16[30720,256]{1,0:T(8,128)(2,1)} async-done(((bf16[960,256]{1,0:T(8,128)(2,1)}), bf16[30720,256]{1,0:T(8,128)(2,1)}) %all-gather.7.cloned.1.call-update) | async-done | bytes 15728656 | tf_op jit(solution)/shard_map/all_gather | solution.py:997
  199.9 21.5 %ffn.2 = (f32[4,512,256]{2,1,0:T(8,128)}, f32[4,512,256]{2,1,0:T(8,128)}, bf16[2,2,4,480,256]{4,3,2,1,0:T(8,128)(2,1)}, bf16[2,2,4,480,256]{4,3,2,1,0:T(8,128)(2,1)}) custom-call(s32[3]{0:T(128)} %pad_add_fusion.meta_ref, bf16[4,512,256]{2,1,0:T(8,128)(2,1)} %get-tuple-element.293.x_ref, bf16[4,512,256]{2,1,0:T(8,128)(2,1)} %get-tuple-element.294.fg_ref, ...), custom_call_target="tpu_custom_call" | custom-call | flops 11324620800 | bytes 22609920 | tf_op jit(solution)/shard_map/ffn/pallas_call | solution.py:464
  221.7 21.3 %ffn.3 = (f32[4,512,256]{2,1,0:T(8,128)}, f32[4,512,256]{2,1,0:T(8,128)}, bf16[2,2,4,480,256]{4,3,2,1,0:T(8,128)(2,1)}, bf16[2,2,4,480,256]{4,3,2,1,0:T(8,128)(2,1)}) custom-call(s32[3]{0:T(128)} %pad_add_fusion.meta_ref, bf16[4,512,256]{2,1,0:T(8,128)(2,1)} %get-tuple-element.293.x_ref, bf16[4,512,256]{2,1,0:T(8,128)(2,1)} %get-tuple-element.294.fg_ref, ...), custom_call_target="tpu_custom_call" | custom-call | flops 11324620800 | bytes 22609920 | tf_op jit(solution)/shard_map/ffn/pallas_call | solution.py:464
  250.7 4.7 fusion
  255.5 8.3 %middle_step.1 = (bf16[512,960]{1,0:T(8,128)(2,1)}, f32[4,512,256]{2,1,0:T(8,128)}, bf16[4,512,256]{2,1,0:T(8,128)(2,1)}, f32[4,1,256]{2,1,0:T(1,128)}, f32[4,1,256]{2,1,0:T(1,128)}) custom-call(f32[4,512,256]{2,1,0:T(8,128)} %get-tuple-element.290.mid_ref, bf16[4,512,256]{2,1,0:T(8,128)(2,1)} %pad.41.hid_ref, bf16[4,512,256]{2,1,0:T(8,128)(2,1)} %pad.42.cot_ref, ...), custom_call_target="tpu_custom_call" | custom-call | flops 14745600 | bytes 17694720 | tf_op jit(solution)/shard_map/middle_step/pallas_call | solution.py:529
  263.8 5.8 %fusion.1 = (bf16[8,480,256]{2,1,0:T(8,128)(2,1)S(1)}, bf16[8,480,256]{2,1,0:T(8,128)(2,1)}) fusion(bf16[1,2,4,480,256]{4,3,2,1,0:T(8,128)(2,1)} %get-tuple-element.509, bf16[16,480,256]{2,1,0:T(8,128)(2,1)} %bitcast.45, bf16[1,2,4,480,256]{4,3,2,1,0:T(8,128)(2,1)} %get-tuple-element.510), kind=kLoop, calls=%fused_computation.4 | loop fusion | flops 7864320 | bytes 11796480 | tf_op jit(solution)/shard_map/convert_element_type | solution.py:716
  272.1 6.0 %out_back.1.do_ref = bf16[512,1920]{1,0:T(8,128)(2,1)} custom-call(bf16[4,512,256]{2,1,0:T(8,128)(2,1)} %get-tuple-element.317.ag_ref, bf16[4,1920,256]{2,1,0:T(8,128)(2,1)} %bitcast.178), custom_call_target="tpu_custom_call" | custom-call | flops 1887436800 | bytes 5898240 | tf_op jit(solution)/shard_map/out_back/pallas_call | solution.py:562
  278.1 37.5 %attention_backward.1 = (bf16[512,1920]{1,0:T(8,128)(2,1)}, bf16[2,256,640]{2,1,0:T(8,128)(2,1)}, bf16[2,256,640]{2,1,0:T(8,128)(2,1)}, bf16[2,256,640]{2,1,0:T(...) custom-call(s32[6]{0:T(128)} %stack.100.slot_ref, ...), custom_call_target="tpu_custom_call" | custom-call | flops 15099494400 | bytes 15728640 | tf_op jit(solution)/shard_map/attention_backward/pallas_call | solution.py:342
  317.1 9.6 %qo_back.1 = (bf16[2,2,960,256]{3,2,1,0:T(8,128)(2,1)}, bf16[2,2,960,256]{3,2,1,0:T(8,128)(2,1)}, f32[4,512,256]{2,1,0:T(8,128)}) custom-call(s32[1]{0:T(128)} %bitcast.35.meta_ref, bf16[512,1920]{1,0:T(8,128)(2,1)} %get-tuple-element.328.dq_ref, bf16[4,512,256]{2,1,0:T(8,128)(2,1)} %get-tuple-element.251.xn_ref, bf16[4,1920,256]{2,1,0:T(8,128)(2,1)} %bitcast.168, ...), custom_call_target="tpu_custom_call" | custom-call | flops 3774873600 | bytes 13762560 | tf_op jit(solution)/shard_map/qo_back/pallas_call | solution.py:598
  326.7 3.4 add_convert_fusion.1
  345.1 3.5 collective-permute-start.25
  348.6 5.9 %collective-permute-done.16 = bf16[2,256,640]{2,1,0:T(8,128)(2,1)} collective-permute-done((bf16[2,256,640]{2,1,0:T(8,128)(2,1)}, bf16[2,256,640]{2,1,0:T(8,128)(2,1)}, u32[]{:S(2)}, u32[]{:S(2)}) %collective-permute-start.16) | collective-permute-done | bytes 655392 | tf_op jit(solution)/shard_map/ppermute | solution.py:841
  362.1 42.9 %collective-permute-start.26 = (bf16[2,480,256]{2,1,0:T(8,128)(2,1)}, bf16[2,480,256]{2,1,0:T(8,128)(2,1)}, u32[]{:S(2)}, u32[]{:S(2)}) collective-permute-start(bf16[2,480,256]{2,1,0:T(8,128)(2,1)} %get-tuple-element.396), channel_id=1, source_target_pairs={{0,2},{1,3},{2,0},{3,1},{4,6},{5,7},{6,4},{7,5},{8,10},{9,11},{10,... | collective-permute-start | bytes 1474568 | tf_op jit(solution)/shard_map/ppermute | solution.py:731
  407.3 10.6 %collective-permute-done.21 = bf16[2,256,640]{2,1,0:T(8,128)(2,1)S(1)} collective-permute-done((bf16[2,256,640]{2,1,0:T(8,128)(2,1)S(1)}, bf16[2,256,640]{2,1,0:T(8,128)(2,1)S(1)}, u32[]{:S(2)}, u32[]{:S(2)}) %collective-permute-start.21) | collective-permute-done | bytes 655392 | tf_op jit(solution)/shard_map/ppermute | solution.py:841
  420.2 4.0 kv_back.1
  427.1 6.1 %final_step.1 = (f32[512,960]{1,0:T(8,128)}, f32[4,1,256]{2,1,0:T(1,128)}) custom-call(f32[4,512,256]{2,1,0:T(8,128)} %get-tuple-element.341.xg_ref, bf16[512,640]{1,0:T(8,128)(2,1)} %get-tuple-element.387.kvb_ref, bf16[4,640,256]{2,1,0:T(8,128)(2,1)} %bitcast.170, bf16[4,512,256]{2,1,0:T(8,128)(2,1)} %pad.41.hid_ref, ...), custom_call_target="tpu_custom_call" | custom-call | flops 629145600 | bytes 9830400 | tf_op jit(solution)/shard_map/final_step/pallas_call | solution.py:679
  443.9 3.2 collective-permute-start.36
  448.7 11.2 %collective-permute-done.33 = bf16[2,480,256]{2,1,0:T(8,128)(2,1)S(1)} collective-permute-done((bf16[2,480,256]{2,1,0:T(8,128)(2,1)S(1)}, bf16[2,480,256]{2,1,0:T(8,128)(2,1)S(1)}, u32[]{:S(2)}, u32[]{:S(2)}) %collective-permute-start.33) | collective-permute-done | bytes 491552 | tf_op jit(solution)/shard_map/ppermute | solution.py:731
  460.7 3.1 collective-permute-done.32
  464.1 3.5 collective-permute-start.39
  476.7 5.7 %collective-permute-done.39 = bf16[1,480,256]{2,1,0:T(8,128)(2,1)} collective-permute-done((bf16[1,480,256]{2,1,0:T(8,128)(2,1)S(1)}, bf16[1,480,256]{2,1,0:T(8,128)(2,1)}, u32[]{:S(2)}, u32[]{:S(2)}) %collective-permute-start.39) | collective-permute-done | bytes 245792 | tf_op jit(solution)/shard_map/ppermute | solution.py:731
  (247 shorter events, 135.5 us)
Async XLA Ops:
  7.2 86.1 %all-gather.5.cloned.1.call-start = ((), (), s32[]{:S(2)}) async-start(), calls=%async_computation | async-start | bytes 4055040 | tf_op jit(solution)/shard_map/all_gather | solution.py:984
  9.7 190.3 %all-gather.7.cloned.1.call-start = ((), (), s32[]{:S(2)}) async-start(), calls=%async_computation.1 | async-start | bytes 16220160 | tf_op jit(solution)/shard_map/all_gather | solution.py:997
  10.5 21.5 %collective-permute-start = (bf16[80,256]{1,0:T(8,128)(2,1)S(1)}, bf16[80,256]{1,0:T(8,128)(2,1)S(1)}, u32[]{:S(2)}, u32[]{:S(2)}) collective-permute-start(bf16[80,256]{1,0:T(8,128)(2,1)S(1)} %fusion.37), channel_id=1, source_target_pairs={{0,4},{1,5},{2,6},{3,7},{4,0},{5,1},{6,2},{7,3},{8,12},{9,13},{10,... | collective-permute-start | bytes 122888 | tf_op jit(solution)/shard_map/ppermute | solution.py:731
  46.2 9.0 %collective-permute-start.3 = (bf16[2,2,2,80,256]{4,3,0,1,2:T(8,128)(2,1)S(1)}, bf16[2,2,2,80,256]{4,3,0,1,2:T(8,128)(2,1)S(1)}, u32[]{:S(2)}, u32[]{:S(2)}) collective-permute-start(bf16[2,2,2,80,256]{4,3,0,1,2:T(8,128)(2,1)S(1)} %pad_maximum_fusion.5), channel_id=1, source_target_pairs={{0,16},{1,17},{2,18},{3,19},{4,20},{5,21},{6,22},{7,23},{8,24},{9,... | collective-permute-start | bytes 983048 | tf_op jit(solution)/shard_map/ppermute | solution.py:731
  64.0 22.1 %collective-permute-start.5 = (bf16[2,272,640]{2,1,0:T(8,128)(2,1)}, bf16[2,272,640]{2,1,0:T(8,128)(2,1)S(1)}, u32[]{:S(2)}, u32[]{:S(2)}) collective-permute-start(bf16[2,272,640]{2,1,0:T(8,128)(2,1)} %kv_project.1.refs_0_), channel_id=1, source_target_pairs={{0,2},{1,3},{2,4},{3,5},{4,6},{5,7},{8,10},{9,11},{10,12},{11,13},... | collective-permute-start | bytes 2088968 | tf_op jit(solution)/shard_map/ppermute | solution.py:841
  88.1 19.7 %collective-permute-start.7 = (bf16[2,272,640]{2,1,0:T(8,128)(2,1)}, bf16[2,272,640]{2,1,0:T(8,128)(2,1)}, u32[]{:S(2)}, u32[]{:S(2)}) collective-permute-start(bf16[2,272,640]{2,1,0:T(8,128)(2,1)} %broadcast_select_fusion.3), channel_id=1, source_target_pairs={{0,1},{2,3},{4,5},{6,7},{7,6},{8,9},{10,11},{12,13},{14,15},{15,14... | collective-permute-start | bytes 2088968 | tf_op jit(solution)/shard_map/ppermute | solution.py:841
  92.5 15.3 %collective-permute-start.6 = (bf16[2,272,640]{2,1,0:T(8,128)(2,1)S(1)}, bf16[2,272,640]{2,1,0:T(8,128)(2,1)S(1)}, u32[]{:S(2)}, u32[]{:S(2)}) collective-permute-start(bf16[2,272,640]{2,1,0:T(8,128)(2,1)S(1)} %collective-permute-done.5), channel_id=1, source_target_pairs={{2,4},{3,5},{4,6},{5,7},{10,12},{11,13},{12,14},{13,15},{18,20},{1... | collective-permute-start | bytes 2088968 | tf_op jit(solution)/shard_map/ppermute | solution.py:841
  221.4 27.3 %collective-permute-start.11 = (bf16[2,2,4,480,256]{4,3,2,1,0:T(8,128)(2,1)}, bf16[2,2,4,480,256]{4,3,2,1,0:T(8,128)(2,1)S(1)}, u32[]{:S(2)}, u32[]{:S(2)}) collective-permute-start(bf16[2,2,4,480,256]{4,3,2,1,0:T(8,128)(2,1)} %get-tuple-element.301), channel_id=1, source_target_pairs={{0,8},{1,9},{2,10},{3,11},{4,12},{5,13},{6,14},{7,15},{8,0},{9,1},... | collective-permute-start | bytes 11796488 | tf_op jit(solution)/shard_map/ppermute | solution.py:731
  243.0 20.8 %collective-permute-start.12 = (bf16[2,2,4,480,256]{4,3,2,1,0:T(8,128)(2,1)}, bf16[2,2,4,480,256]{4,3,2,1,0:T(8,128)(2,1)}, u32[]{:S(2)}, u32[]{:S(2)}) collective-permute-start(bf16[2,2,4,480,256]{4,3,2,1,0:T(8,128)(2,1)} %get-tuple-element.319), channel_id=1, source_target_pairs={{0,8},{1,9},{2,10},{3,11},{4,12},{5,13},{6,14},{7,15},{8,0},{9,1},... | collective-permute-start | bytes 11796488 | tf_op jit(solution)/shard_map/ppermute | solution.py:731
  269.6 46.0 %collective-permute-start.13 = (bf16[8,480,256]{2,1,0:T(8,128)(2,1)}, bf16[8,480,256]{2,1,0:T(8,128)(2,1)}, u32[]{:S(2)}, u32[]{:S(2)}) collective-permute-start(bf16[8,480,256]{2,1,0:T(8,128)(2,1)} %get-tuple-element.330), channel_id=1, source_target_pairs={{0,1},{1,0},{2,3},{3,2},{4,5},{5,4},{6,7},{7,6},{8,9},{9,8},{10,11... | collective-permute-start | bytes 5898248 | tf_op jit(solution)/shard_map/ppermute | solution.py:731
  270.2 45.4 %collective-permute-start.14 = (bf16[8,480,256]{2,1,0:T(8,128)(2,1)}, bf16[8,480,256]{2,1,0:T(8,128)(2,1)}, u32[]{:S(2)}, u32[]{:S(2)}) collective-permute-start(bf16[8,480,256]{2,1,0:T(8,128)(2,1)} %get-tuple-element.335), channel_id=1, source_target_pairs={{0,16},{1,17},{2,18},{3,19},{4,20},{5,21},{6,22},{7,23},{8,24},{9,... | collective-permute-start | bytes 5898248 | tf_op jit(solution)/shard_map/ppermute | solution.py:731
  315.6 14.5 %collective-permute-start.15 = (bf16[2,256,640]{2,1,0:T(8,128)(2,1)}, bf16[2,256,640]{2,1,0:T(8,128)(2,1)}, u32[]{:S(2)}, u32[]{:S(2)}) collective-permute-start(bf16[2,256,640]{2,1,0:T(8,128)(2,1)} %get-tuple-element.345), channel_id=1, source_target_pairs={{5,4},{4,5},{7,6},{6,7},{13,12},{12,13},{15,14},{14,15},{21,20},{2... | collective-permute-start | bytes 1966088 | tf_op jit(solution)/shard_map/ppermute | solution.py:841
  331.5 11.5 %collective-permute-start.20 = (bf16[2,2,960,256]{3,2,1,0:T(8,128)(2,1)S(1)}, bf16[2,2,960,256]{3,2,1,0:T(8,128)(2,1)S(1)}, u32[]{:S(2)}, u32[]{:S(2)}) collective-permute-start(bf16[2,2,960,256]{3,2,1,0:T(8,128)(2,1)S(1)} %copy-done.26), channel_id=1, source_target_pairs={{0,8},{1,9},{2,10},{3,11},{4,12},{5,13},{6,14},{7,15},{8,0},{9,1},... | collective-permute-start | bytes 5898248 | tf_op jit(solution)/shard_map/ppermute | solution.py:731
  333.2 24.9 %collective-permute-start.23 = (bf16[4,480,256]{2,1,0:T(8,128)(2,1)}, bf16[4,480,256]{2,1,0:T(8,128)(2,1)}, u32[]{:S(2)}, u32[]{:S(2)}) collective-permute-start(bf16[4,480,256]{2,1,0:T(8,128)(2,1)} %get-tuple-element.374), channel_id=1, source_target_pairs={{0,16},{1,17},{2,18},{3,19},{4,20},{5,21},{6,22},{7,23},{8,24},{9,... | collective-permute-start | bytes 2949128 | tf_op jit(solution)/shard_map/ppermute | solution.py:731
  334.7 19.8 %collective-permute-start.16 = (bf16[2,256,640]{2,1,0:T(8,128)(2,1)}, bf16[2,256,640]{2,1,0:T(8,128)(2,1)}, u32[]{:S(2)}, u32[]{:S(2)}) collective-permute-start(bf16[2,256,640]{2,1,0:T(8,128)(2,1)} %get-tuple-element.350), channel_id=1, source_target_pairs={{1,0},{3,2},{5,4},{7,6},{6,7},{9,8},{11,10},{13,12},{15,14},{14,15... | collective-permute-start | bytes 1966088 | tf_op jit(solution)/shard_map/ppermute | solution.py:841
  338.6 15.9 %collective-permute-start.19 = (bf16[2,256,640]{2,1,0:T(8,128)(2,1)}, bf16[2,256,640]{2,1,0:T(8,128)(2,1)}, u32[]{:S(2)}, u32[]{:S(2)}) collective-permute-start(bf16[2,256,640]{2,1,0:T(8,128)(2,1)} %fusion.8), channel_id=1, source_target_pairs={{4,2},{5,3},{6,4},{7,5},{12,10},{13,11},{14,12},{15,13},{20,18},{2... | collective-permute-start | bytes 1966088 | tf_op jit(solution)/shard_map/ppermute | solution.py:841
  344.5 60.5 %collective-permute-start.22 = (bf16[1,2,8,120,256]{4,3,2,1,0:T(8,128)(2,1)}, bf16[1,2,8,120,256]{4,3,2,1,0:T(8,128)(2,1)}, u32[]{:S(2)}, u32[]{:S(2)}) collective-permute-start(bf16[1,2,8,120,256]{4,3,2,1,0:T(8,128)(2,1)} %get-tuple-element.373), channel_id=1, source_target_pairs={{0,16},{1,17},{2,18},{3,19},{4,20},{5,21},{6,22},{7,23},{8,24},{9,... | collective-permute-start | bytes 2949128 | tf_op jit(solution)/shard_map/ppermute | solution.py:731
  345.1 91.4 %collective-permute-start.25 = (bf16[4,480,256]{2,1,0:T(8,128)(2,1)}, bf16[4,480,256]{2,1,0:T(8,128)(2,1)}, u32[]{:S(2)}, u32[]{:S(2)}) collective-permute-start(bf16[4,480,256]{2,1,0:T(8,128)(2,1)} %get-tuple-element.395), channel_id=1, source_target_pairs={{0,1},{1,0},{2,3},{3,2},{4,5},{5,4},{6,7},{7,6},{8,9},{9,8},{10,11... | collective-permute-start | bytes 2949128 | tf_op jit(solution)/shard_map/ppermute | solution.py:731
  358.1 59.8 %collective-permute-start.21 = (bf16[2,256,640]{2,1,0:T(8,128)(2,1)S(1)}, bf16[2,256,640]{2,1,0:T(8,128)(2,1)S(1)}, u32[]{:S(2)}, u32[]{:S(2)}) collective-permute-start(bf16[2,256,640]{2,1,0:T(8,128)(2,1)S(1)} %fusion.11), channel_id=1, source_target_pairs={{2,0},{3,1},{4,2},{5,3},{6,4},{7,5},{10,8},{11,9},{12,10},{13,11},... | collective-permute-start | bytes 1966088 | tf_op jit(solution)/shard_map/ppermute | solution.py:841
  362.1 73.3 %collective-permute-start.26 = (bf16[2,480,256]{2,1,0:T(8,128)(2,1)}, bf16[2,480,256]{2,1,0:T(8,128)(2,1)}, u32[]{:S(2)}, u32[]{:S(2)}) collective-permute-start(bf16[2,480,256]{2,1,0:T(8,128)(2,1)} %get-tuple-element.396), channel_id=1, source_target_pairs={{0,2},{1,3},{2,0},{3,1},{4,6},{5,7},{6,4},{7,5},{8,10},{9,11},{10,... | collective-permute-start | bytes 1474568 | tf_op jit(solution)/shard_map/ppermute | solution.py:731
  425.3 8.9 %collective-permute-start.27 = (bf16[2,2,5,64,256]{4,3,2,1,0:T(8,128)(2,1)S(1)}, bf16[2,2,5,64,256]{4,3,2,1,0:T(8,128)(2,1)}, u32[]{:S(2)}, u32[]{:S(2)}) collective-permute-start(bf16[2,2,5,64,256]{4,3,2,1,0:T(8,128)(2,1)S(1)} %bitcast.196), channel_id=1, source_target_pairs={{0,8},{1,9},{2,10},{3,11},{4,12},{5,13},{6,14},{7,15},{8,0},{9,1},... | collective-permute-start | bytes 1966088 | tf_op jit(solution)/shard_map/ppermute | solution.py:731
  426.5 14.0 %collective-permute-start.24 = (bf16[2,4,120,256]{3,2,0,1:T(8,128)(2,1)}, bf16[2,4,120,256]{3,2,0,1:T(8,128)(2,1)}, u32[]{:S(2)}, u32[]{:S(2)}) collective-permute-start(bf16[2,4,120,256]{3,2,0,1:T(8,128)(2,1)} %fusion.17), channel_id=1, source_target_pairs={{0,1},{1,0},{2,3},{3,2},{4,5},{5,4},{6,7},{7,6},{8,9},{9,8},{10,11... | collective-permute-start | bytes 1474568 | tf_op jit(solution)/shard_map/ppermute | solution.py:731
  436.4 10.6 %collective-permute-start.29 = (bf16[1,2,8,40,256]{4,3,2,1,0:T(8,128)(2,1)S(1)}, bf16[1,2,8,40,256]{4,3,2,1,0:T(8,128)(2,1)S(1)}, u32[]{:S(2)}, u32[]{:S(2)}) collective-permute-start(bf16[1,2,8,40,256]{4,3,2,1,0:T(8,128)(2,1)S(1)} %get-tuple-element.413), channel_id=1, source_target_pairs={{0,16},{1,17},{2,18},{3,19},{4,20},{5,21},{6,22},{7,23},{8,24},{9,... | collective-permute-start | bytes 983048 | tf_op jit(solution)/shard_map/ppermute | solution.py:731
  440.5 19.4 %collective-permute-start.33 = (bf16[2,480,256]{2,1,0:T(8,128)(2,1)S(1)}, bf16[2,480,256]{2,1,0:T(8,128)(2,1)S(1)}, u32[]{:S(2)}, u32[]{:S(2)}) collective-permute-start(bf16[2,480,256]{2,1,0:T(8,128)(2,1)S(1)} %get-tuple-element.423), channel_id=1, source_target_pairs={{0,2},{1,3},{2,0},{3,1},{4,6},{5,7},{6,4},{7,5},{8,10},{9,11},{10,... | collective-permute-start | bytes 1474568 | tf_op jit(solution)/shard_map/ppermute | solution.py:731
  441.8 22.1 %collective-permute-start.32 = (bf16[2,2,120,256]{3,2,0,1:T(8,128)(2,1)S(1)}, bf16[2,2,120,256]{3,2,0,1:T(8,128)(2,1)S(1)}, u32[]{:S(2)}, u32[]{:S(2)}) collective-permute-start(bf16[2,2,120,256]{3,2,0,1:T(8,128)(2,1)S(1)} %get-tuple-element.422), channel_id=1, source_target_pairs={{0,2},{1,3},{2,0},{3,1},{4,6},{5,7},{6,4},{7,5},{8,10},{9,11},{10,... | collective-permute-start | bytes 737288 | tf_op jit(solution)/shard_map/ppermute | solution.py:731
  443.9 23.8 %collective-permute-start.36 = (bf16[1,480,256]{2,1,0:T(8,128)(2,1)S(1)}, bf16[1,480,256]{2,1,0:T(8,128)(2,1)}, u32[]{:S(2)}, u32[]{:S(2)}) collective-permute-start(bf16[1,480,256]{2,1,0:T(8,128)(2,1)S(1)} %add_convert_fusion.15), channel_id=1, source_target_pairs={{0,4},{1,5},{2,6},{3,7},{4,0},{5,1},{6,2},{7,3},{8,12},{9,13},{10,... | collective-permute-start | bytes 737288 | tf_op jit(solution)/shard_map/ppermute | solution.py:731
  447.1 16.8 %collective-permute-start.31 = (bf16[2,4,40,256]{3,2,1,0:T(8,128)(2,1)S(1)}, bf16[2,4,40,256]{3,2,1,0:T(8,128)(2,1)S(1)}, u32[]{:S(2)}, u32[]{:S(2)}) collective-permute-start(bf16[2,4,40,256]{3,2,1,0:T(8,128)(2,1)S(1)} %get-tuple-element.421), channel_id=1, source_target_pairs={{0,1},{1,0},{2,3},{3,2},{4,5},{5,4},{6,7},{7,6},{8,9},{9,8},{10,11... | collective-permute-start | bytes 491528 | tf_op jit(solution)/shard_map/ppermute | solution.py:731
  448.0 19.5 %collective-permute-start.30 = (f32[3,4,1,256]{3,2,1,0:T(1,128)S(1)}, f32[3,4,1,256]{3,2,1,0:T(1,128)S(1)}, u32[]{:S(2)}, u32[]{:S(2)}) collective-permute-start(f32[3,4,1,256]{3,2,1,0:T(1,128)S(1)} %fusion.49), channel_id=1, source_target_pairs={{0,16},{1,17},{2,18},{3,19},{4,20},{5,21},{6,22},{7,23},{8,24},{9,... | collective-permute-start | bytes 36872 | tf_op jit(solution)/shard_map/ppermute | solution.py:731
  464.1 18.3 %collective-permute-start.39 = (bf16[1,480,256]{2,1,0:T(8,128)(2,1)S(1)}, bf16[1,480,256]{2,1,0:T(8,128)(2,1)}, u32[]{:S(2)}, u32[]{:S(2)}) collective-permute-start(bf16[1,480,256]{2,1,0:T(8,128)(2,1)S(1)} %add_convert_fusion.12), channel_id=1, source_target_pairs={{0,4},{1,5},{2,6},{3,7},{4,0},{5,1},{6,2},{7,3},{8,12},{9,13},{10,... | collective-permute-start | bytes 737288 | tf_op jit(solution)/shard_map/ppermute | solution.py:731
  467.5 17.0 %collective-permute-start.38 = (bf16[2,1,120,256]{3,2,0,1:T(8,128)(2,1)S(1)}, bf16[2,1,120,256]{3,2,0,1:T(8,128)(2,1)}, u32[]{:S(2)}, u32[]{:S(2)}) collective-permute-start(bf16[2,1,120,256]{3,2,0,1:T(8,128)(2,1)S(1)} %fusion.27), channel_id=1, source_target_pairs={{0,4},{1,5},{2,6},{3,7},{4,0},{5,1},{6,2},{7,3},{8,12},{9,13},{10,... | collective-permute-start | bytes 368648 | tf_op jit(solution)/shard_map/ppermute | solution.py:731
  469.5 20.1 %collective-permute-start.41 = (bf16[2,1,40,256]{3,2,0,1:T(8,128)(2,1)}, bf16[2,1,40,256]{3,2,0,1:T(8,128)(2,1)}, u32[]{:S(2)}, u32[]{:S(2)}) collective-permute-start(bf16[2,1,40,256]{3,2,0,1:T(8,128)(2,1)} %fusion.36), channel_id=1, source_target_pairs={{0,4},{1,5},{2,6},{3,7},{4,0},{5,1},{6,2},{7,3},{8,12},{9,13},{10,... | collective-permute-start | bytes 122888 | tf_op jit(solution)/shard_map/ppermute | solution.py:731
  475.2 9.7 %collective-permute-start.37 = (f32[3,4,1,256]{3,2,1,0:T(1,128)S(1)}, f32[3,4,1,256]{3,2,1,0:T(1,128)S(1)}, u32[]{:S(2)}, u32[]{:S(2)}) collective-permute-start(f32[3,4,1,256]{3,2,1,0:T(1,128)S(1)} %add.302), channel_id=1, source_target_pairs={{0,2},{1,3},{2,0},{3,1},{4,6},{5,7},{6,4},{7,5},{8,10},{9,11},{10,... | collective-permute-start | bytes 36872 | tf_op jit(solution)/shard_map/ppermute | solution.py:731
  (42 other events, 215.5 us)
Sparse Core Ops, SparseCore 0:
  11.5 65.2 all-gather.4
  79.7 120.2 all-gather.6

commit v5 on v4

--- a/solution.py
+++ b/solution.py
@@ -376,7 +376,7 @@
 
 def out_project(o, wo_pad, hid4, gain):
     parts, tokens, width = hid4.shape
-    rows = 256
+    rows = min(512, tokens)
     block = pl.BlockSpec((parts, rows, width), lambda i: (0, i, 0))
     column = pl.BlockSpec((rows, 1), lambda i: (i, 0))
     return pl.pallas_call(
@@ -558,7 +558,7 @@
 
 def out_back(ag4, wo_pad):
     parts, tokens, width = ag4.shape
-    rows = 256
+    rows = min(512, tokens)
     return pl.pallas_call(
         out_back_kernel,
         grid=(tokens // rows,),

time: 517 us -> 518 us (level)
  no operation moved by 1% of the time
where the time goes in v5:
time: 518 us; the launch traced here: 508 us
  Pallas kernels  157 us (30%)
  waiting for transfers between devices  135 us (26%)
  starting transfers between devices  93.8 us (18%)
  other arithmetic  57.8 us (11%)
  local copies, waits for them, and re-layouts  48.9 us (9%)
  between operations  15.4 us (3%)
    ppermute x30, starting transfers between devices, swap(): lax.ppermute(self.clock.at(array), AXES, [(i, i ^ flip) for i in range(se...  77 us
    all_gather x1, waiting for transfers between devices, shards(): large_all = lax.all_gather(clock.after(large), AXES, axis=0, tiled=False)  53.3 us
    pallas_call x2, Pallas kernels, ffn(): pl.pallas_call(ffn_kernel, grid_spec=pltpu.PrefetchScalarGridSpec(num_sca...  42.8 us
    ppermute x30, waiting for transfers between devices, swap(): lax.ppermute(self.clock.at(array), AXES, [(i, i ^ flip) for i in range(se...  40.9 us
    ppermute x12, waiting for transfers between devices, move(): return lax.ppermute(self.clock.at(array), AXES, pairs)  40.6 us
    pallas_call x1, Pallas kernels, attention_backward(): pl.pallas_call(functools.partial(backward_kernel, slots), grid_spec=pltpu...  37.5 us
    convert_element_type x18, other arithmetic, add(): return (mine.astype(F32) + other.astype(F32)).astype(dtype)  27.6 us
    unnamed x74, local copies, waits for them, and re-layouts  21.8 us
  transfers between devices with their start and end apart: 44, of which 17 were waited for; matrix products, arithmetic and copies ran while one was open for 16% of the time, Pallas kernels for 27%

profile of v5, /device:TPU:0, one launch (start us, length us, event | category | flops | bytes accessed | tf_op | source)
XLA Modules:
  0.0 508.1 jit_solution(5480864096952410553)
XLA Ops:
  10.5 4.1 collective-permute-start
  34.3 4.6 first_norm.1
  41.1 5.0 collective-permute-done.2
  50.3 4.9 collective-permute-done.3
  60.0 4.0 kv_project.1.refs_0_
  65.7 20.4 %collective-permute-done.5 = bf16[2,272,640]{2,1,0:T(8,128)(2,1)S(1)} collective-permute-done((bf16[2,272,640]{2,1,0:T(8,128)(2,1)}, bf16[2,272,640]{2,1,0:T(8,128)(2,1)S(1)}, u32[]{:S(2)}, u32[]{:S(2)}) %collective-permute-start.5) | collective-permute-done | bytes 696352 | tf_op jit(solution)/shard_map/ppermute | solution.py:841
  88.1 4.4 collective-permute-start.7
  97.9 6.1 %q_project.1.q_ref = bf16[512,1920]{1,0:T(8,128)(2,1)} custom-call(bf16[4,512,256]{2,1,0:T(8,128)(2,1)} %get-tuple-element.251.xn_ref, bf16[4,1920,256]{2,1,0:T(8,128)(2,1)} %bitcast.167, f32[512,128]{1,0:T(8,128)} %get-tuple-element.552.cos_ref, f32[512,128]{1,0:T(8,128)} %get-tuple-element.549.sin_ref), custom_call_target="tpu_custom_call" | custom-call | flops 1887436800 | bytes 5898240 | tf_op jit(solution)/shard_map/q_project/pallas_call | solution.py:157
  104.0 3.7 collective-permute-done.7.refs_1_
  118.5 20.8 %attention_forward.1 = (bf16[512,1920]{1,0:T(8,128)(2,1)}, f32[2,5,1,768]{3,2,1,0:T(1,128)}) custom-call(s32[6]{0:T(128)} %stack.100.slot_ref, bf16[512,1920]{1,0:T(8,128)(2,1)} %q_project.1.q_ref, f32[2,1,256]{2,1,0:T(1,128)} %reshape.337.seg_ref, bf16[2,272,640]{2,1,0:T(8,128)(2,1)} %kv_project.1.refs_0_, ...), custom_call_target="tpu_custom_call" | custom-call | flops 6039797760 | bytes 7864320 | tf_op jit(solution)/shard_map/attention_forward/pallas_call | solution.py:270
  139.3 7.3 %out_project.1 = (f32[4,512,256]{2,1,0:T(8,128)}, bf16[4,512,256]{2,1,0:T(8,128)(2,1)}, f32[512,1]{1,0:T(8,128)}) custom-call(bf16[512,1920]{1,0:T(8,128)(2,1)} %get-tuple-element.289.o_ref, bf16[4,1920,256]{2,1,0:T(8,128)(2,1)} %bitcast.177, bf16[4,512,256]{2,1,0:T(8,128)(2,1)} %pad.41.hid_ref, f32[4,1,256]{2,1,0:T(1,128)} %pad_convert_fusion.gain_ref), custom_call_target="tpu_custom_call" | custom-call | flops 1887436800 | bytes 7864320 | tf_op jit(solution)/shard_map/out_project/pallas_call | solution.py:382
  146.6 53.3 %all-gather.7.cloned.1.call-done = bf16[30720,256]{1,0:T(8,128)(2,1)} async-done(((bf16[960,256]{1,0:T(8,128)(2,1)}), bf16[30720,256]{1,0:T(8,128)(2,1)}) %all-gather.7.cloned.1.call-update) | async-done | bytes 15728656 | tf_op jit(solution)/shard_map/all_gather | solution.py:997
  199.9 21.5 %ffn.2 = (f32[4,512,256]{2,1,0:T(8,128)}, f32[4,512,256]{2,1,0:T(8,128)}, bf16[2,2,4,480,256]{4,3,2,1,0:T(8,128)(2,1)}, bf16[2,2,4,480,256]{4,3,2,1,0:T(8,128)(2,1)}) custom-call(s32[3]{0:T(128)} %pad_add_fusion.meta_ref, bf16[4,512,256]{2,1,0:T(8,128)(2,1)} %get-tuple-element.293.x_ref, bf16[4,512,256]{2,1,0:T(8,128)(2,1)} %get-tuple-element.294.fg_ref, ...), custom_call_target="tpu_custom_call" | custom-call | flops 11324620800 | bytes 22609920 | tf_op jit(solution)/shard_map/ffn/pallas_call | solution.py:464
  221.7 21.3 %ffn.3 = (f32[4,512,256]{2,1,0:T(8,128)}, f32[4,512,256]{2,1,0:T(8,128)}, bf16[2,2,4,480,256]{4,3,2,1,0:T(8,128)(2,1)}, bf16[2,2,4,480,256]{4,3,2,1,0:T(8,128)(2,1)}) custom-call(s32[3]{0:T(128)} %pad_add_fusion.meta_ref, bf16[4,512,256]{2,1,0:T(8,128)(2,1)} %get-tuple-element.293.x_ref, bf16[4,512,256]{2,1,0:T(8,128)(2,1)} %get-tuple-element.294.fg_ref, ...), custom_call_target="tpu_custom_call" | custom-call | flops 11324620800 | bytes 22609920 | tf_op jit(solution)/shard_map/ffn/pallas_call | solution.py:464
  250.7 4.7 fusion
  255.5 8.5 %middle_step.1 = (bf16[512,960]{1,0:T(8,128)(2,1)}, f32[4,512,256]{2,1,0:T(8,128)}, bf16[4,512,256]{2,1,0:T(8,128)(2,1)}, f32[4,1,256]{2,1,0:T(1,128)}, f32[4,1,256]{2,1,0:T(1,128)}) custom-call(f32[4,512,256]{2,1,0:T(8,128)} %get-tuple-element.290.mid_ref, bf16[4,512,256]{2,1,0:T(8,128)(2,1)} %pad.41.hid_ref, bf16[4,512,256]{2,1,0:T(8,128)(2,1)} %pad.42.cot_ref, ...), custom_call_target="tpu_custom_call" | custom-call | flops 14745600 | bytes 17694720 | tf_op jit(solution)/shard_map/middle_step/pallas_call | solution.py:529
  264.0 5.8 %fusion.1 = (bf16[8,480,256]{2,1,0:T(8,128)(2,1)S(1)}, bf16[8,480,256]{2,1,0:T(8,128)(2,1)}) fusion(bf16[1,2,4,480,256]{4,3,2,1,0:T(8,128)(2,1)} %get-tuple-element.509, bf16[16,480,256]{2,1,0:T(8,128)(2,1)} %bitcast.45, bf16[1,2,4,480,256]{4,3,2,1,0:T(8,128)(2,1)} %get-tuple-element.510), kind=kLoop, calls=%fused_computation.4 | loop fusion | flops 7864320 | bytes 11796480 | tf_op jit(solution)/shard_map/convert_element_type | solution.py:716
  272.3 6.1 %out_back.1.do_ref = bf16[512,1920]{1,0:T(8,128)(2,1)} custom-call(bf16[4,512,256]{2,1,0:T(8,128)(2,1)} %get-tuple-element.317.ag_ref, bf16[4,1920,256]{2,1,0:T(8,128)(2,1)} %bitcast.178), custom_call_target="tpu_custom_call" | custom-call | flops 1887436800 | bytes 5898240 | tf_op jit(solution)/shard_map/out_back/pallas_call | solution.py:562
  278.4 37.5 %attention_backward.1 = (bf16[512,1920]{1,0:T(8,128)(2,1)}, bf16[2,256,640]{2,1,0:T(8,128)(2,1)}, bf16[2,256,640]{2,1,0:T(8,128)(2,1)}, bf16[2,256,640]{2,1,0:T(...) custom-call(s32[6]{0:T(128)} %stack.100.slot_ref, ...), custom_call_target="tpu_custom_call" | custom-call | flops 15099494400 | bytes 15728640 | tf_op jit(solution)/shard_map/attention_backward/pallas_call | solution.py:342
  317.4 9.6 %qo_back.1 = (bf16[2,2,960,256]{3,2,1,0:T(8,128)(2,1)}, bf16[2,2,960,256]{3,2,1,0:T(8,128)(2,1)}, f32[4,512,256]{2,1,0:T(8,128)}) custom-call(s32[1]{0:T(128)} %bitcast.35.meta_ref, bf16[512,1920]{1,0:T(8,128)(2,1)} %get-tuple-element.328.dq_ref, bf16[4,512,256]{2,1,0:T(8,128)(2,1)} %get-tuple-element.251.xn_ref, bf16[4,1920,256]{2,1,0:T(8,128)(2,1)} %bitcast.168, ...), custom_call_target="tpu_custom_call" | custom-call | flops 3774873600 | bytes 13762560 | tf_op jit(solution)/shard_map/qo_back/pallas_call | solution.py:598
  327.0 3.4 add_convert_fusion.1
  345.6 3.5 collective-permute-start.25
  349.1 5.6 %collective-permute-done.16 = bf16[2,256,640]{2,1,0:T(8,128)(2,1)} collective-permute-done((bf16[2,256,640]{2,1,0:T(8,128)(2,1)}, bf16[2,256,640]{2,1,0:T(8,128)(2,1)}, u32[]{:S(2)}, u32[]{:S(2)}) %collective-permute-start.16) | collective-permute-done | bytes 655392 | tf_op jit(solution)/shard_map/ppermute | solution.py:841
  362.1 43.5 %collective-permute-start.26 = (bf16[2,480,256]{2,1,0:T(8,128)(2,1)}, bf16[2,480,256]{2,1,0:T(8,128)(2,1)}, u32[]{:S(2)}, u32[]{:S(2)}) collective-permute-start(bf16[2,480,256]{2,1,0:T(8,128)(2,1)} %get-tuple-element.396), channel_id=1, source_target_pairs={{0,2},{1,3},{2,0},{3,1},{4,6},{5,7},{6,4},{7,5},{8,10},{9,11},{10,... | collective-permute-start | bytes 1474568 | tf_op jit(solution)/shard_map/ppermute | solution.py:731
  408.0 10.8 %collective-permute-done.21 = bf16[2,256,640]{2,1,0:T(8,128)(2,1)S(1)} collective-permute-done((bf16[2,256,640]{2,1,0:T(8,128)(2,1)S(1)}, bf16[2,256,640]{2,1,0:T(8,128)(2,1)S(1)}, u32[]{:S(2)}, u32[]{:S(2)}) %collective-permute-start.21) | collective-permute-done | bytes 655392 | tf_op jit(solution)/shard_map/ppermute | solution.py:841
  421.0 4.0 kv_back.1
  428.0 6.1 %final_step.1 = (f32[512,960]{1,0:T(8,128)}, f32[4,1,256]{2,1,0:T(1,128)}) custom-call(f32[4,512,256]{2,1,0:T(8,128)} %get-tuple-element.341.xg_ref, bf16[512,640]{1,0:T(8,128)(2,1)} %get-tuple-element.387.kvb_ref, bf16[4,640,256]{2,1,0:T(8,128)(2,1)} %bitcast.170, bf16[4,512,256]{2,1,0:T(8,128)(2,1)} %pad.41.hid_ref, ...), custom_call_target="tpu_custom_call" | custom-call | flops 629145600 | bytes 9830400 | tf_op jit(solution)/shard_map/final_step/pallas_call | solution.py:679
  444.7 3.2 collective-permute-start.36
  449.5 11.2 %collective-permute-done.33 = bf16[2,480,256]{2,1,0:T(8,128)(2,1)S(1)} collective-permute-done((bf16[2,480,256]{2,1,0:T(8,128)(2,1)S(1)}, bf16[2,480,256]{2,1,0:T(8,128)(2,1)S(1)}, u32[]{:S(2)}, u32[]{:S(2)}) %collective-permute-start.33) | collective-permute-done | bytes 491552 | tf_op jit(solution)/shard_map/ppermute | solution.py:731
  461.6 3.1 collective-permute-done.32
  464.9 3.5 collective-permute-start.39
  477.6 5.7 %collective-permute-done.39 = bf16[1,480,256]{2,1,0:T(8,128)(2,1)} collective-permute-done((bf16[1,480,256]{2,1,0:T(8,128)(2,1)S(1)}, bf16[1,480,256]{2,1,0:T(8,128)(2,1)}, u32[]{:S(2)}, u32[]{:S(2)}) %collective-permute-start.39) | collective-permute-done | bytes 245792 | tf_op jit(solution)/shard_map/ppermute | solution.py:731
  (247 shorter events, 135.5 us)
Async XLA Ops:
  7.2 86.1 %all-gather.5.cloned.1.call-start = ((), (), s32[]{:S(2)}) async-start(), calls=%async_computation | async-start | bytes 4055040 | tf_op jit(solution)/shard_map/all_gather | solution.py:984
  9.7 190.3 %all-gather.7.cloned.1.call-start = ((), (), s32[]{:S(2)}) async-start(), calls=%async_computation.1 | async-start | bytes 16220160 | tf_op jit(solution)/shard_map/all_gather | solution.py:997
  10.5 21.5 %collective-permute-start = (bf16[80,256]{1,0:T(8,128)(2,1)S(1)}, bf16[80,256]{1,0:T(8,128)(2,1)S(1)}, u32[]{:S(2)}, u32[]{:S(2)}) collective-permute-start(bf16[80,256]{1,0:T(8,128)(2,1)S(1)} %fusion.37), channel_id=1, source_target_pairs={{0,4},{1,5},{2,6},{3,7},{4,0},{5,1},{6,2},{7,3},{8,12},{9,13},{10,... | collective-permute-start | bytes 122888 | tf_op jit(solution)/shard_map/ppermute | solution.py:731
  46.2 9.0 %collective-permute-start.3 = (bf16[2,2,2,80,256]{4,3,0,1,2:T(8,128)(2,1)S(1)}, bf16[2,2,2,80,256]{4,3,0,1,2:T(8,128)(2,1)S(1)}, u32[]{:S(2)}, u32[]{:S(2)}) collective-permute-start(bf16[2,2,2,80,256]{4,3,0,1,2:T(8,128)(2,1)S(1)} %pad_maximum_fusion.5), channel_id=1, source_target_pairs={{0,16},{1,17},{2,18},{3,19},{4,20},{5,21},{6,22},{7,23},{8,24},{9,... | collective-permute-start | bytes 983048 | tf_op jit(solution)/shard_map/ppermute | solution.py:731
  64.0 22.1 %collective-permute-start.5 = (bf16[2,272,640]{2,1,0:T(8,128)(2,1)}, bf16[2,272,640]{2,1,0:T(8,128)(2,1)S(1)}, u32[]{:S(2)}, u32[]{:S(2)}) collective-permute-start(bf16[2,272,640]{2,1,0:T(8,128)(2,1)} %kv_project.1.refs_0_), channel_id=1, source_target_pairs={{0,2},{1,3},{2,4},{3,5},{4,6},{5,7},{8,10},{9,11},{10,12},{11,13},... | collective-permute-start | bytes 2088968 | tf_op jit(solution)/shard_map/ppermute | solution.py:841
  88.1 19.7 %collective-permute-start.7 = (bf16[2,272,640]{2,1,0:T(8,128)(2,1)}, bf16[2,272,640]{2,1,0:T(8,128)(2,1)}, u32[]{:S(2)}, u32[]{:S(2)}) collective-permute-start(bf16[2,272,640]{2,1,0:T(8,128)(2,1)} %broadcast_select_fusion.3), channel_id=1, source_target_pairs={{0,1},{2,3},{4,5},{6,7},{7,6},{8,9},{10,11},{12,13},{14,15},{15,14... | collective-permute-start | bytes 2088968 | tf_op jit(solution)/shard_map/ppermute | solution.py:841
  92.5 15.3 %collective-permute-start.6 = (bf16[2,272,640]{2,1,0:T(8,128)(2,1)S(1)}, bf16[2,272,640]{2,1,0:T(8,128)(2,1)S(1)}, u32[]{:S(2)}, u32[]{:S(2)}) collective-permute-start(bf16[2,272,640]{2,1,0:T(8,128)(2,1)S(1)} %collective-permute-done.5), channel_id=1, source_target_pairs={{2,4},{3,5},{4,6},{5,7},{10,12},{11,13},{12,14},{13,15},{18,20},{1... | collective-permute-start | bytes 2088968 | tf_op jit(solution)/shard_map/ppermute | solution.py:841
  221.4 27.3 %collective-permute-start.11 = (bf16[2,2,4,480,256]{4,3,2,1,0:T(8,128)(2,1)}, bf16[2,2,4,480,256]{4,3,2,1,0:T(8,128)(2,1)S(1)}, u32[]{:S(2)}, u32[]{:S(2)}) collective-permute-start(bf16[2,2,4,480,256]{4,3,2,1,0:T(8,128)(2,1)} %get-tuple-element.301), channel_id=1, source_target_pairs={{0,8},{1,9},{2,10},{3,11},{4,12},{5,13},{6,14},{7,15},{8,0},{9,1},... | collective-permute-start | bytes 11796488 | tf_op jit(solution)/shard_map/ppermute | solution.py:731
  243.0 20.9 %collective-permute-start.12 = (bf16[2,2,4,480,256]{4,3,2,1,0:T(8,128)(2,1)}, bf16[2,2,4,480,256]{4,3,2,1,0:T(8,128)(2,1)}, u32[]{:S(2)}, u32[]{:S(2)}) collective-permute-start(bf16[2,2,4,480,256]{4,3,2,1,0:T(8,128)(2,1)} %get-tuple-element.319), channel_id=1, source_target_pairs={{0,8},{1,9},{2,10},{3,11},{4,12},{5,13},{6,14},{7,15},{8,0},{9,1},... | collective-permute-start | bytes 11796488 | tf_op jit(solution)/shard_map/ppermute | solution.py:731
  269.8 46.0 %collective-permute-start.13 = (bf16[8,480,256]{2,1,0:T(8,128)(2,1)}, bf16[8,480,256]{2,1,0:T(8,128)(2,1)}, u32[]{:S(2)}, u32[]{:S(2)}) collective-permute-start(bf16[8,480,256]{2,1,0:T(8,128)(2,1)} %get-tuple-element.330), channel_id=1, source_target_pairs={{0,1},{1,0},{2,3},{3,2},{4,5},{5,4},{6,7},{7,6},{8,9},{9,8},{10,11... | collective-permute-start | bytes 5898248 | tf_op jit(solution)/shard_map/ppermute | solution.py:731
  270.4 45.5 %collective-permute-start.14 = (bf16[8,480,256]{2,1,0:T(8,128)(2,1)}, bf16[8,480,256]{2,1,0:T(8,128)(2,1)}, u32[]{:S(2)}, u32[]{:S(2)}) collective-permute-start(bf16[8,480,256]{2,1,0:T(8,128)(2,1)} %get-tuple-element.335), channel_id=1, source_target_pairs={{0,16},{1,17},{2,18},{3,19},{4,20},{5,21},{6,22},{7,23},{8,24},{9,... | collective-permute-start | bytes 5898248 | tf_op jit(solution)/shard_map/ppermute | solution.py:731
  315.9 14.5 %collective-permute-start.15 = (bf16[2,256,640]{2,1,0:T(8,128)(2,1)}, bf16[2,256,640]{2,1,0:T(8,128)(2,1)}, u32[]{:S(2)}, u32[]{:S(2)}) collective-permute-start(bf16[2,256,640]{2,1,0:T(8,128)(2,1)} %get-tuple-element.345), channel_id=1, source_target_pairs={{5,4},{4,5},{7,6},{6,7},{13,12},{12,13},{15,14},{14,15},{21,20},{2... | collective-permute-start | bytes 1966088 | tf_op jit(solution)/shard_map/ppermute | solution.py:841
  331.8 11.7 %collective-permute-start.20 = (bf16[2,2,960,256]{3,2,1,0:T(8,128)(2,1)S(1)}, bf16[2,2,960,256]{3,2,1,0:T(8,128)(2,1)S(1)}, u32[]{:S(2)}, u32[]{:S(2)}) collective-permute-start(bf16[2,2,960,256]{3,2,1,0:T(8,128)(2,1)S(1)} %copy-done.26), channel_id=1, source_target_pairs={{0,8},{1,9},{2,10},{3,11},{4,12},{5,13},{6,14},{7,15},{8,0},{9,1},... | collective-permute-start | bytes 5898248 | tf_op jit(solution)/shard_map/ppermute | solution.py:731
  333.4 24.9 %collective-permute-start.23 = (bf16[4,480,256]{2,1,0:T(8,128)(2,1)}, bf16[4,480,256]{2,1,0:T(8,128)(2,1)}, u32[]{:S(2)}, u32[]{:S(2)}) collective-permute-start(bf16[4,480,256]{2,1,0:T(8,128)(2,1)} %get-tuple-element.374), channel_id=1, source_target_pairs={{0,16},{1,17},{2,18},{3,19},{4,20},{5,21},{6,22},{7,23},{8,24},{9,... | collective-permute-start | bytes 2949128 | tf_op jit(solution)/shard_map/ppermute | solution.py:731
  334.9 19.8 %collective-permute-start.16 = (bf16[2,256,640]{2,1,0:T(8,128)(2,1)}, bf16[2,256,640]{2,1,0:T(8,128)(2,1)}, u32[]{:S(2)}, u32[]{:S(2)}) collective-permute-start(bf16[2,256,640]{2,1,0:T(8,128)(2,1)} %get-tuple-element.350), channel_id=1, source_target_pairs={{1,0},{3,2},{5,4},{7,6},{6,7},{9,8},{11,10},{13,12},{15,14},{14,15... | collective-permute-start | bytes 1966088 | tf_op jit(solution)/shard_map/ppermute | solution.py:841
  338.8 15.9 %collective-permute-start.19 = (bf16[2,256,640]{2,1,0:T(8,128)(2,1)}, bf16[2,256,640]{2,1,0:T(8,128)(2,1)}, u32[]{:S(2)}, u32[]{:S(2)}) collective-permute-start(bf16[2,256,640]{2,1,0:T(8,128)(2,1)} %fusion.8), channel_id=1, source_target_pairs={{4,2},{5,3},{6,4},{7,5},{12,10},{13,11},{14,12},{15,13},{20,18},{2... | collective-permute-start | bytes 1966088 | tf_op jit(solution)/shard_map/ppermute | solution.py:841
  345.0 60.7 %collective-permute-start.22 = (bf16[1,2,8,120,256]{4,3,2,1,0:T(8,128)(2,1)}, bf16[1,2,8,120,256]{4,3,2,1,0:T(8,128)(2,1)}, u32[]{:S(2)}, u32[]{:S(2)}) collective-permute-start(bf16[1,2,8,120,256]{4,3,2,1,0:T(8,128)(2,1)} %get-tuple-element.373), channel_id=1, source_target_pairs={{0,16},{1,17},{2,18},{3,19},{4,20},{5,21},{6,22},{7,23},{8,24},{9,... | collective-permute-start | bytes 2949128 | tf_op jit(solution)/shard_map/ppermute | solution.py:731
  345.6 91.8 %collective-permute-start.25 = (bf16[4,480,256]{2,1,0:T(8,128)(2,1)}, bf16[4,480,256]{2,1,0:T(8,128)(2,1)}, u32[]{:S(2)}, u32[]{:S(2)}) collective-permute-start(bf16[4,480,256]{2,1,0:T(8,128)(2,1)} %get-tuple-element.395), channel_id=1, source_target_pairs={{0,1},{1,0},{2,3},{3,2},{4,5},{5,4},{6,7},{7,6},{8,9},{9,8},{10,11... | collective-permute-start | bytes 2949128 | tf_op jit(solution)/shard_map/ppermute | solution.py:731
  358.4 60.4 %collective-permute-start.21 = (bf16[2,256,640]{2,1,0:T(8,128)(2,1)S(1)}, bf16[2,256,640]{2,1,0:T(8,128)(2,1)S(1)}, u32[]{:S(2)}, u32[]{:S(2)}) collective-permute-start(bf16[2,256,640]{2,1,0:T(8,128)(2,1)S(1)} %fusion.11), channel_id=1, source_target_pairs={{2,0},{3,1},{4,2},{5,3},{6,4},{7,5},{10,8},{11,9},{12,10},{13,11},... | collective-permute-start | bytes 1966088 | tf_op jit(solution)/shard_map/ppermute | solution.py:841
  362.1 74.2 %collective-permute-start.26 = (bf16[2,480,256]{2,1,0:T(8,128)(2,1)}, bf16[2,480,256]{2,1,0:T(8,128)(2,1)}, u32[]{:S(2)}, u32[]{:S(2)}) collective-permute-start(bf16[2,480,256]{2,1,0:T(8,128)(2,1)} %get-tuple-element.396), channel_id=1, source_target_pairs={{0,2},{1,3},{2,0},{3,1},{4,6},{5,7},{6,4},{7,5},{8,10},{9,11},{10,... | collective-permute-start | bytes 1474568 | tf_op jit(solution)/shard_map/ppermute | solution.py:731
  426.1 8.9 %collective-permute-start.27 = (bf16[2,2,5,64,256]{4,3,2,1,0:T(8,128)(2,1)S(1)}, bf16[2,2,5,64,256]{4,3,2,1,0:T(8,128)(2,1)}, u32[]{:S(2)}, u32[]{:S(2)}) collective-permute-start(bf16[2,2,5,64,256]{4,3,2,1,0:T(8,128)(2,1)S(1)} %bitcast.196), channel_id=1, source_target_pairs={{0,8},{1,9},{2,10},{3,11},{4,12},{5,13},{6,14},{7,15},{8,0},{9,1},... | collective-permute-start | bytes 1966088 | tf_op jit(solution)/shard_map/ppermute | solution.py:731
  427.4 14.0 %collective-permute-start.24 = (bf16[2,4,120,256]{3,2,0,1:T(8,128)(2,1)}, bf16[2,4,120,256]{3,2,0,1:T(8,128)(2,1)}, u32[]{:S(2)}, u32[]{:S(2)}) collective-permute-start(bf16[2,4,120,256]{3,2,0,1:T(8,128)(2,1)} %fusion.17), channel_id=1, source_target_pairs={{0,1},{1,0},{2,3},{3,2},{4,5},{5,4},{6,7},{7,6},{8,9},{9,8},{10,11... | collective-permute-start | bytes 1474568 | tf_op jit(solution)/shard_map/ppermute | solution.py:731
  437.3 10.6 %collective-permute-start.29 = (bf16[1,2,8,40,256]{4,3,2,1,0:T(8,128)(2,1)S(1)}, bf16[1,2,8,40,256]{4,3,2,1,0:T(8,128)(2,1)S(1)}, u32[]{:S(2)}, u32[]{:S(2)}) collective-permute-start(bf16[1,2,8,40,256]{4,3,2,1,0:T(8,128)(2,1)S(1)} %get-tuple-element.413), channel_id=1, source_target_pairs={{0,16},{1,17},{2,18},{3,19},{4,20},{5,21},{6,22},{7,23},{8,24},{9,... | collective-permute-start | bytes 983048 | tf_op jit(solution)/shard_map/ppermute | solution.py:731
  441.4 19.4 %collective-permute-start.33 = (bf16[2,480,256]{2,1,0:T(8,128)(2,1)S(1)}, bf16[2,480,256]{2,1,0:T(8,128)(2,1)S(1)}, u32[]{:S(2)}, u32[]{:S(2)}) collective-permute-start(bf16[2,480,256]{2,1,0:T(8,128)(2,1)S(1)} %get-tuple-element.423), channel_id=1, source_target_pairs={{0,2},{1,3},{2,0},{3,1},{4,6},{5,7},{6,4},{7,5},{8,10},{9,11},{10,... | collective-permute-start | bytes 1474568 | tf_op jit(solution)/shard_map/ppermute | solution.py:731
  442.6 22.1 %collective-permute-start.32 = (bf16[2,2,120,256]{3,2,0,1:T(8,128)(2,1)S(1)}, bf16[2,2,120,256]{3,2,0,1:T(8,128)(2,1)S(1)}, u32[]{:S(2)}, u32[]{:S(2)}) collective-permute-start(bf16[2,2,120,256]{3,2,0,1:T(8,128)(2,1)S(1)} %get-tuple-element.422), channel_id=1, source_target_pairs={{0,2},{1,3},{2,0},{3,1},{4,6},{5,7},{6,4},{7,5},{8,10},{9,11},{10,... | collective-permute-start | bytes 737288 | tf_op jit(solution)/shard_map/ppermute | solution.py:731
  444.7 23.8 %collective-permute-start.36 = (bf16[1,480,256]{2,1,0:T(8,128)(2,1)S(1)}, bf16[1,480,256]{2,1,0:T(8,128)(2,1)}, u32[]{:S(2)}, u32[]{:S(2)}) collective-permute-start(bf16[1,480,256]{2,1,0:T(8,128)(2,1)S(1)} %add_convert_fusion.15), channel_id=1, source_target_pairs={{0,4},{1,5},{2,6},{3,7},{4,0},{5,1},{6,2},{7,3},{8,12},{9,13},{10,... | collective-permute-start | bytes 737288 | tf_op jit(solution)/shard_map/ppermute | solution.py:731
  448.0 16.8 %collective-permute-start.31 = (bf16[2,4,40,256]{3,2,1,0:T(8,128)(2,1)S(1)}, bf16[2,4,40,256]{3,2,1,0:T(8,128)(2,1)S(1)}, u32[]{:S(2)}, u32[]{:S(2)}) collective-permute-start(bf16[2,4,40,256]{3,2,1,0:T(8,128)(2,1)S(1)} %get-tuple-element.421), channel_id=1, source_target_pairs={{0,1},{1,0},{2,3},{3,2},{4,5},{5,4},{6,7},{7,6},{8,9},{9,8},{10,11... | collective-permute-start | bytes 491528 | tf_op jit(solution)/shard_map/ppermute | solution.py:731
  448.9 19.5 %collective-permute-start.30 = (f32[3,4,1,256]{3,2,1,0:T(1,128)S(1)}, f32[3,4,1,256]{3,2,1,0:T(1,128)S(1)}, u32[]{:S(2)}, u32[]{:S(2)}) collective-permute-start(f32[3,4,1,256]{3,2,1,0:T(1,128)S(1)} %fusion.49), channel_id=1, source_target_pairs={{0,16},{1,17},{2,18},{3,19},{4,20},{5,21},{6,22},{7,23},{8,24},{9,... | collective-permute-start | bytes 36872 | tf_op jit(solution)/shard_map/ppermute | solution.py:731
  464.9 18.3 %collective-permute-start.39 = (bf16[1,480,256]{2,1,0:T(8,128)(2,1)S(1)}, bf16[1,480,256]{2,1,0:T(8,128)(2,1)}, u32[]{:S(2)}, u32[]{:S(2)}) collective-permute-start(bf16[1,480,256]{2,1,0:T(8,128)(2,1)S(1)} %add_convert_fusion.12), channel_id=1, source_target_pairs={{0,4},{1,5},{2,6},{3,7},{4,0},{5,1},{6,2},{7,3},{8,12},{9,13},{10,... | collective-permute-start | bytes 737288 | tf_op jit(solution)/shard_map/ppermute | solution.py:731
  468.4 17.0 %collective-permute-start.38 = (bf16[2,1,120,256]{3,2,0,1:T(8,128)(2,1)S(1)}, bf16[2,1,120,256]{3,2,0,1:T(8,128)(2,1)}, u32[]{:S(2)}, u32[]{:S(2)}) collective-permute-start(bf16[2,1,120,256]{3,2,0,1:T(8,128)(2,1)S(1)} %fusion.27), channel_id=1, source_target_pairs={{0,4},{1,5},{2,6},{3,7},{4,0},{5,1},{6,2},{7,3},{8,12},{9,13},{10,... | collective-permute-start | bytes 368648 | tf_op jit(solution)/shard_map/ppermute | solution.py:731
  470.3 20.1 %collective-permute-start.41 = (bf16[2,1,40,256]{3,2,0,1:T(8,128)(2,1)}, bf16[2,1,40,256]{3,2,0,1:T(8,128)(2,1)}, u32[]{:S(2)}, u32[]{:S(2)}) collective-permute-start(bf16[2,1,40,256]{3,2,0,1:T(8,128)(2,1)} %fusion.36), channel_id=1, source_target_pairs={{0,4},{1,5},{2,6},{3,7},{4,0},{5,1},{6,2},{7,3},{8,12},{9,13},{10,... | collective-permute-start | bytes 122888 | tf_op jit(solution)/shard_map/ppermute | solution.py:731
  476.1 9.7 %collective-permute-start.37 = (f32[3,4,1,256]{3,2,1,0:T(1,128)S(1)}, f32[3,4,1,256]{3,2,1,0:T(1,128)S(1)}, u32[]{:S(2)}, u32[]{:S(2)}) collective-permute-start(f32[3,4,1,256]{3,2,1,0:T(1,128)S(1)} %add.302), channel_id=1, source_target_pairs={{0,2},{1,3},{2,0},{3,1},{4,6},{5,7},{6,4},{7,5},{8,10},{9,11},{10,... | collective-permute-start | bytes 36872 | tf_op jit(solution)/shard_map/ppermute | solution.py:731
  (42 other events, 215.5 us)
Sparse Core Ops, SparseCore 0:
  11.5 65.2 all-gather.4
  79.7 120.2 all-gather.6

commit v6 on v4

--- a/solution.py
+++ b/solution.py
@@ -522,7 +522,7 @@
 
 def middle_step(mid4, hid4, cot4, outs, grads, mix, slope, s2, gain, router):
     parts, tokens, width = mid4.shape
-    rows = 128
+    rows = 256
     block = pl.BlockSpec((parts, rows, width), lambda i: (0, i, 0))
     column = pl.BlockSpec((rows, 1), lambda i: (i, 0))
     vector = whole((parts, 1, width))

time: 517 us -> 516 us (level)
  no operation moved by 1% of the time
where the time goes in v6:
time: 516 us; the launch traced here: 507 us
  Pallas kernels  156 us (30%)
  waiting for transfers between devices  135 us (26%)
  starting transfers between devices  93.3 us (18%)
  other arithmetic  57.8 us (11%)
  local copies, waits for them, and re-layouts  48.9 us (9%)
  between operations  15.3 us (3%)
    ppermute x30, starting transfers between devices, swap(): lax.ppermute(self.clock.at(array), AXES, [(i, i ^ flip) for i in range(se...  76.5 us
    all_gather x1, waiting for transfers between devices, shards(): large_all = lax.all_gather(clock.after(large), AXES, axis=0, tiled=False)  53.9 us
    pallas_call x2, Pallas kernels, ffn(): pl.pallas_call(ffn_kernel, grid_spec=pltpu.PrefetchScalarGridSpec(num_sca...  42.8 us
    ppermute x30, waiting for transfers between devices, swap(): lax.ppermute(self.clock.at(array), AXES, [(i, i ^ flip) for i in range(se...  40.8 us
    ppermute x12, waiting for transfers between devices, move(): return lax.ppermute(self.clock.at(array), AXES, pairs)  40.7 us
    pallas_call x1, Pallas kernels, attention_backward(): pl.pallas_call(functools.partial(backward_kernel, slots), grid_spec=pltpu...  37.5 us
    convert_element_type x18, other arithmetic, add(): return (mine.astype(F32) + other.astype(F32)).astype(dtype)  27.6 us
    unnamed x74, local copies, waits for them, and re-layouts  21.8 us
  transfers between devices with their start and end apart: 44, of which 17 were waited for; matrix products, arithmetic and copies ran while one was open for 16% of the time, Pallas kernels for 27%

profile of v6, /device:TPU:0, one launch (start us, length us, event | category | flops | bytes accessed | tf_op | source)
XLA Modules:
  0.0 506.6 jit_solution(8326386015951571067)
XLA Ops:
  10.5 4.1 collective-permute-start
  34.3 4.6 first_norm.1
  41.1 5.0 collective-permute-done.2
  50.3 4.9 collective-permute-done.3
  60.0 4.0 kv_project.1.refs_0_
  65.7 20.4 %collective-permute-done.5 = bf16[2,272,640]{2,1,0:T(8,128)(2,1)S(1)} collective-permute-done((bf16[2,272,640]{2,1,0:T(8,128)(2,1)}, bf16[2,272,640]{2,1,0:T(8,128)(2,1)S(1)}, u32[]{:S(2)}, u32[]{:S(2)}) %collective-permute-start.5) | collective-permute-done | bytes 696352 | tf_op jit(solution)/shard_map/ppermute | solution.py:841
  88.1 4.4 collective-permute-start.7
  97.9 6.1 %q_project.1.q_ref = bf16[512,1920]{1,0:T(8,128)(2,1)} custom-call(bf16[4,512,256]{2,1,0:T(8,128)(2,1)} %get-tuple-element.251.xn_ref, bf16[4,1920,256]{2,1,0:T(8,128)(2,1)} %bitcast.167, f32[512,128]{1,0:T(8,128)} %get-tuple-element.552.cos_ref, f32[512,128]{1,0:T(8,128)} %get-tuple-element.549.sin_ref), custom_call_target="tpu_custom_call" | custom-call | flops 1887436800 | bytes 5898240 | tf_op jit(solution)/shard_map/q_project/pallas_call | solution.py:157
  104.0 3.7 collective-permute-done.7.refs_1_
  118.5 20.8 %attention_forward.1 = (bf16[512,1920]{1,0:T(8,128)(2,1)}, f32[2,5,1,768]{3,2,1,0:T(1,128)}) custom-call(s32[6]{0:T(128)} %stack.100.slot_ref, bf16[512,1920]{1,0:T(8,128)(2,1)} %q_project.1.q_ref, f32[2,1,256]{2,1,0:T(1,128)} %reshape.337.seg_ref, bf16[2,272,640]{2,1,0:T(8,128)(2,1)} %kv_project.1.refs_0_, ...), custom_call_target="tpu_custom_call" | custom-call | flops 6039797760 | bytes 7864320 | tf_op jit(solution)/shard_map/attention_forward/pallas_call | solution.py:270
  139.3 6.6 %out_project.1 = (f32[4,512,256]{2,1,0:T(8,128)}, bf16[4,512,256]{2,1,0:T(8,128)(2,1)}, f32[512,1]{1,0:T(8,128)}) custom-call(bf16[512,1920]{1,0:T(8,128)(2,1)} %get-tuple-element.289.o_ref, bf16[4,1920,256]{2,1,0:T(8,128)(2,1)} %bitcast.177, bf16[4,512,256]{2,1,0:T(8,128)(2,1)} %pad.41.hid_ref, f32[4,1,256]{2,1,0:T(1,128)} %pad_convert_fusion.gain_ref), custom_call_target="tpu_custom_call" | custom-call | flops 1887436800 | bytes 7864320 | tf_op jit(solution)/shard_map/out_project/pallas_call | solution.py:382
  146.0 53.9 %all-gather.7.cloned.1.call-done = bf16[30720,256]{1,0:T(8,128)(2,1)} async-done(((bf16[960,256]{1,0:T(8,128)(2,1)}), bf16[30720,256]{1,0:T(8,128)(2,1)}) %all-gather.7.cloned.1.call-update) | async-done | bytes 15728656 | tf_op jit(solution)/shard_map/all_gather | solution.py:997
  199.9 21.5 %ffn.2 = (f32[4,512,256]{2,1,0:T(8,128)}, f32[4,512,256]{2,1,0:T(8,128)}, bf16[2,2,4,480,256]{4,3,2,1,0:T(8,128)(2,1)}, bf16[2,2,4,480,256]{4,3,2,1,0:T(8,128)(2,1)}) custom-call(s32[3]{0:T(128)} %pad_add_fusion.meta_ref, bf16[4,512,256]{2,1,0:T(8,128)(2,1)} %get-tuple-element.293.x_ref, bf16[4,512,256]{2,1,0:T(8,128)(2,1)} %get-tuple-element.294.fg_ref, ...), custom_call_target="tpu_custom_call" | custom-call | flops 11324620800 | bytes 22609920 | tf_op jit(solution)/shard_map/ffn/pallas_call | solution.py:464
  221.7 21.3 %ffn.3 = (f32[4,512,256]{2,1,0:T(8,128)}, f32[4,512,256]{2,1,0:T(8,128)}, bf16[2,2,4,480,256]{4,3,2,1,0:T(8,128)(2,1)}, bf16[2,2,4,480,256]{4,3,2,1,0:T(8,128)(2,1)}) custom-call(s32[3]{0:T(128)} %pad_add_fusion.meta_ref, bf16[4,512,256]{2,1,0:T(8,128)(2,1)} %get-tuple-element.293.x_ref, bf16[4,512,256]{2,1,0:T(8,128)(2,1)} %get-tuple-element.294.fg_ref, ...), custom_call_target="tpu_custom_call" | custom-call | flops 11324620800 | bytes 22609920 | tf_op jit(solution)/shard_map/ffn/pallas_call | solution.py:464
  250.7 4.7 fusion
  255.5 7.7 %middle_step.1 = (bf16[512,960]{1,0:T(8,128)(2,1)}, f32[4,512,256]{2,1,0:T(8,128)}, bf16[4,512,256]{2,1,0:T(8,128)(2,1)}, f32[4,1,256]{2,1,0:T(1,128)}, f32[4,1,256]{2,1,0:T(1,128)}) custom-call(f32[4,512,256]{2,1,0:T(8,128)} %get-tuple-element.290.mid_ref, bf16[4,512,256]{2,1,0:T(8,128)(2,1)} %pad.41.hid_ref, bf16[4,512,256]{2,1,0:T(8,128)(2,1)} %pad.42.cot_ref, ...), custom_call_target="tpu_custom_call" | custom-call | flops 14745600 | bytes 17694720 | tf_op jit(solution)/shard_map/middle_step/pallas_call | solution.py:529
  263.2 5.8 %fusion.1 = (bf16[8,480,256]{2,1,0:T(8,128)(2,1)S(1)}, bf16[8,480,256]{2,1,0:T(8,128)(2,1)}) fusion(bf16[1,2,4,480,256]{4,3,2,1,0:T(8,128)(2,1)} %get-tuple-element.509, bf16[16,480,256]{2,1,0:T(8,128)(2,1)} %bitcast.45, bf16[1,2,4,480,256]{4,3,2,1,0:T(8,128)(2,1)} %get-tuple-element.510), kind=kLoop, calls=%fused_computation.4 | loop fusion | flops 7864320 | bytes 11796480 | tf_op jit(solution)/shard_map/convert_element_type | solution.py:716
  271.5 6.0 %out_back.1.do_ref = bf16[512,1920]{1,0:T(8,128)(2,1)} custom-call(bf16[4,512,256]{2,1,0:T(8,128)(2,1)} %get-tuple-element.317.ag_ref, bf16[4,1920,256]{2,1,0:T(8,128)(2,1)} %bitcast.178), custom_call_target="tpu_custom_call" | custom-call | flops 1887436800 | bytes 5898240 | tf_op jit(solution)/shard_map/out_back/pallas_call | solution.py:562
  277.5 37.5 %attention_backward.1 = (bf16[512,1920]{1,0:T(8,128)(2,1)}, bf16[2,256,640]{2,1,0:T(8,128)(2,1)}, bf16[2,256,640]{2,1,0:T(8,128)(2,1)}, bf16[2,256,640]{2,1,0:T(...) custom-call(s32[6]{0:T(128)} %stack.100.slot_ref, ...), custom_call_target="tpu_custom_call" | custom-call | flops 15099494400 | bytes 15728640 | tf_op jit(solution)/shard_map/attention_backward/pallas_call | solution.py:342
  316.5 9.6 %qo_back.1 = (bf16[2,2,960,256]{3,2,1,0:T(8,128)(2,1)}, bf16[2,2,960,256]{3,2,1,0:T(8,128)(2,1)}, f32[4,512,256]{2,1,0:T(8,128)}) custom-call(s32[1]{0:T(128)} %bitcast.35.meta_ref, bf16[512,1920]{1,0:T(8,128)(2,1)} %get-tuple-element.328.dq_ref, bf16[4,512,256]{2,1,0:T(8,128)(2,1)} %get-tuple-element.251.xn_ref, bf16[4,1920,256]{2,1,0:T(8,128)(2,1)} %bitcast.168, ...), custom_call_target="tpu_custom_call" | custom-call | flops 3774873600 | bytes 13762560 | tf_op jit(solution)/shard_map/qo_back/pallas_call | solution.py:598
  326.1 3.4 add_convert_fusion.1
  344.5 3.5 collective-permute-start.25
  347.9 5.9 %collective-permute-done.16 = bf16[2,256,640]{2,1,0:T(8,128)(2,1)} collective-permute-done((bf16[2,256,640]{2,1,0:T(8,128)(2,1)}, bf16[2,256,640]{2,1,0:T(8,128)(2,1)}, u32[]{:S(2)}, u32[]{:S(2)}) %collective-permute-start.16) | collective-permute-done | bytes 655392 | tf_op jit(solution)/shard_map/ppermute | solution.py:841
  361.5 42.9 %collective-permute-start.26 = (bf16[2,480,256]{2,1,0:T(8,128)(2,1)}, bf16[2,480,256]{2,1,0:T(8,128)(2,1)}, u32[]{:S(2)}, u32[]{:S(2)}) collective-permute-start(bf16[2,480,256]{2,1,0:T(8,128)(2,1)} %get-tuple-element.396), channel_id=1, source_target_pairs={{0,2},{1,3},{2,0},{3,1},{4,6},{5,7},{6,4},{7,5},{8,10},{9,11},{10,... | collective-permute-start | bytes 1474568 | tf_op jit(solution)/shard_map/ppermute | solution.py:731
  406.7 10.6 %collective-permute-done.21 = bf16[2,256,640]{2,1,0:T(8,128)(2,1)S(1)} collective-permute-done((bf16[2,256,640]{2,1,0:T(8,128)(2,1)S(1)}, bf16[2,256,640]{2,1,0:T(8,128)(2,1)S(1)}, u32[]{:S(2)}, u32[]{:S(2)}) %collective-permute-start.21) | collective-permute-done | bytes 655392 | tf_op jit(solution)/shard_map/ppermute | solution.py:841
  419.6 4.0 kv_back.1
  426.5 6.1 %final_step.1 = (f32[512,960]{1,0:T(8,128)}, f32[4,1,256]{2,1,0:T(1,128)}) custom-call(f32[4,512,256]{2,1,0:T(8,128)} %get-tuple-element.341.xg_ref, bf16[512,640]{1,0:T(8,128)(2,1)} %get-tuple-element.387.kvb_ref, bf16[4,640,256]{2,1,0:T(8,128)(2,1)} %bitcast.170, bf16[4,512,256]{2,1,0:T(8,128)(2,1)} %pad.41.hid_ref, ...), custom_call_target="tpu_custom_call" | custom-call | flops 629145600 | bytes 9830400 | tf_op jit(solution)/shard_map/final_step/pallas_call | solution.py:679
  443.2 3.2 collective-permute-start.36
  448.1 11.2 %collective-permute-done.33 = bf16[2,480,256]{2,1,0:T(8,128)(2,1)S(1)} collective-permute-done((bf16[2,480,256]{2,1,0:T(8,128)(2,1)S(1)}, bf16[2,480,256]{2,1,0:T(8,128)(2,1)S(1)}, u32[]{:S(2)}, u32[]{:S(2)}) %collective-permute-start.33) | collective-permute-done | bytes 491552 | tf_op jit(solution)/shard_map/ppermute | solution.py:731
  460.1 3.1 collective-permute-done.32
  463.4 3.5 collective-permute-start.39
  476.1 5.7 %collective-permute-done.39 = bf16[1,480,256]{2,1,0:T(8,128)(2,1)} collective-permute-done((bf16[1,480,256]{2,1,0:T(8,128)(2,1)S(1)}, bf16[1,480,256]{2,1,0:T(8,128)(2,1)}, u32[]{:S(2)}, u32[]{:S(2)}) %collective-permute-start.39) | collective-permute-done | bytes 245792 | tf_op jit(solution)/shard_map/ppermute | solution.py:731
  (247 shorter events, 135.5 us)
Async XLA Ops:
  7.2 86.1 %all-gather.5.cloned.1.call-start = ((), (), s32[]{:S(2)}) async-start(), calls=%async_computation | async-start | bytes 4055040 | tf_op jit(solution)/shard_map/all_gather | solution.py:984
  9.7 190.3 %all-gather.7.cloned.1.call-start = ((), (), s32[]{:S(2)}) async-start(), calls=%async_computation.1 | async-start | bytes 16220160 | tf_op jit(solution)/shard_map/all_gather | solution.py:997
  10.5 21.5 %collective-permute-start = (bf16[80,256]{1,0:T(8,128)(2,1)S(1)}, bf16[80,256]{1,0:T(8,128)(2,1)S(1)}, u32[]{:S(2)}, u32[]{:S(2)}) collective-permute-start(bf16[80,256]{1,0:T(8,128)(2,1)S(1)} %fusion.37), channel_id=1, source_target_pairs={{0,4},{1,5},{2,6},{3,7},{4,0},{5,1},{6,2},{7,3},{8,12},{9,13},{10,... | collective-permute-start | bytes 122888 | tf_op jit(solution)/shard_map/ppermute | solution.py:731
  46.2 9.0 %collective-permute-start.3 = (bf16[2,2,2,80,256]{4,3,0,1,2:T(8,128)(2,1)S(1)}, bf16[2,2,2,80,256]{4,3,0,1,2:T(8,128)(2,1)S(1)}, u32[]{:S(2)}, u32[]{:S(2)}) collective-permute-start(bf16[2,2,2,80,256]{4,3,0,1,2:T(8,128)(2,1)S(1)} %pad_maximum_fusion.5), channel_id=1, source_target_pairs={{0,16},{1,17},{2,18},{3,19},{4,20},{5,21},{6,22},{7,23},{8,24},{9,... | collective-permute-start | bytes 983048 | tf_op jit(solution)/shard_map/ppermute | solution.py:731
  64.0 22.1 %collective-permute-start.5 = (bf16[2,272,640]{2,1,0:T(8,128)(2,1)}, bf16[2,272,640]{2,1,0:T(8,128)(2,1)S(1)}, u32[]{:S(2)}, u32[]{:S(2)}) collective-permute-start(bf16[2,272,640]{2,1,0:T(8,128)(2,1)} %kv_project.1.refs_0_), channel_id=1, source_target_pairs={{0,2},{1,3},{2,4},{3,5},{4,6},{5,7},{8,10},{9,11},{10,12},{11,13},... | collective-permute-start | bytes 2088968 | tf_op jit(solution)/shard_map/ppermute | solution.py:841
  88.1 19.7 %collective-permute-start.7 = (bf16[2,272,640]{2,1,0:T(8,128)(2,1)}, bf16[2,272,640]{2,1,0:T(8,128)(2,1)}, u32[]{:S(2)}, u32[]{:S(2)}) collective-permute-start(bf16[2,272,640]{2,1,0:T(8,128)(2,1)} %broadcast_select_fusion.3), channel_id=1, source_target_pairs={{0,1},{2,3},{4,5},{6,7},{7,6},{8,9},{10,11},{12,13},{14,15},{15,14... | collective-permute-start | bytes 2088968 | tf_op jit(solution)/shard_map/ppermute | solution.py:841
  92.5 15.3 %collective-permute-start.6 = (bf16[2,272,640]{2,1,0:T(8,128)(2,1)S(1)}, bf16[2,272,640]{2,1,0:T(8,128)(2,1)S(1)}, u32[]{:S(2)}, u32[]{:S(2)}) collective-permute-start(bf16[2,272,640]{2,1,0:T(8,128)(2,1)S(1)} %collective-permute-done.5), channel_id=1, source_target_pairs={{2,4},{3,5},{4,6},{5,7},{10,12},{11,13},{12,14},{13,15},{18,20},{1... | collective-permute-start | bytes 2088968 | tf_op jit(solution)/shard_map/ppermute | solution.py:841
  221.4 27.3 %collective-permute-start.11 = (bf16[2,2,4,480,256]{4,3,2,1,0:T(8,128)(2,1)}, bf16[2,2,4,480,256]{4,3,2,1,0:T(8,128)(2,1)S(1)}, u32[]{:S(2)}, u32[]{:S(2)}) collective-permute-start(bf16[2,2,4,480,256]{4,3,2,1,0:T(8,128)(2,1)} %get-tuple-element.301), channel_id=1, source_target_pairs={{0,8},{1,9},{2,10},{3,11},{4,12},{5,13},{6,14},{7,15},{8,0},{9,1},... | collective-permute-start | bytes 11796488 | tf_op jit(solution)/shard_map/ppermute | solution.py:731
  243.0 20.1 %collective-permute-start.12 = (bf16[2,2,4,480,256]{4,3,2,1,0:T(8,128)(2,1)}, bf16[2,2,4,480,256]{4,3,2,1,0:T(8,128)(2,1)}, u32[]{:S(2)}, u32[]{:S(2)}) collective-permute-start(bf16[2,2,4,480,256]{4,3,2,1,0:T(8,128)(2,1)} %get-tuple-element.319), channel_id=1, source_target_pairs={{0,8},{1,9},{2,10},{3,11},{4,12},{5,13},{6,14},{7,15},{8,0},{9,1},... | collective-permute-start | bytes 11796488 | tf_op jit(solution)/shard_map/ppermute | solution.py:731
  269.0 46.0 %collective-permute-start.13 = (bf16[8,480,256]{2,1,0:T(8,128)(2,1)}, bf16[8,480,256]{2,1,0:T(8,128)(2,1)}, u32[]{:S(2)}, u32[]{:S(2)}) collective-permute-start(bf16[8,480,256]{2,1,0:T(8,128)(2,1)} %get-tuple-element.330), channel_id=1, source_target_pairs={{0,1},{1,0},{2,3},{3,2},{4,5},{5,4},{6,7},{7,6},{8,9},{9,8},{10,11... | collective-permute-start | bytes 5898248 | tf_op jit(solution)/shard_map/ppermute | solution.py:731
  269.6 45.4 %collective-permute-start.14 = (bf16[8,480,256]{2,1,0:T(8,128)(2,1)}, bf16[8,480,256]{2,1,0:T(8,128)(2,1)}, u32[]{:S(2)}, u32[]{:S(2)}) collective-permute-start(bf16[8,480,256]{2,1,0:T(8,128)(2,1)} %get-tuple-element.335), channel_id=1, source_target_pairs={{0,16},{1,17},{2,18},{3,19},{4,20},{5,21},{6,22},{7,23},{8,24},{9,... | collective-permute-start | bytes 5898248 | tf_op jit(solution)/shard_map/ppermute | solution.py:731
  315.0 14.5 %collective-permute-start.15 = (bf16[2,256,640]{2,1,0:T(8,128)(2,1)}, bf16[2,256,640]{2,1,0:T(8,128)(2,1)}, u32[]{:S(2)}, u32[]{:S(2)}) collective-permute-start(bf16[2,256,640]{2,1,0:T(8,128)(2,1)} %get-tuple-element.345), channel_id=1, source_target_pairs={{5,4},{4,5},{7,6},{6,7},{13,12},{12,13},{15,14},{14,15},{21,20},{2... | collective-permute-start | bytes 1966088 | tf_op jit(solution)/shard_map/ppermute | solution.py:841
  330.9 11.5 %collective-permute-start.20 = (bf16[2,2,960,256]{3,2,1,0:T(8,128)(2,1)S(1)}, bf16[2,2,960,256]{3,2,1,0:T(8,128)(2,1)S(1)}, u32[]{:S(2)}, u32[]{:S(2)}) collective-permute-start(bf16[2,2,960,256]{3,2,1,0:T(8,128)(2,1)S(1)} %copy-done.26), channel_id=1, source_target_pairs={{0,8},{1,9},{2,10},{3,11},{4,12},{5,13},{6,14},{7,15},{8,0},{9,1},... | collective-permute-start | bytes 5898248 | tf_op jit(solution)/shard_map/ppermute | solution.py:731
  332.6 24.9 %collective-permute-start.23 = (bf16[4,480,256]{2,1,0:T(8,128)(2,1)}, bf16[4,480,256]{2,1,0:T(8,128)(2,1)}, u32[]{:S(2)}, u32[]{:S(2)}) collective-permute-start(bf16[4,480,256]{2,1,0:T(8,128)(2,1)} %get-tuple-element.374), channel_id=1, source_target_pairs={{0,16},{1,17},{2,18},{3,19},{4,20},{5,21},{6,22},{7,23},{8,24},{9,... | collective-permute-start | bytes 2949128 | tf_op jit(solution)/shard_map/ppermute | solution.py:731
  334.1 19.8 %collective-permute-start.16 = (bf16[2,256,640]{2,1,0:T(8,128)(2,1)}, bf16[2,256,640]{2,1,0:T(8,128)(2,1)}, u32[]{:S(2)}, u32[]{:S(2)}) collective-permute-start(bf16[2,256,640]{2,1,0:T(8,128)(2,1)} %get-tuple-element.350), channel_id=1, source_target_pairs={{1,0},{3,2},{5,4},{7,6},{6,7},{9,8},{11,10},{13,12},{15,14},{14,15... | collective-permute-start | bytes 1966088 | tf_op jit(solution)/shard_map/ppermute | solution.py:841
  338.0 15.9 %collective-permute-start.19 = (bf16[2,256,640]{2,1,0:T(8,128)(2,1)}, bf16[2,256,640]{2,1,0:T(8,128)(2,1)}, u32[]{:S(2)}, u32[]{:S(2)}) collective-permute-start(bf16[2,256,640]{2,1,0:T(8,128)(2,1)} %fusion.8), channel_id=1, source_target_pairs={{4,2},{5,3},{6,4},{7,5},{12,10},{13,11},{14,12},{15,13},{20,18},{2... | collective-permute-start | bytes 1966088 | tf_op jit(solution)/shard_map/ppermute | solution.py:841
  343.9 60.5 %collective-permute-start.22 = (bf16[1,2,8,120,256]{4,3,2,1,0:T(8,128)(2,1)}, bf16[1,2,8,120,256]{4,3,2,1,0:T(8,128)(2,1)}, u32[]{:S(2)}, u32[]{:S(2)}) collective-permute-start(bf16[1,2,8,120,256]{4,3,2,1,0:T(8,128)(2,1)} %get-tuple-element.373), channel_id=1, source_target_pairs={{0,16},{1,17},{2,18},{3,19},{4,20},{5,21},{6,22},{7,23},{8,24},{9,... | collective-permute-start | bytes 2949128 | tf_op jit(solution)/shard_map/ppermute | solution.py:731
  344.5 91.4 %collective-permute-start.25 = (bf16[4,480,256]{2,1,0:T(8,128)(2,1)}, bf16[4,480,256]{2,1,0:T(8,128)(2,1)}, u32[]{:S(2)}, u32[]{:S(2)}) collective-permute-start(bf16[4,480,256]{2,1,0:T(8,128)(2,1)} %get-tuple-element.395), channel_id=1, source_target_pairs={{0,1},{1,0},{2,3},{3,2},{4,5},{5,4},{6,7},{7,6},{8,9},{9,8},{10,11... | collective-permute-start | bytes 2949128 | tf_op jit(solution)/shard_map/ppermute | solution.py:731
  357.5 59.8 %collective-permute-start.21 = (bf16[2,256,640]{2,1,0:T(8,128)(2,1)S(1)}, bf16[2,256,640]{2,1,0:T(8,128)(2,1)S(1)}, u32[]{:S(2)}, u32[]{:S(2)}) collective-permute-start(bf16[2,256,640]{2,1,0:T(8,128)(2,1)S(1)} %fusion.11), channel_id=1, source_target_pairs={{2,0},{3,1},{4,2},{5,3},{6,4},{7,5},{10,8},{11,9},{12,10},{13,11},... | collective-permute-start | bytes 1966088 | tf_op jit(solution)/shard_map/ppermute | solution.py:841
  361.5 73.3 %collective-permute-start.26 = (bf16[2,480,256]{2,1,0:T(8,128)(2,1)}, bf16[2,480,256]{2,1,0:T(8,128)(2,1)}, u32[]{:S(2)}, u32[]{:S(2)}) collective-permute-start(bf16[2,480,256]{2,1,0:T(8,128)(2,1)} %get-tuple-element.396), channel_id=1, source_target_pairs={{0,2},{1,3},{2,0},{3,1},{4,6},{5,7},{6,4},{7,5},{8,10},{9,11},{10,... | collective-permute-start | bytes 1474568 | tf_op jit(solution)/shard_map/ppermute | solution.py:731
  424.7 8.9 %collective-permute-start.27 = (bf16[2,2,5,64,256]{4,3,2,1,0:T(8,128)(2,1)S(1)}, bf16[2,2,5,64,256]{4,3,2,1,0:T(8,128)(2,1)}, u32[]{:S(2)}, u32[]{:S(2)}) collective-permute-start(bf16[2,2,5,64,256]{4,3,2,1,0:T(8,128)(2,1)S(1)} %bitcast.196), channel_id=1, source_target_pairs={{0,8},{1,9},{2,10},{3,11},{4,12},{5,13},{6,14},{7,15},{8,0},{9,1},... | collective-permute-start | bytes 1966088 | tf_op jit(solution)/shard_map/ppermute | solution.py:731
  425.9 14.0 %collective-permute-start.24 = (bf16[2,4,120,256]{3,2,0,1:T(8,128)(2,1)}, bf16[2,4,120,256]{3,2,0,1:T(8,128)(2,1)}, u32[]{:S(2)}, u32[]{:S(2)}) collective-permute-start(bf16[2,4,120,256]{3,2,0,1:T(8,128)(2,1)} %fusion.17), channel_id=1, source_target_pairs={{0,1},{1,0},{2,3},{3,2},{4,5},{5,4},{6,7},{7,6},{8,9},{9,8},{10,11... | collective-permute-start | bytes 1474568 | tf_op jit(solution)/shard_map/ppermute | solution.py:731
  435.8 10.6 %collective-permute-start.29 = (bf16[1,2,8,40,256]{4,3,2,1,0:T(8,128)(2,1)S(1)}, bf16[1,2,8,40,256]{4,3,2,1,0:T(8,128)(2,1)S(1)}, u32[]{:S(2)}, u32[]{:S(2)}) collective-permute-start(bf16[1,2,8,40,256]{4,3,2,1,0:T(8,128)(2,1)S(1)} %get-tuple-element.413), channel_id=1, source_target_pairs={{0,16},{1,17},{2,18},{3,19},{4,20},{5,21},{6,22},{7,23},{8,24},{9,... | collective-permute-start | bytes 983048 | tf_op jit(solution)/shard_map/ppermute | solution.py:731
  439.9 19.4 %collective-permute-start.33 = (bf16[2,480,256]{2,1,0:T(8,128)(2,1)S(1)}, bf16[2,480,256]{2,1,0:T(8,128)(2,1)S(1)}, u32[]{:S(2)}, u32[]{:S(2)}) collective-permute-start(bf16[2,480,256]{2,1,0:T(8,128)(2,1)S(1)} %get-tuple-element.423), channel_id=1, source_target_pairs={{0,2},{1,3},{2,0},{3,1},{4,6},{5,7},{6,4},{7,5},{8,10},{9,11},{10,... | collective-permute-start | bytes 1474568 | tf_op jit(solution)/shard_map/ppermute | solution.py:731
  441.2 22.1 %collective-permute-start.32 = (bf16[2,2,120,256]{3,2,0,1:T(8,128)(2,1)S(1)}, bf16[2,2,120,256]{3,2,0,1:T(8,128)(2,1)S(1)}, u32[]{:S(2)}, u32[]{:S(2)}) collective-permute-start(bf16[2,2,120,256]{3,2,0,1:T(8,128)(2,1)S(1)} %get-tuple-element.422), channel_id=1, source_target_pairs={{0,2},{1,3},{2,0},{3,1},{4,6},{5,7},{6,4},{7,5},{8,10},{9,11},{10,... | collective-permute-start | bytes 737288 | tf_op jit(solution)/shard_map/ppermute | solution.py:731
  443.2 23.8 %collective-permute-start.36 = (bf16[1,480,256]{2,1,0:T(8,128)(2,1)S(1)}, bf16[1,480,256]{2,1,0:T(8,128)(2,1)}, u32[]{:S(2)}, u32[]{:S(2)}) collective-permute-start(bf16[1,480,256]{2,1,0:T(8,128)(2,1)S(1)} %add_convert_fusion.15), channel_id=1, source_target_pairs={{0,4},{1,5},{2,6},{3,7},{4,0},{5,1},{6,2},{7,3},{8,12},{9,13},{10,... | collective-permute-start | bytes 737288 | tf_op jit(solution)/shard_map/ppermute | solution.py:731
  446.5 16.8 %collective-permute-start.31 = (bf16[2,4,40,256]{3,2,1,0:T(8,128)(2,1)S(1)}, bf16[2,4,40,256]{3,2,1,0:T(8,128)(2,1)S(1)}, u32[]{:S(2)}, u32[]{:S(2)}) collective-permute-start(bf16[2,4,40,256]{3,2,1,0:T(8,128)(2,1)S(1)} %get-tuple-element.421), channel_id=1, source_target_pairs={{0,1},{1,0},{2,3},{3,2},{4,5},{5,4},{6,7},{7,6},{8,9},{9,8},{10,11... | collective-permute-start | bytes 491528 | tf_op jit(solution)/shard_map/ppermute | solution.py:731
  447.4 19.5 %collective-permute-start.30 = (f32[3,4,1,256]{3,2,1,0:T(1,128)S(1)}, f32[3,4,1,256]{3,2,1,0:T(1,128)S(1)}, u32[]{:S(2)}, u32[]{:S(2)}) collective-permute-start(f32[3,4,1,256]{3,2,1,0:T(1,128)S(1)} %fusion.49), channel_id=1, source_target_pairs={{0,16},{1,17},{2,18},{3,19},{4,20},{5,21},{6,22},{7,23},{8,24},{9,... | collective-permute-start | bytes 36872 | tf_op jit(solution)/shard_map/ppermute | solution.py:731
  463.4 18.3 %collective-permute-start.39 = (bf16[1,480,256]{2,1,0:T(8,128)(2,1)S(1)}, bf16[1,480,256]{2,1,0:T(8,128)(2,1)}, u32[]{:S(2)}, u32[]{:S(2)}) collective-permute-start(bf16[1,480,256]{2,1,0:T(8,128)(2,1)S(1)} %add_convert_fusion.12), channel_id=1, source_target_pairs={{0,4},{1,5},{2,6},{3,7},{4,0},{5,1},{6,2},{7,3},{8,12},{9,13},{10,... | collective-permute-start | bytes 737288 | tf_op jit(solution)/shard_map/ppermute | solution.py:731
  466.9 17.0 %collective-permute-start.38 = (bf16[2,1,120,256]{3,2,0,1:T(8,128)(2,1)S(1)}, bf16[2,1,120,256]{3,2,0,1:T(8,128)(2,1)}, u32[]{:S(2)}, u32[]{:S(2)}) collective-permute-start(bf16[2,1,120,256]{3,2,0,1:T(8,128)(2,1)S(1)} %fusion.27), channel_id=1, source_target_pairs={{0,4},{1,5},{2,6},{3,7},{4,0},{5,1},{6,2},{7,3},{8,12},{9,13},{10,... | collective-permute-start | bytes 368648 | tf_op jit(solution)/shard_map/ppermute | solution.py:731
  468.9 20.1 %collective-permute-start.41 = (bf16[2,1,40,256]{3,2,0,1:T(8,128)(2,1)}, bf16[2,1,40,256]{3,2,0,1:T(8,128)(2,1)}, u32[]{:S(2)}, u32[]{:S(2)}) collective-permute-start(bf16[2,1,40,256]{3,2,0,1:T(8,128)(2,1)} %fusion.36), channel_id=1, source_target_pairs={{0,4},{1,5},{2,6},{3,7},{4,0},{5,1},{6,2},{7,3},{8,12},{9,13},{10,... | collective-permute-start | bytes 122888 | tf_op jit(solution)/shard_map/ppermute | solution.py:731
  474.6 9.7 %collective-permute-start.37 = (f32[3,4,1,256]{3,2,1,0:T(1,128)S(1)}, f32[3,4,1,256]{3,2,1,0:T(1,128)S(1)}, u32[]{:S(2)}, u32[]{:S(2)}) collective-permute-start(f32[3,4,1,256]{3,2,1,0:T(1,128)S(1)} %add.302), channel_id=1, source_target_pairs={{0,2},{1,3},{2,0},{3,1},{4,6},{5,7},{6,4},{7,5},{8,10},{9,11},{10,... | collective-permute-start | bytes 36872 | tf_op jit(solution)/shard_map/ppermute | solution.py:731
  (42 other events, 215.5 us)
Sparse Core Ops, SparseCore 0:
  11.5 65.2 all-gather.4
  79.7 120.2 all-gather.6
